TPU v7x, 32 devices: a whole 2x2x4 slice. The times are simulated.
32 devices in a mesh: tok: 8 (over z, y), head: 4 (over x, core).
Axes of the slice: x: 2, y: 2, z: 4, core: 2. Of those that a mesh axis runs over, the one named last changes fastest.
Arguments:
- tokens: bfloat16 [16384, 768], P('tok'), may hold values from -6 to 6
- latents: bfloat16 [512, 768], P('tok'), may hold values from -6 to 6
- image_groups: int32 [5], replicated, may hold values from 1 to 58, as said below
- read_query: bfloat16 [768, 768], P(None, 'head'), may hold values from -0.4375 to 0.4375
- read_key: bfloat16 [768, 768], P(None, 'head'), may hold values from -0.21875 to 0.21875
- read_value: bfloat16 [768, 768], P(None, 'head'), may hold values from -0.21875 to 0.21875
- read_out: bfloat16 [768, 768], P('head'), may hold values from -1.25 to 1.25
- write_query: bfloat16 [768, 768], P(None, 'head'), may hold values from -0.4375 to 0.4375
- write_key: bfloat16 [768, 768], P(None, 'head'), may hold values from -0.21875 to 0.21875
- write_value: bfloat16 [768, 768], P(None, 'head'), may hold values from -0.21875 to 0.21875
- write_out: bfloat16 [768, 768], P('head'), may hold values from -1.25 to 1.25
- mlp_in: bfloat16 [768, 3072], P(None, 'head'), may hold values from -0.21875 to 0.21875
- mlp_out: bfloat16 [3072, 768], P('head'), may hold values from -0.109375 to 0.109375
- cotangent: bfloat16 [16384, 768], P('tok'), may hold values from -6 to 6
Outputs:
- layer_out: bfloat16 [16384, 768], P(('tok', 'head'))
- input_grad: float32 [16384, 768], P(('tok', 'head'))
- latent_grad: float32 [512, 768], P(('tok', 'head'))
- grad_read_query: float32 [768, 768], P('tok', 'head')
- grad_read_key: float32 [768, 768], P('tok', 'head')
- grad_read_value: float32 [768, 768], P('tok', 'head')
- grad_read_out: float32 [768, 768], P('head', 'tok')
- grad_write_query: float32 [768, 768], P('tok', 'head')
- grad_write_key: float32 [768, 768], P('tok', 'head')
- grad_write_value: float32 [768, 768], P('tok', 'head')
- grad_write_out: float32 [768, 768], P('head', 'tok')
- grad_mlp_in: float32 [768, 3072], P('tok', 'head')
- grad_mlp_out: float32 [3072, 768], P('head', 'tok')
Inputs may be any that keep to these rules, and one draw needn't show every extreme that they name: `image_groups`: groups of each image; the counts add up to 64; the middle image is the largest, every other image has 1 or 2 groups.
All inputs are finite; a program needn't handle non-finite values.
Results may differ from a plain program's by a relative error of at most 0.025.
The roundings to bfloat16 on the way count: a program that leaves them out, or rounds other values in their place, can miss the bound.
Values may be sent and summed in bfloat16 or wider, within the bound.
A program may use at most 256 MiB of HBM per device.

v0:
```python
import jax
import jax.numpy as jnp
from jax import lax
from jax.sharding import PartitionSpec as P

HD = 64
GROUP = 256
LPG = 8


epsilon = 1e-05
triple = lax.Precision.HIGH


def norm_rows(values):
    center = values - jnp.mean(values, axis=-1, keepdims=True)
    return center * lax.rsqrt(jnp.mean(center * center, axis=-1, keepdims=True) + epsilon)


def matmul(left, right):
    return jnp.dot(left, right, preferred_element_type=jnp.float32)


def left_trans(left, right):
    return lax.dot_general(
        left, right, (((0,), (0,)), ((), ())), preferred_element_type=jnp.float32
    )


def right_trans(left, right):
    return lax.dot_general(
        left, right, (((1,), (1,)), ((), ())), preferred_element_type=jnp.float32
    )


def heads_view(values):
    return values.reshape(values.shape[0], values.shape[1] // HD, HD)


def shards(
    tokens,
    latents,
    image_groups,
    read_query,
    read_key,
    read_value,
    read_out,
    write_query,
    write_key,
    write_value,
    write_out,
    mlp_in,
    mlp_out,
    cotangent,
):
    rows = tokens.shape[0]
    owned = latents.shape[0]
    column = read_query.shape[1]
    heads_here = column // HD
    tok_count = lax.axis_size("tok")
    head_count = lax.axis_size("head")
    tok_index = lax.axis_index("tok")
    head_index = lax.axis_index("head")
    groups_here = rows // GROUP
    total_groups = groups_here * tok_count
    all_latents = total_groups * LPG
    bounds = jnp.cumsum(image_groups)
    group_ids = jnp.arange(total_groups, dtype=jnp.int32)
    group_image = jnp.sum((bounds[None, :] <= group_ids[:, None]).astype(jnp.int32), axis=1)
    latent_image = jnp.repeat(group_image, LPG, total_repeat_length=all_latents)
    local_groups = lax.dynamic_slice_in_dim(group_image, tok_index * groups_here, groups_here)
    token_image = jnp.repeat(local_groups, GROUP, total_repeat_length=rows)
    own_image = lax.dynamic_slice_in_dim(latent_image, tok_index * owned, owned)
    key_image = jnp.concatenate([token_image, own_image], axis=0)
    key_count = rows + owned
    tokens_full = tokens.astype(jnp.float32)
    latents_full = latents.astype(jnp.float32)
    normed_x = norm_rows(tokens_full).astype(jnp.bfloat16)
    normed_lat = norm_rows(latents_full).astype(jnp.bfloat16)
    query_own = matmul(normed_lat, read_query).astype(jnp.bfloat16)
    query_all = lax.all_gather(query_own, "tok", axis=0, tiled=True)
    keys_here = jnp.concatenate(
        [matmul(normed_x, read_key), matmul(normed_lat, read_key)], axis=0
    ).astype(jnp.bfloat16)
    values_here = jnp.concatenate(
        [matmul(normed_x, read_value), matmul(normed_lat, read_value)], axis=0
    ).astype(jnp.bfloat16)
    keys_split = heads_view(keys_here)
    values_split = heads_view(values_here)
    latent_block = min(512, all_latents)
    latent_blocks = all_latents // latent_block

    def read_scores(query_block, image_block):
        scores = (
            jnp.einsum(
                "qhd,khd->qhk",
                heads_view(query_block),
                keys_split,
                preferred_element_type=jnp.float32,
            )
            * 0.125
        )
        mask = (image_block[:, None] == key_image[None, :])[:, None, :]
        return (scores, mask)

    def read_block(operands):
        query_block, image_block = operands
        scores, mask = read_scores(query_block, image_block)
        weights = jnp.where(mask, jnp.exp(scores), 0.0)
        totals = jnp.sum(weights, axis=-1)
        summed = jnp.einsum(
            "qhk,khd->qhd",
            weights,
            values_split,
            precision=triple,
            preferred_element_type=jnp.float32,
        )
        return (totals, summed.reshape(query_block.shape[0], column))

    query_blocks = query_all.reshape(latent_blocks, latent_block, column)
    image_blocks = latent_image.reshape(latent_blocks, latent_block)
    totals, sums = lax.map(read_block, (query_blocks, image_blocks))
    totals = totals.reshape(all_latents, heads_here)
    sums = sums.reshape(all_latents, column)
    totals_all, sums_all = lax.psum((totals, sums), "tok")
    total_own = lax.dynamic_slice_in_dim(totals_all, tok_index * owned, owned)
    sum_own = lax.dynamic_slice_in_dim(sums_all, tok_index * owned, owned)
    mixed_wide = (heads_view(sum_own) / total_own[:, :, None]).reshape(owned, column)
    read_mixed = mixed_wide.astype(jnp.bfloat16)
    latents_one = latents_full + lax.psum(matmul(read_mixed, read_out), "head")
    normed_one, norm_one_back = jax.vjp(norm_rows, latents_one)
    normed_one = normed_one.astype(jnp.bfloat16)
    wkey_own = matmul(normed_one, write_key).astype(jnp.bfloat16)
    wvalue_own = matmul(normed_one, write_value).astype(jnp.bfloat16)
    wkey_all, wvalue_all = (
        lax.all_gather(wkey_own, "tok", axis=0, tiled=True),
        lax.all_gather(wvalue_own, "tok", axis=0, tiled=True),
    )
    wkey_split = heads_view(wkey_all)
    wvalue_split = heads_view(wvalue_all)
    query_write = matmul(normed_x, write_query).astype(jnp.bfloat16)
    row_block = min(512, rows)
    row_blocks = rows // row_block

    def write_scores(query_block, image_block):
        scores = (
            jnp.einsum(
                "qhd,khd->qhk",
                heads_view(query_block),
                wkey_split,
                preferred_element_type=jnp.float32,
            )
            * 0.125
        )
        mask = (image_block[:, None] == latent_image[None, :])[:, None, :]
        return (scores, mask)

    def write_block(operands):
        query_block, image_block = operands
        scores, mask = write_scores(query_block, image_block)
        weights = jnp.where(mask, jnp.exp(scores), 0.0)
        totals_block = jnp.sum(weights, axis=-1, keepdims=True)
        probs = (weights / totals_block).astype(jnp.bfloat16)
        mixed = jnp.einsum("qhk,khd->qhd", probs, wvalue_split, preferred_element_type=jnp.float32)
        return (
            mixed.reshape(query_block.shape[0], column).astype(jnp.bfloat16),
            jnp.log(totals_block[:, :, 0]),
        )

    wquery_blocks = query_write.reshape(row_blocks, row_block, column)
    token_blocks = token_image.reshape(row_blocks, row_block)
    write_mixed, write_logs = lax.map(write_block, (wquery_blocks, token_blocks))
    write_mixed = write_mixed.reshape(rows, column)
    tokens_one = tokens_full + lax.psum(matmul(write_mixed, write_out), "head")
    normed_two, norm_two_back = jax.vjp(norm_rows, tokens_one)
    normed_two = normed_two.astype(jnp.bfloat16)
    inner = matmul(normed_two, mlp_in)
    activated, gelu_back = jax.vjp(jax.nn.gelu, inner)
    activated = activated.astype(jnp.bfloat16)
    quarter = rows // head_count
    row_start = head_index * quarter
    branch = lax.psum_scatter(matmul(activated, mlp_out), "head", scatter_dimension=0, tiled=True)
    layer_out = (lax.dynamic_slice_in_dim(tokens_one, row_start, quarter) + branch).astype(
        jnp.bfloat16
    )
    grad_mlp_out = left_trans(activated, cotangent)
    grad_act = right_trans(cotangent, mlp_out)
    grad_inner = gelu_back(grad_act)[0].astype(jnp.bfloat16)
    grad_mlp_in = left_trans(normed_two, grad_inner)
    grad_normed_two = lax.psum(right_trans(grad_inner, mlp_in), "head")
    grad_tokens_one = cotangent.astype(jnp.float32) + norm_two_back(grad_normed_two)[0]
    grad_branch = grad_tokens_one.astype(jnp.bfloat16)
    grad_write_out = left_trans(write_mixed, grad_branch)
    grad_wmixed = right_trans(grad_branch, write_out).astype(jnp.bfloat16)

    def write_back(carry, operands):
        key_total, value_total = carry
        query_block, image_block, grad_block, log_block = operands
        scores, mask = write_scores(query_block, image_block)
        probs = jnp.where(mask, jnp.exp(scores - log_block[:, :, None]), 0.0)
        grad_probs = jnp.einsum(
            "qhd,khd->qhk", heads_view(grad_block), wvalue_split, preferred_element_type=jnp.float32
        )
        delta = jnp.sum(probs * grad_probs, axis=-1, keepdims=True)
        grad_scores = (probs * (grad_probs - delta)).astype(jnp.bfloat16)
        grad_query = (
            jnp.einsum("qhk,khd->qhd", grad_scores, wkey_split, preferred_element_type=jnp.float32)
            * 0.125
        )
        key_total = (
            key_total
            + jnp.einsum(
                "qhk,qhd->khd",
                grad_scores,
                heads_view(query_block),
                preferred_element_type=jnp.float32,
            ).reshape(all_latents, column)
            * 0.125
        )
        value_total = value_total + jnp.einsum(
            "qhk,qhd->khd",
            probs.astype(jnp.bfloat16),
            heads_view(grad_block),
            preferred_element_type=jnp.float32,
        ).reshape(all_latents, column)
        return (
            (key_total, value_total),
            grad_query.reshape(query_block.shape[0], column).astype(jnp.bfloat16),
        )

    latent_zeros = jnp.zeros((all_latents, column), jnp.float32)
    (grad_wkey_all, grad_wvalue_all), grad_wquery = lax.scan(
        write_back,
        (latent_zeros, latent_zeros),
        (
            wquery_blocks,
            token_blocks,
            grad_wmixed.reshape(row_blocks, row_block, column),
            write_logs,
        ),
    )
    grad_wquery = grad_wquery.reshape(rows, column)
    grad_wkey, grad_wvalue = (
        lax.psum_scatter(grad_wkey_all, "tok", scatter_dimension=0, tiled=True),
        lax.psum_scatter(grad_wvalue_all, "tok", scatter_dimension=0, tiled=True),
    )
    grad_wkey = grad_wkey.astype(jnp.bfloat16)
    grad_wvalue = grad_wvalue.astype(jnp.bfloat16)
    grad_write_key = left_trans(normed_one, grad_wkey)
    grad_write_value = left_trans(normed_one, grad_wvalue)
    grad_write_query = left_trans(normed_x, grad_wquery)
    grad_normed_one = lax.psum(
        right_trans(grad_wkey, write_key) + right_trans(grad_wvalue, write_value), "head"
    )
    grad_latents_one = norm_one_back(grad_normed_one)[0]
    grad_latent_branch = grad_latents_one.astype(jnp.bfloat16)
    grad_read_out = left_trans(read_mixed, grad_latent_branch)
    grad_rmixed = right_trans(grad_latent_branch, read_out).astype(jnp.bfloat16)
    grad_rmixed_wide = grad_rmixed.astype(jnp.float32)
    delta_own = jnp.sum(heads_view(grad_rmixed_wide * mixed_wide), axis=-1)
    log_own = jnp.log(total_own)
    grad_mixed_all, delta_all, log_all = (
        lax.all_gather(grad_rmixed_wide, "tok", axis=0, tiled=True),
        lax.all_gather(delta_own, "tok", axis=0, tiled=True),
        lax.all_gather(log_own, "tok", axis=0, tiled=True),
    )
    grad_mixed_all = grad_mixed_all.astype(jnp.bfloat16)

    def read_back(carry, operands):
        key_total, value_total = carry
        query_block, image_block, grad_block, delta_block, log_block = operands
        scores, mask = read_scores(query_block, image_block)
        probs = jnp.where(mask, jnp.exp(scores - log_block[:, :, None]), 0.0)
        grad_probs = jnp.einsum(
            "qhd,khd->qhk", heads_view(grad_block), values_split, preferred_element_type=jnp.float32
        )
        grad_scores = (probs * (grad_probs - delta_block[:, :, None])).astype(jnp.bfloat16)
        grad_query = (
            jnp.einsum("qhk,khd->qhd", grad_scores, keys_split, preferred_element_type=jnp.float32)
            * 0.125
        )
        key_total = (
            key_total
            + jnp.einsum(
                "qhk,qhd->khd",
                grad_scores,
                heads_view(query_block),
                preferred_element_type=jnp.float32,
            ).reshape(key_count, column)
            * 0.125
        )
        value_total = value_total + jnp.einsum(
            "qhk,qhd->khd",
            probs,
            heads_view(grad_block),
            precision=triple,
            preferred_element_type=jnp.float32,
        ).reshape(key_count, column)
        return ((key_total, value_total), grad_query.reshape(query_block.shape[0], column))

    key_zeros = jnp.zeros((key_count, column), jnp.float32)
    (grad_keys, grad_values), grad_query_all = lax.scan(
        read_back,
        (key_zeros, key_zeros),
        (
            query_blocks,
            image_blocks,
            grad_mixed_all.reshape(latent_blocks, latent_block, column),
            delta_all.reshape(latent_blocks, latent_block, heads_here),
            log_all.reshape(latent_blocks, latent_block, heads_here),
        ),
    )
    grad_query_all = grad_query_all.reshape(all_latents, column)
    grad_query_own = lax.psum_scatter(
        grad_query_all, "tok", scatter_dimension=0, tiled=True
    ).astype(jnp.bfloat16)
    grad_keys = grad_keys.astype(jnp.bfloat16)
    grad_values = grad_values.astype(jnp.bfloat16)
    grad_key_tok = grad_keys[:rows]
    grad_key_lat = grad_keys[rows:]
    grad_value_tok = grad_values[:rows]
    grad_value_lat = grad_values[rows:]
    grad_read_query = left_trans(normed_lat, grad_query_own)
    grad_read_key = left_trans(normed_x, grad_key_tok) + left_trans(normed_lat, grad_key_lat)
    grad_read_value = left_trans(normed_x, grad_value_tok) + left_trans(normed_lat, grad_value_lat)
    grad_normed_x = (
        right_trans(grad_key_tok, read_key)
        + right_trans(grad_value_tok, read_value)
        + right_trans(grad_wquery, write_query)
    )
    grad_normed_lat = (
        right_trans(grad_query_own, read_query)
        + right_trans(grad_key_lat, read_key)
        + right_trans(grad_value_lat, read_value)
    )
    grad_x_rows, grad_lat_rows = (
        lax.psum_scatter(grad_normed_x, "head", scatter_dimension=0, tiled=True),
        lax.psum_scatter(grad_normed_lat, "head", scatter_dimension=0, tiled=True),
    )
    latent_quarter = owned // head_count
    latent_start = head_index * latent_quarter
    token_rows = lax.dynamic_slice_in_dim(tokens_full, row_start, quarter)
    unused_x, norm_x_back = jax.vjp(norm_rows, token_rows)
    input_grad = (
        lax.dynamic_slice_in_dim(grad_tokens_one, row_start, quarter) + norm_x_back(grad_x_rows)[0]
    )
    latent_rows = lax.dynamic_slice_in_dim(latents_full, latent_start, latent_quarter)
    unused_lat, norm_lat_back = jax.vjp(norm_rows, latent_rows)
    latent_grad = (
        lax.dynamic_slice_in_dim(grad_latents_one, latent_start, latent_quarter)
        + norm_lat_back(grad_lat_rows)[0]
    )
    summed = (
        lax.psum_scatter(grad_read_query, "tok", scatter_dimension=0, tiled=True),
        lax.psum_scatter(grad_read_key, "tok", scatter_dimension=0, tiled=True),
        lax.psum_scatter(grad_read_value, "tok", scatter_dimension=0, tiled=True),
        lax.psum_scatter(grad_read_out, "tok", scatter_dimension=1, tiled=True),
        lax.psum_scatter(grad_write_query, "tok", scatter_dimension=0, tiled=True),
        lax.psum_scatter(grad_write_key, "tok", scatter_dimension=0, tiled=True),
        lax.psum_scatter(grad_write_value, "tok", scatter_dimension=0, tiled=True),
        lax.psum_scatter(grad_write_out, "tok", scatter_dimension=1, tiled=True),
        lax.psum_scatter(grad_mlp_in, "tok", scatter_dimension=0, tiled=True),
        lax.psum_scatter(grad_mlp_out, "tok", scatter_dimension=1, tiled=True),
    )
    return (
        layer_out,
        input_grad,
        latent_grad,
        summed[0],
        summed[1],
        summed[2],
        summed[3],
        summed[4],
        summed[5],
        summed[6],
        summed[7],
        summed[8],
        summed[9],
    )


def solution(mesh):
    return jax.shard_map(
        shards,
        mesh=mesh,
        in_specs=(
            P("tok", None),
            P("tok", None),
            P(),
            P(None, "head"),
            P(None, "head"),
            P(None, "head"),
            P("head", None),
            P(None, "head"),
            P(None, "head"),
            P(None, "head"),
            P("head", None),
            P(None, "head"),
            P("head", None),
            P("tok", None),
        ),
        out_specs=(
            P(("tok", "head"), None),
            P(("tok", "head"), None),
            P(("tok", "head"), None),
            P("tok", "head"),
            P("tok", "head"),
            P("tok", "head"),
            P("head", "tok"),
            P("tok", "head"),
            P("tok", "head"),
            P("tok", "head"),
            P("head", "tok"),
            P("tok", "head"),
            P("head", "tok"),
        ),
        check_vma=False,
    )
```

profile of v0, /device:TPU:0, one launch (start us, length us, event | category | flops | bytes accessed | tf_op | source)
XLA Modules:
  0.0 1754.9 jit_solution(60146640197802202)
XLA Ops:
  25.2 4.5 compare_select_fusion.1
  30.8 35.8 %select_select_fusion.1 = s32[512]{0:T(512)S(1)} fusion(pred[512]{0:T(512)(128)(4,1)S(1)} %get-tuple-element.433, pred[512]{0:T(512)(128)(4,1)S(1)} %get-tuple-element.432, pred[512]{0:T(512)(128)(4,1)S(1)} %get-tuple-element.431, pred[512]{0:T(512)(128)(4,1)S(1)} %get-tuple-element.430, pred[512]{0:T(512)(128)(4,1)S(1)} %get-tuple-element.429, ...), kind=kLoop, calls=%fused_computation.222 | loop fusion | flops 33792 | bytes 35572 | tf_op jit(solution)/shard_map/jit(_take)/select_n | solution.py:70
  66.7 5.2 select_select_fusion
  74.4 32.7 %all_gather.18 = bf16[512,192]{1,0:T(8,128)(2,1)S(1)} all-gather(bf16[64,192]{1,0:T(8,128)(2,1)S(1)} %convolution_convert_fusion.7), channel_id=1, replica_groups=mesh['tok'=8,'head'=4] {'tok'}, dimensions={0}, use_global_device_ids=true | all-gather | bytes 221184 | tf_op jit(solution)/shard_map/all_gather | solution.py:81
  110.3 4.5 fusion.21
  114.9 4.9 fusion.22
  120.9 21.8 %psum.43 = f32[512,3]{0,1:T(4,128)S(1)} all-reduce(f32[512,3]{0,1:T(4,128)S(1)} %get-tuple-element.572), channel_id=1, replica_groups=mesh['tok'=8,'head'=4] {'tok'}, use_global_device_ids=true, to_apply=%region_8.9 | all-reduce | flops 1536 | bytes 12288 | tf_op jit(solution)/shard_map/psum | solution.py:125
  142.9 51.6 %all-reduce.6.cloned.1.call-done = f32[512,192]{1,0:T(8,128)} async-done(((f32[512,192]{1,0:T(8,128)}), f32[512,192]{1,0:T(8,128)}) %all-reduce.6.cloned.1.call-update) | async-done | bytes 393232 | tf_op jit(solution)/shard_map/psum | solution.py:125
  200.4 28.1 %all-reduce.8.cloned.1.call-done = f32[64,768]{1,0:T(8,128)} async-done(((f32[64,768]{1,0:T(8,128)}), f32[64,768]{1,0:T(8,128)}) %all-reduce.8.cloned.1.call-update) | async-done | bytes 196624 | tf_op jit(solution)/shard_map/psum | solution.py:130
  232.0 30.9 %all_gather.19 = bf16[512,192]{1,0:T(8,128)(2,1)S(1)} all-gather(bf16[64,192]{1,0:T(8,128)(2,1)S(1)} %convolution_convert_fusion.6), channel_id=1, replica_groups=mesh['tok'=8,'head'=4] {'tok'}, dimensions={0}, use_global_device_ids=true | all-gather | bytes 221184 | tf_op jit(solution)/shard_map/all_gather | solution.py:136
  263.3 30.8 %all_gather.20 = bf16[512,192]{1,0:T(8,128)(2,1)S(1)} all-gather(bf16[64,192]{1,0:T(8,128)(2,1)S(1)} %convolution_convert_fusion.5), channel_id=1, replica_groups=mesh['tok'=8,'head'=4] {'tok'}, dimensions={0}, use_global_device_ids=true | all-gather | bytes 221184 | tf_op jit(solution)/shard_map/all_gather | solution.py:137
  294.9 18.8 %while.7 = (s32[]{:T(128)}, bf16[4,512,192]{1,2,0:T(8,128)(2,1)S(1)}, f32[4,512,3]{1,2,0:T(4,128)}, s32[4,512]{1,0:T(4,128)S(1)}, s32[512]{0:T(512)S(1)}, /*inde...) while((s32[]{:T(128)}, ...), condition=%wide.region_14.15_spmd, body=%wide.region_12.14_spmd.sunk | while | flops 207190528 | bytes 8686185 | solution.py:172
  319.7 7.1 fusion.102
  326.9 111.2 %all-reduce.10.cloned.1.call-done = f32[2048,768]{1,0:T(8,128)} async-done(((f32[2048,768]{1,0:T(8,128)}), f32[2048,768]{1,0:T(8,128)}) %all-reduce.10.cloned.1.call-update) | async-done | bytes 6291472 | tf_op jit(solution)/shard_map/psum | solution.py:174
  438.1 4.4 fusion.93
  447.5 7.9 fusion.39
  457.0 4.6 fusion.103
  462.1 119.5 %all-reduce.12.cloned.1.call-done = f32[2048,768]{1,0:T(8,128)} async-done(((f32[2048,768]{1,0:T(8,128)}), f32[2048,768]{1,0:T(8,128)}) %all-reduce.12.cloned.1.call-update) | async-done | bytes 6291472 | tf_op jit(solution)/shard_map/psum | solution.py:190
  581.6 5.7 multiply_reduce_fusion
  598.4 41.7 %while.8 = (s32[]{:T(128)}, f32[512,192]{0,1:T(8,128)S(1)}, f32[512,192]{0,1:T(8,128)}, bf16[4,512,192]{1,2,0:T(8,128)(2,1)}, bf16[4,512,192]{1,2,0:T(8,128)(2,1...) while((s32[]{:T(128)}, f32[512,192]{0,1:T(8,128)S(1)}, ...), condition=%wide.region_24.25_spmd.clone, body=%wide.region_22.24_spmd.clone.sunk | while | flops 511343104 | bytes 30055060 | solution.py:232
  643.3 60.2 %reduce-scatter.49.cloned.1.call-done = f32[64,192]{1,0:T(8,128)} async-done(((f32[512,192]{1,0:T(8,128)}), f32[64,192]{1,0:T(8,128)}) %reduce-scatter.49.cloned.1.call-update) | async-done | bytes 49168
  705.6 62.4 %reduce-scatter.51.cloned.1.call-done = f32[64,192]{1,0:T(8,128)} async-done(((f32[512,192]{1,0:T(8,128)}), f32[64,192]{1,0:T(8,128)}) %reduce-scatter.51.cloned.1.call-update) | async-done | bytes 49168
  770.8 26.0 %all-gather = f32[8,64,3]{1,2,0:T(4,128)S(1)} all-gather(f32[1,64,3]{1,2,0:T(4,128)S(1)} %get-tuple-element.476), channel_id=1, replica_groups=mesh['tok'=8,'head'=4] {'tok'}, dimensions={0}, use_global_device_ids=true | all-gather | bytes 6912 | tf_op jit(solution)/shard_map/all_gather | solution.py:265
  796.9 4.8 all-reduce.14.cloned.1.call-done
  805.2 30.9 %all_gather.22 = bf16[512,192]{1,0:T(8,128)(2,1)S(1)} all-gather(bf16[64,192]{1,0:T(8,128)(2,1)S(1)} %get-tuple-element.493), channel_id=1, replica_groups=mesh['tok'=8,'head'=4] {'tok'}, dimensions={0}, use_global_device_ids=true | all-gather | bytes 221184 | tf_op jit(solution)/shard_map/all_gather | solution.py:263
  836.3 26.2 %all-gather.1 = f32[8,64,3]{1,2,0:T(4,128)S(1)} all-gather(f32[1,64,3]{1,2,0:T(4,128)S(1)} %bitcast.380), channel_id=1, replica_groups=mesh['tok'=8,'head'=4] {'tok'}, dimensions={0}, use_global_device_ids=true | all-gather | bytes 6912 | tf_op jit(solution)/shard_map/all_gather | solution.py:264
  862.6 7.8 fusion.17
  875.6 5.0 fusion.51
  881.9 9.3 fusion.45
  891.3 5.0 fusion.44
  896.3 39.7 %reduce-scatter.53.cloned.1.call-done = f32[64,192]{1,0:T(8,128)} async-done(((f32[512,192]{1,0:T(8,128)}), f32[64,192]{1,0:T(8,128)}) %reduce-scatter.53.cloned.1.call-update) | async-done | bytes 49168
  938.6 9.5 fusion.86
  960.4 8.1 fusion.87
  968.8 8.3 fusion.85
  988.3 5.0 convert_element_type.138
  995.0 5.7 reduce-scatter.57.cloned.1.call-done
  1003.7 62.7 %reduce-scatter.55.cloned.1.call-done = f32[96,192]{1,0:T(8,128)} async-done(((f32[768,192]{1,0:T(8,128)}), f32[96,192]{1,0:T(8,128)}) %reduce-scatter.55.cloned.1.call-update) | async-done | bytes 73744
  1068.0 19.5 %reduce-scatter.31.cloned.1.call-done = f32[16,768]{1,0:T(8,128)} async-done(((f32[64,768]{1,0:T(8,128)}), f32[16,768]{1,0:T(8,128)}) %reduce-scatter.31.cloned.1.call-update) | async-done | bytes 49168 | tf_op jit(solution)/shard_map/reduce_scatter | solution.py:338
  1090.2 58.1 %reduce-scatter.27.cloned.1.call-done = f32[512,768]{1,0:T(8,128)} async-done(((f32[2048,768]{1,0:T(8,128)}), f32[512,768]{1,0:T(8,128)}) %reduce-scatter.27.cloned.1.call-update) | async-done | bytes 1572880 | tf_op jit(solution)/shard_map/reduce_scatter | solution.py:182
  1151.3 58.1 %reduce-scatter.29.cloned.1.call-done = f32[512,768]{1,0:T(8,128)} async-done(((f32[2048,768]{1,0:T(8,128)}), f32[512,768]{1,0:T(8,128)}) %reduce-scatter.29.cloned.1.call-update) | async-done | bytes 1572880 | tf_op jit(solution)/shard_map/reduce_scatter | solution.py:337
  1217.0 58.7 %reduce-scatter.39.cloned.1.call-done = f32[96,192]{1,0:T(8,128)} async-done(((f32[768,192]{1,0:T(8,128)}), f32[96,192]{1,0:T(8,128)}) %reduce-scatter.39.cloned.1.call-update) | async-done | bytes 73744 | tf_op jit(solution)/shard_map/reduce_scatter | solution.py:358
  1275.7 72.3 %reduce-scatter.45.cloned.1.call-done = f32[96,768]{1,0:T(8,128)} async-done(((f32[768,768]{1,0:T(8,128)}), f32[96,768]{1,0:T(8,128)}) %reduce-scatter.45.cloned.1.call-update) | async-done | bytes 294928 | tf_op jit(solution)/shard_map/reduce_scatter | solution.py:362
  1348.0 72.5 %reduce-scatter.47.cloned.1.call-done = f32[768,96]{0,1:T(8,128)} async-done(((f32[768,768]{0,1:T(8,128)}), f32[768,96]{0,1:T(8,128)}) %reduce-scatter.47.cloned.1.call-update) | async-done | bytes 294928 | tf_op jit(solution)/shard_map/reduce_scatter | solution.py:363
  1420.4 65.7 %reduce-scatter.41.cloned.1.call-done = f32[96,192]{1,0:T(8,128)} async-done(((f32[768,192]{1,0:T(8,128)}), f32[96,192]{1,0:T(8,128)}) %reduce-scatter.41.cloned.1.call-update) | async-done | bytes 73744 | tf_op jit(solution)/shard_map/reduce_scatter | solution.py:359
  1486.1 65.2 %reduce-scatter.43.cloned.1.call-done = f32[96,192]{1,0:T(8,128)} async-done(((f32[768,192]{1,0:T(8,128)}), f32[96,192]{1,0:T(8,128)}) %reduce-scatter.43.cloned.1.call-update) | async-done | bytes 73744 | tf_op jit(solution)/shard_map/reduce_scatter | solution.py:360
  1551.3 65.7 %reduce-scatter.37.cloned.1.call-done = f32[96,192]{1,0:T(8,128)} async-done(((f32[768,192]{1,0:T(8,128)}), f32[96,192]{1,0:T(8,128)}) %reduce-scatter.37.cloned.1.call-update) | async-done | bytes 73744 | tf_op jit(solution)/shard_map/reduce_scatter | solution.py:356
  1617.0 65.1 %reduce-scatter.35.cloned.1.call-done = f32[96,192]{1,0:T(8,128)} async-done(((f32[768,192]{1,0:T(8,128)}), f32[96,192]{1,0:T(8,128)}) %reduce-scatter.35.cloned.1.call-update) | async-done | bytes 73744 | tf_op jit(solution)/shard_map/reduce_scatter | solution.py:355
  1682.1 65.7 %reduce-scatter.33.cloned.1.call-done = f32[96,192]{1,0:T(8,128)} async-done(((f32[768,192]{1,0:T(8,128)}), f32[96,192]{1,0:T(8,128)}) %reduce-scatter.33.cloned.1.call-update) | async-done | bytes 73744 | tf_op jit(solution)/shard_map/reduce_scatter | solution.py:354
  (365 shorter events, 184.5 us)
Async XLA Ops:
  7.2 436.2 %copy-start = (bf16[768,768]{1,0:T(8,128)(2,1)S(1)}, bf16[768,768]{1,0:T(8,128)(2,1)}, u32[]{:S(2)}) copy-start(bf16[768,768]{1,0:T(8,128)(2,1)} %param.33) | copy-start | bytes 3538948
  7.2 187.3 %all-reduce.6.cloned.1.call-start = ((), (), s32[]{:S(2)}) async-start(), calls=%async_computation.16 | async-start | bytes 1048576 | tf_op jit(solution)/shard_map/psum | solution.py:125
  12.3 60.7 %copy-start.39 = (f32[64]{0:T(128)}, f32[64]{0:T(128)S(1)}, u32[]{:S(2)}) copy-start(f32[64]{0:T(128)S(1)} %broadcast_multiply_fusion.5) | copy-start | bytes 772
  13.4 59.6 %copy-start.43 = (f32[64]{0:T(128)}, f32[64]{0:T(128)S(1)}, u32[]{:S(2)}) copy-start(f32[64]{0:T(128)S(1)} %add_rsqrt_fusion.1) | copy-start | bytes 772
  20.9 45.8 %copy-start.45 = (pred[2048]{0:T(1024)(128)(4,1)S(1)}, pred[2048]{0:T(1024)(128)(4,1)}, u32[]{:S(2)}) copy-start(pred[2048]{0:T(1024)(128)(4,1)} %constant.410) | copy-start | bytes 6148
  20.9 45.8 %copy-start.46 = (pred[2048]{0:T(1024)(128)(4,1)S(1)}, pred[2048]{0:T(1024)(128)(4,1)}, u32[]{:S(2)}) copy-start(pred[2048]{0:T(1024)(128)(4,1)} %constant.411) | copy-start | bytes 6148
  20.9 45.8 %copy-start.47 = (pred[2048]{0:T(1024)(128)(4,1)S(1)}, pred[2048]{0:T(1024)(128)(4,1)}, u32[]{:S(2)}) copy-start(pred[2048]{0:T(1024)(128)(4,1)} %constant.412) | copy-start | bytes 6148
  20.9 45.8 %copy-start.48 = (pred[2048]{0:T(1024)(128)(4,1)S(1)}, pred[2048]{0:T(1024)(128)(4,1)}, u32[]{:S(2)}) copy-start(pred[2048]{0:T(1024)(128)(4,1)} %constant.413) | copy-start | bytes 6148
  20.9 45.8 %copy-start.49 = (pred[2048]{0:T(1024)(128)(4,1)S(1)}, pred[2048]{0:T(1024)(128)(4,1)}, u32[]{:S(2)}) copy-start(pred[2048]{0:T(1024)(128)(4,1)} %constant.414) | copy-start | bytes 6148
  20.9 45.8 %copy-start.50 = (pred[2048]{0:T(1024)(128)(4,1)S(1)}, pred[2048]{0:T(1024)(128)(4,1)}, u32[]{:S(2)}) copy-start(pred[2048]{0:T(1024)(128)(4,1)} %constant.415) | copy-start | bytes 6148
  21.0 45.7 %copy-start.51 = (pred[2048]{0:T(1024)(128)(4,1)S(1)}, pred[2048]{0:T(1024)(128)(4,1)}, u32[]{:S(2)}) copy-start(pred[2048]{0:T(1024)(128)(4,1)} %constant.416) | copy-start | bytes 6148
  22.2 92.7 %copy-start.30 = (bf16[2048,192]{0,1:T(8,128)(2,1)}, bf16[2048,192]{0,1:T(8,128)(2,1)S(1)}, u32[]{:S(2)}) copy-start(bf16[2048,192]{0,1:T(8,128)(2,1)S(1)} %convolution_convert_fusion.1) | copy-start | bytes 2359300
  73.0 41.9 %copy-start.28 = (pred[512,2112]{0,1:T(8,128)(4,1)}, pred[512,2112]{0,1:T(8,128)(4,1)S(1)}, u32[]{:S(2)}) copy-start(pred[512,2112]{0,1:T(8,128)(4,1)S(1)} %broadcast_compare_fusion.2) | copy-start | bytes 3244036
  114.9 80.5 %copy-start.24 = (bf16[192,768]{1,0:T(8,128)(2,1)S(1)}, bf16[192,768]{1,0:T(8,128)(2,1)}, u32[]{:S(2)}) copy-start(bf16[192,768]{1,0:T(8,128)(2,1)} %param.28) | copy-start | bytes 884740
  119.8 111.9 %copy-start.26 = (bf16[768,192]{0,1:T(8,128)(2,1)S(1)}, bf16[768,192]{0,1:T(8,128)(2,1)}, u32[]{:S(2)}) copy-start(bf16[768,192]{0,1:T(8,128)(2,1)} %param.30) | copy-start | bytes 884740
  119.8 143.2 %copy-start.27 = (bf16[768,192]{0,1:T(8,128)(2,1)S(1)}, bf16[768,192]{0,1:T(8,128)(2,1)}, u32[]{:S(2)}) copy-start(bf16[768,192]{0,1:T(8,128)(2,1)} %param.31) | copy-start | bytes 884740
  120.9 107.6 %all-reduce.8.cloned.1.call-start = ((), (), s32[]{:S(2)}) async-start(), calls=%async_computation.17 | async-start | bytes 393216 | tf_op jit(solution)/shard_map/psum | solution.py:130
  196.3 241.8 %all-reduce.10.cloned.1.call-start = ((), (), s32[]{:S(2)}) async-start(), calls=%async_computation.18 | async-start | bytes 12582912 | tf_op jit(solution)/shard_map/psum | solution.py:174
  229.6 65.3 %copy-start.42 = (f32[64]{0:T(128)}, f32[64]{0:T(128)S(1)}, u32[]{:S(2)}) copy-start(f32[64]{0:T(128)S(1)} %broadcast_multiply_fusion.4) | copy-start | bytes 772
  230.7 64.2 %copy-start.53 = (f32[64]{0:T(128)}, f32[64]{0:T(128)S(1)}, u32[]{:S(2)}) copy-start(f32[64]{0:T(128)S(1)} %multiply_reduce_fusion.6) | copy-start | bytes 772
  230.7 64.2 %copy-start.52 = (f32[64]{0:T(128)}, f32[64]{0:T(128)S(1)}, u32[]{:S(2)}) copy-start(f32[64]{0:T(128)S(1)} %fusion.74) | copy-start | bytes 772
  231.8 63.1 %copy-start.15 = (bf16[64,768]{1,0:T(8,128)(2,1)}, bf16[64,768]{1,0:T(8,128)(2,1)S(1)}, u32[]{:S(2)}) copy-start(bf16[64,768]{1,0:T(8,128)(2,1)S(1)} %multiply_convert_fusion.3) | copy-start | bytes 294916
  294.9 19.9 %copy-start.17 = (bf16[192,768]{1,0:T(8,128)(2,1)S(1)}, bf16[192,768]{1,0:T(8,128)(2,1)}, u32[]{:S(2)}) copy-start(bf16[192,768]{1,0:T(8,128)(2,1)} %param.32) | copy-start | bytes 884740
  318.5 263.1 %all-reduce.12.cloned.1.call-start = ((), (), s32[]{:S(2)}) async-start(), calls=%async_computation.20 | async-start | bytes 12582912 | tf_op jit(solution)/shard_map/psum | solution.py:190
  461.7 241.8 %reduce-scatter.49.cloned.1.call-start = ((), (), s32[]{:S(2)}) async-start(), calls=%async_computation.32 | async-start | bytes 589824
  640.1 164.8 %copy-start.25 = (bf16[192,768]{1,0:T(8,128)(2,1)S(1)}, bf16[192,768]{1,0:T(8,128)(2,1)}, u32[]{:S(2)}) copy-start(bf16[192,768]{1,0:T(8,128)(2,1)} %param.28) | copy-start | bytes 884740
  640.1 222.5 %copy-start.29 = (pred[512,2112]{0,1:T(8,128)(4,1)S(1)}, pred[512,2112]{0,1:T(8,128)(4,1)}, u32[]{:S(2)}) copy-start(pred[512,2112]{0,1:T(8,128)(4,1)} %copy-done.28) | copy-start | bytes 3244036
  640.1 222.5 %copy-start.38 = (bf16[64,192]{0,1:T(8,128)(2,1)S(1)}, bf16[64,192]{0,1:T(8,128)(2,1)}, u32[]{:S(2)}) copy-start(bf16[64,192]{0,1:T(8,128)(2,1)} %copy.144) | copy-start | bytes 73732
  641.2 126.8 %reduce-scatter.51.cloned.1.call-start = ((), (), s32[]{:S(2)}) async-start(), calls=%async_computation.33 | async-start | bytes 589824
  643.3 158.4 %all-reduce.14.cloned.1.call-start = ((), (), s32[]{:S(2)}) async-start(), calls=%async_computation.21 | async-start | bytes 393216 | tf_op jit(solution)/shard_map/psum | solution.py:252
  770.8 165.2 %reduce-scatter.53.cloned.1.call-start = ((), (), s32[]{:S(2)}) async-start(), calls=%async_computation.34 | async-start | bytes 589824
  875.5 125.3 %reduce-scatter.57.cloned.1.call-start = ((), (), s32[]{:S(2)}) async-start(), calls=%async_computation.36 | async-start | bytes 884736
  880.6 185.8 %reduce-scatter.55.cloned.1.call-start = ((), (), s32[]{:S(2)}) async-start(), calls=%async_computation.35 | async-start | bytes 884736
  881.9 205.7 %reduce-scatter.31.cloned.1.call-start = ((), (), s32[]{:S(2)}) async-start(), calls=%async_computation.23 | async-start | bytes 245760 | tf_op jit(solution)/shard_map/reduce_scatter | solution.py:338
  891.2 45.7 %copy-start.33 = (bf16[768,192]{0,1:T(8,128)(2,1)S(1)}, bf16[768,192]{0,1:T(8,128)(2,1)}, u32[]{:S(2)}) copy-start(bf16[768,192]{0,1:T(8,128)(2,1)} %param.25) | copy-start | bytes 884740
  891.2 45.9 %copy-start.22 = (bf16[768,192]{0,1:T(8,128)(2,1)S(1)}, bf16[768,192]{0,1:T(8,128)(2,1)}, u32[]{:S(2)}) copy-start(bf16[768,192]{0,1:T(8,128)(2,1)} %param.26) | copy-start | bytes 884740
  891.2 46.2 %copy-start.20 = (bf16[768,192]{0,1:T(8,128)(2,1)S(1)}, bf16[768,192]{0,1:T(8,128)(2,1)}, u32[]{:S(2)}) copy-start(bf16[768,192]{0,1:T(8,128)(2,1)} %param.27) | copy-start | bytes 884740
  938.3 210.0 %reduce-scatter.27.cloned.1.call-start = ((), (), s32[]{:S(2)}) async-start(), calls=%async_computation.19 | async-start | bytes 7864320 | tf_op jit(solution)/shard_map/reduce_scatter | solution.py:182
  948.1 261.3 %reduce-scatter.29.cloned.1.call-start = ((), (), s32[]{:S(2)}) async-start(), calls=%async_computation.22 | async-start | bytes 7864320 | tf_op jit(solution)/shard_map/reduce_scatter | solution.py:337
  955.4 320.3 %reduce-scatter.39.cloned.1.call-start = ((), (), s32[]{:S(2)}) async-start(), calls=%async_computation.27 | async-start | bytes 884736 | tf_op jit(solution)/shard_map/reduce_scatter | solution.py:358
  960.3 387.6 %reduce-scatter.45.cloned.1.call-start = ((), (), s32[]{:S(2)}) async-start(), calls=%async_computation.30 | async-start | bytes 2654208 | tf_op jit(solution)/shard_map/reduce_scatter | solution.py:362
  968.5 451.9 %reduce-scatter.47.cloned.1.call-start = ((), (), s32[]{:S(2)}) async-start(), calls=%async_computation.31 | async-start | bytes 2654208 | tf_op jit(solution)/shard_map/reduce_scatter | solution.py:363
  977.1 509.0 %reduce-scatter.41.cloned.1.call-start = ((), (), s32[]{:S(2)}) async-start(), calls=%async_computation.28 | async-start | bytes 884736 | tf_op jit(solution)/shard_map/reduce_scatter | solution.py:359
  978.4 572.9 %reduce-scatter.43.cloned.1.call-start = ((), (), s32[]{:S(2)}) async-start(), calls=%async_computation.29 | async-start | bytes 884736 | tf_op jit(solution)/shard_map/reduce_scatter | solution.py:360
  979.7 637.3 %reduce-scatter.37.cloned.1.call-start = ((), (), s32[]{:S(2)}) async-start(), calls=%async_computation.26 | async-start | bytes 884736 | tf_op jit(solution)/shard_map/reduce_scatter | solution.py:356
  984.0 698.2 %reduce-scatter.35.cloned.1.call-start = ((), (), s32[]{:S(2)}) async-start(), calls=%async_computation.25 | async-start | bytes 884736 | tf_op jit(solution)/shard_map/reduce_scatter | solution.py:355
  988.2 759.6 %reduce-scatter.33.cloned.1.call-start = ((), (), s32[]{:S(2)}) async-start(), calls=%async_computation.24 | async-start | bytes 884736 | tf_op jit(solution)/shard_map/reduce_scatter | solution.py:354
  1148.3 599.5 %copy-start.1 = (bf16[768,768]{1,0:T(8,128)(2,1)S(1)}, bf16[768,768]{1,0:T(8,128)(2,1)}, u32[]{:S(2)}) copy-start(bf16[768,768]{1,0:T(8,128)(2,1)} %param.33) | copy-start | bytes 3538948
  (32 other events, 154.0 us)
Sparse Core Ops, SparseCore 0:
  121.0 73.4 all-reduce.5
  197.5 30.9 all-reduce.7
  318.6 119.4 all-reduce.9
  461.8 119.7 all-reduce.11
  641.3 62.1 reduce-scatter.48
  707.0 60.8 reduce-scatter.50
  770.9 30.7 all-reduce.13
  875.6 60.3 reduce-scatter.52
  939.3 61.4 reduce-scatter.56
  1004.9 61.4 reduce-scatter.54
  1068.8 18.6 reduce-scatter.30
  1089.9 58.3 reduce-scatter.26
  1151.0 58.3 reduce-scatter.28
  1213.2 62.4 reduce-scatter.38
  1280.0 67.9 reduce-scatter.44
  1352.3 68.0 reduce-scatter.46
  1424.5 61.5 reduce-scatter.40
  1489.8 61.4 reduce-scatter.42
  1555.5 61.4 reduce-scatter.36
  1620.8 61.3 reduce-scatter.34
  1686.4 61.4 reduce-scatter.32
where the time goes:
time: 1760 us; the launch traced here: 1750 us
  waiting for transfers between devices  1210 us (69%)
  blocking collectives  199 us (11%)
  matrix products  155 us (9%)
  other arithmetic  112 us (6%)
  local copies, waits for them, and re-layouts  58.3 us (3%)
    unnamed x26, waiting for transfers between devices  231 us
    psum x1, waiting for transfers between devices, shards(): grad_normed_two = lax.psum(right_trans(grad_inner, mlp_in), 'head')  119 us
    psum x1, waiting for transfers between devices, shards(): tokens_one = tokens_full + lax.psum(matmul(write_mixed, write_out), 'head')  111 us
    reduce_scatter x1, waiting for transfers between devices, shards(): lax.psum_scatter(grad_mlp_out, 'tok', scatter_dimension=1, tiled=True)  72.5 us
    reduce_scatter x1, waiting for transfers between devices, shards(): lax.psum_scatter(grad_mlp_in, 'tok', scatter_dimension=0, tiled=True)  72.3 us
    reduce_scatter x1, waiting for transfers between devices, shards(): lax.psum_scatter(grad_read_value, 'tok', scatter_dimension=0, tiled=True)  65.7 us
    reduce_scatter x1, waiting for transfers between devices, shards(): lax.psum_scatter(grad_read_query, 'tok', scatter_dimension=0, tiled=True)  65.7 us
    reduce_scatter x1, waiting for transfers between devices, shards(): lax.psum_scatter(grad_write_key, 'tok', scatter_dimension=0, tiled=True)  65.7 us
  transfers between devices with their start and end apart: 21, of which 21 were waited for; matrix products, arithmetic and copies ran while one was open for 6% of the time, Pallas kernels for 0%

commit v1 on v0

--- a/solution.py
+++ b/solution.py
@@ -1,7 +1,13 @@
+from functools import partial
+
 import jax
 import jax.numpy as jnp
 from jax import lax
+from jax.experimental import pallas as pl
+from jax.experimental.pallas import tpu as pltpu
 from jax.sharding import PartitionSpec as P
+
+MESH = pl.DeviceIdType.MESH
 
 HD = 64
 GROUP = 256
@@ -31,6 +37,94 @@
     return lax.dot_general(
         left, right, (((1,), (1,)), ((), ())), preferred_element_type=jnp.float32
     )
+
+
+def grad_kernel(outer, parts_ref, out_ref, got_one, sums, got_two, send_one, recv_one, send_two, recv_two):
+    tok = lax.axis_index("tok")
+    head = lax.axis_index("head")
+    mine = tok // 2
+    side = lax.rem(tok, 2)
+    partner = mine * 2 + (1 - side)
+    barrier = pltpu.get_barrier_semaphore()
+    pl.semaphore_signal(barrier, inc=1, device_id=(partner, head), device_id_type=MESH)
+
+    def greet(step, carry):
+        peer = lax.rem(mine + step, outer) * 2 + side
+        pl.semaphore_signal(barrier, inc=1, device_id=(peer, head), device_id_type=MESH)
+        return carry
+
+    lax.fori_loop(1, outer, greet, 0)
+    pl.semaphore_wait(barrier, outer)
+
+    def first(block):
+        return pltpu.make_async_remote_copy(
+            src_ref=parts_ref.at[block, 1 - side],
+            dst_ref=got_one.at[block],
+            send_sem=send_one.at[block],
+            recv_sem=recv_one.at[block],
+            device_id=(partner, head),
+            device_id_type=MESH,
+        )
+
+    def second(block, source):
+        return pltpu.make_async_remote_copy(
+            src_ref=sums.at[block],
+            dst_ref=got_two.at[source],
+            send_sem=send_two.at[block],
+            recv_sem=recv_two.at[source],
+            device_id=(block * 2 + side, head),
+            device_id_type=MESH,
+        )
+
+    def start_first(step, carry):
+        first(lax.rem(mine + step, outer)).start()
+        return carry
+
+    lax.fori_loop(1, outer + 1, start_first, 0)
+
+    def start_second(step, carry):
+        block = lax.rem(mine + step, outer)
+        first(block).wait()
+        total = parts_ref[block, side].astype(jnp.float32) + got_one[block].astype(jnp.float32)
+        sums[block] = total.astype(jnp.bfloat16)
+        second(block, mine).start()
+        return carry
+
+    lax.fori_loop(1, outer, start_second, 0)
+    first(mine).wait()
+    out_ref[...] = parts_ref[mine, side].astype(jnp.float32) + got_one[mine].astype(jnp.float32)
+
+    def finish(step, carry):
+        source = lax.rem(mine + step, outer)
+        second(lax.rem(mine + outer - step, outer), source).wait_recv()
+        out_ref[...] += got_two[source].astype(jnp.float32)
+        return carry
+
+    lax.fori_loop(1, outer, finish, 0)
+
+    def drain(step, carry):
+        second(lax.rem(mine + step, outer), mine).wait_send()
+        return carry
+
+    lax.fori_loop(1, outer, drain, 0)
+
+
+def scatter_grads(parts, tok_count):
+    outer = tok_count // 2
+    rows, width = parts.shape[0] // tok_count, parts.shape[1]
+    slots = pltpu.VMEM((outer, rows, width), jnp.bfloat16)
+    sems = pltpu.SemaphoreType.DMA((outer,))
+    return pl.pallas_call(
+        partial(grad_kernel, outer),
+        out_shape=jax.ShapeDtypeStruct((rows, width), jnp.float32),
+        in_specs=[pl.BlockSpec(memory_space=pltpu.VMEM)],
+        out_specs=pl.BlockSpec(memory_space=pltpu.VMEM),
+        scratch_shapes=[slots, slots, slots, sems, sems, sems, sems],
+        compiler_params=pltpu.CompilerParams(
+            collective_id=0, has_side_effects=True, vmem_limit_bytes=56 << 20
+        ),
+        name="grad_scatter",
+    )(parts.reshape(outer, 2, rows, width))
 
 
 def heads_view(values):
@@ -183,14 +277,14 @@
     layer_out = (lax.dynamic_slice_in_dim(tokens_one, row_start, quarter) + branch).astype(
         jnp.bfloat16
     )
-    grad_mlp_out = left_trans(activated, cotangent)
+    grad_mlp_out = left_trans(cotangent, activated)
     grad_act = right_trans(cotangent, mlp_out)
     grad_inner = gelu_back(grad_act)[0].astype(jnp.bfloat16)
     grad_mlp_in = left_trans(normed_two, grad_inner)
     grad_normed_two = lax.psum(right_trans(grad_inner, mlp_in), "head")
     grad_tokens_one = cotangent.astype(jnp.float32) + norm_two_back(grad_normed_two)[0]
     grad_branch = grad_tokens_one.astype(jnp.bfloat16)
-    grad_write_out = left_trans(write_mixed, grad_branch)
+    grad_write_out = left_trans(grad_branch, write_mixed)
     grad_wmixed = right_trans(grad_branch, write_out).astype(jnp.bfloat16)
 
     def write_back(carry, operands):
@@ -254,7 +348,7 @@
     )
     grad_latents_one = norm_one_back(grad_normed_one)[0]
     grad_latent_branch = grad_latents_one.astype(jnp.bfloat16)
-    grad_read_out = left_trans(read_mixed, grad_latent_branch)
+    grad_read_out = left_trans(grad_latent_branch, read_mixed)
     grad_rmixed = right_trans(grad_latent_branch, read_out).astype(jnp.bfloat16)
     grad_rmixed_wide = grad_rmixed.astype(jnp.float32)
     delta_own = jnp.sum(heads_view(grad_rmixed_wide * mixed_wide), axis=-1)
@@ -350,18 +444,28 @@
         lax.dynamic_slice_in_dim(grad_latents_one, latent_start, latent_quarter)
         + norm_lat_back(grad_lat_rows)[0]
     )
-    summed = (
-        lax.psum_scatter(grad_read_query, "tok", scatter_dimension=0, tiled=True),
-        lax.psum_scatter(grad_read_key, "tok", scatter_dimension=0, tiled=True),
-        lax.psum_scatter(grad_read_value, "tok", scatter_dimension=0, tiled=True),
-        lax.psum_scatter(grad_read_out, "tok", scatter_dimension=1, tiled=True),
-        lax.psum_scatter(grad_write_query, "tok", scatter_dimension=0, tiled=True),
-        lax.psum_scatter(grad_write_key, "tok", scatter_dimension=0, tiled=True),
-        lax.psum_scatter(grad_write_value, "tok", scatter_dimension=0, tiled=True),
-        lax.psum_scatter(grad_write_out, "tok", scatter_dimension=1, tiled=True),
-        lax.psum_scatter(grad_mlp_in, "tok", scatter_dimension=0, tiled=True),
-        lax.psum_scatter(grad_mlp_out, "tok", scatter_dimension=1, tiled=True),
-    )
+    partials = jnp.concatenate(
+        [
+            grad_read_query,
+            grad_read_key,
+            grad_read_value,
+            grad_read_out,
+            grad_write_query,
+            grad_write_key,
+            grad_write_value,
+            grad_write_out,
+            grad_mlp_in,
+            grad_mlp_out,
+        ],
+        axis=1,
+    ).astype(jnp.bfloat16)
+    grads = scatter_grads(partials, tok_count)
+    summed = [grads[:, k * column : (k + 1) * column] for k in range(8)]
+    hidden = mlp_in.shape[1]
+    summed.append(grads[:, 8 * column : 8 * column + hidden])
+    summed.append(grads[:, 8 * column + hidden :].T)
+    summed[3] = summed[3].T
+    summed[7] = summed[7].T
     return (
         layer_out,
         input_grad,

time: 1760 us -> 1120 us (0.64)
  waiting for transfers between devices: 1210 us -> 482 us
  Pallas kernels: 0 us -> 69.4 us
  local copies, waits for them, and re-layouts: 58.3 us -> 80 us
    reduce_scatter x8 -> x0, waiting for transfers between devices: 531 us -> none  [the longest x1 72.5 us: shards(): lax.psum_scatter(grad_mlp_out, 'tok', scatter_dimension=1, tiled=True)]
    pallas_call x0 -> x1, Pallas kernels: none -> 69.4 us  [scatter_grads(): pl.pallas_call(partial(grad_kernel, outer), out_shape=jax.ShapeDtypeStruc...]
    unnamed x26 -> x14, waiting for transfers between devices: 231 us -> 167 us
    reduce_scatter x1, waiting for transfers between devices: 58.1 us -> 0.01 us  [shards(): lax.psum_scatter(matmul(activated, mlp_out), 'head', scatter_dimension=0,...]
    reduce_scatter x1, waiting for transfers between devices: 58.1 us -> 0.01 us  [shards(): lax.psum_scatter(grad_normed_x, 'head', scatter_dimension=0, tiled=True)]
    reduce_scatter x1, waiting for transfers between devices: 19.5 us -> 0.01 us  [shards(): lax.psum_scatter(grad_normed_lat, 'head', scatter_dimension=0, tiled=True)]
  transfers between devices with their start and end apart: 21 -> 11, of which waited for: 21 -> 8; matrix products, arithmetic and copies ran while one was open for 6% -> 11% of each run, Pallas kernels for 0% -> 6%
where the time goes in v1:
time: 1120 us; the launch traced here: 1110 us
  waiting for transfers between devices  482 us (43%)
  blocking collectives  200 us (18%)
  matrix products  147 us (13%)
  other arithmetic  114 us (10%)
  local copies, waits for them, and re-layouts  80 us (7%)
  Pallas kernels  69.4 us (6%)
  between operations  15.8 us (1%)
    unnamed x14, waiting for transfers between devices  167 us
    psum x1, waiting for transfers between devices, shards(): grad_normed_two = lax.psum(right_trans(grad_inner, mlp_in), 'head')  119 us
    psum x1, waiting for transfers between devices, shards(): tokens_one = tokens_full + lax.psum(matmul(write_mixed, write_out), 'head')  111 us
    pallas_call x1, Pallas kernels, scatter_grads(): pl.pallas_call(partial(grad_kernel, outer), out_shape=jax.ShapeDtypeStruc...  69.4 us
    psum x1, waiting for transfers between devices, shards(): totals_all, sums_all = lax.psum((totals, sums), 'tok')  50.8 us
    select_n x1, other arithmetic, shards(): latent_image = jnp.repeat(group_image, LPG, total_repeat_length=all_latents)  35.8 us
    dot_general x12, matrix products, matmul(): return jnp.dot(left, right, preferred_element_type=jnp.float32)  33.2 us
    all_gather x1, blocking collectives, shards(): query_all = lax.all_gather(query_own, 'tok', axis=0, tiled=True)  32.8 us
  transfers between devices with their start and end apart: 11, of which 8 were waited for; matrix products, arithmetic and copies ran while one was open for 11% of the time, Pallas kernels for 6%

profile of v1, /device:TPU:0, one launch (start us, length us, event | category | flops | bytes accessed | tf_op | source)
XLA Modules:
  0.0 1109.8 jit_solution(14670192761978673255)
XLA Ops:
  23.3 4.5 compare_select_fusion.1
  28.9 35.8 %select_select_fusion.1 = s32[512]{0:T(512)S(1)} fusion(pred[512]{0:T(512)(128)(4,1)S(1)} %get-tuple-element.524, pred[512]{0:T(512)(128)(4,1)S(1)} %get-tuple-element.523, pred[512]{0:T(512)(128)(4,1)S(1)} %get-tuple-element.522, pred[512]{0:T(512)(128)(4,1)S(1)} %get-tuple-element.521, pred[512]{0:T(512)(128)(4,1)S(1)} %get-tuple-element.520, ...), kind=kLoop, calls=%fused_computation.231 | loop fusion | flops 33792 | bytes 35572 | tf_op jit(solution)/shard_map/jit(_take)/select_n | solution.py:164
  64.8 5.2 select_select_fusion
  72.5 32.8 %all_gather.18 = bf16[512,192]{1,0:T(8,128)(2,1)S(1)} all-gather(bf16[64,192]{1,0:T(8,128)(2,1)S(1)} %convolution_convert_fusion.15), channel_id=1, replica_groups=mesh['tok'=8,'head'=4] {'tok'}, dimensions={0}, use_global_device_ids=true | all-gather | bytes 221184 | tf_op jit(solution)/shard_map/all_gather | solution.py:175
  108.4 4.5 fusion.21
  113.0 4.9 fusion.22
  119.0 22.0 %psum.43 = f32[512,3]{0,1:T(4,128)S(1)} all-reduce(f32[512,3]{0,1:T(4,128)S(1)} %get-tuple-element.675), channel_id=1, replica_groups=mesh['tok'=8,'head'=4] {'tok'}, use_global_device_ids=true, to_apply=%region_8.9 | all-reduce | flops 1536 | bytes 12288 | tf_op jit(solution)/shard_map/psum | solution.py:219
  141.8 50.8 %all-reduce.6.cloned.1.call-done = f32[512,192]{1,0:T(8,128)} async-done(((f32[512,192]{1,0:T(8,128)}), f32[512,192]{1,0:T(8,128)}) %all-reduce.6.cloned.1.call-update) | async-done | bytes 393232 | tf_op jit(solution)/shard_map/psum | solution.py:219
  194.4 3.1 convolution_convert_fusion.3
  198.5 28.1 %all-reduce.8.cloned.1.call-done = f32[64,768]{1,0:T(8,128)} async-done(((f32[64,768]{1,0:T(8,128)}), f32[64,768]{1,0:T(8,128)}) %all-reduce.8.cloned.1.call-update) | async-done | bytes 196624 | tf_op jit(solution)/shard_map/psum | solution.py:224
  231.1 30.9 %all_gather.19 = bf16[512,192]{1,0:T(8,128)(2,1)S(1)} all-gather(bf16[64,192]{1,0:T(8,128)(2,1)S(1)} %convolution_convert_fusion.14), channel_id=1, replica_groups=mesh['tok'=8,'head'=4] {'tok'}, dimensions={0}, use_global_device_ids=true | all-gather | bytes 221184 | tf_op jit(solution)/shard_map/all_gather | solution.py:230
  262.3 30.8 %all_gather.20 = bf16[512,192]{1,0:T(8,128)(2,1)S(1)} all-gather(bf16[64,192]{1,0:T(8,128)(2,1)S(1)} %convolution_convert_fusion.13), channel_id=1, replica_groups=mesh['tok'=8,'head'=4] {'tok'}, dimensions={0}, use_global_device_ids=true | all-gather | bytes 221184 | tf_op jit(solution)/shard_map/all_gather | solution.py:231
  294.0 16.5 %while.7 = (s32[]{:T(128)}, bf16[4,512,192]{1,2,0:T(8,128)(2,1)S(1)}, f32[4,512,3]{1,2,0:T(4,128)S(1)}, s32[4,512]{1,0:T(4,128)S(1)}, s32[512]{0:T(512)S(1)}, /*...) while((s32[]{:T(128)}, ...), condition=%wide.region_14.15_spmd, body=%wide.region_12.14_spmd.sunk | while | flops 207190528 | bytes 8687725 | solution.py:266
  310.6 4.8 fusion.95
  316.7 7.1 fusion.96
  323.9 111.2 %all-reduce.10.cloned.1.call-done = f32[2048,768]{1,0:T(8,128)} async-done(((f32[2048,768]{1,0:T(8,128)}), f32[2048,768]{1,0:T(8,128)}) %all-reduce.10.cloned.1.call-update) | async-done | bytes 6291472 | tf_op jit(solution)/shard_map/psum | solution.py:268
  435.0 4.4 fusion.87
  440.4 4.2 copy-done.79
  444.5 7.9 fusion.39
  454.1 4.5 fusion.97
  459.1 119.4 %all-reduce.12.cloned.1.call-done = f32[2048,768]{1,0:T(8,128)} async-done(((f32[2048,768]{1,0:T(8,128)}), f32[2048,768]{1,0:T(8,128)}) %all-reduce.12.cloned.1.call-update) | async-done | bytes 6291472 | tf_op jit(solution)/shard_map/psum | solution.py:284
  578.6 5.7 multiply_reduce_fusion
  584.9 4.0 fusion.86
  595.7 39.1 %while.8 = (s32[]{:T(128)}, f32[512,192]{0,1:T(8,128)S(1)}, f32[512,192]{0,1:T(8,128)}, bf16[4,512,192]{1,2,0:T(8,128)(2,1)}, bf16[4,512,192]{1,2,0:T(8,128)(2,1...) while((s32[]{:T(128)}, f32[512,192]{0,1:T(8,128)S(1)}, ...), condition=%wide.region_24.25_spmd.clone, body=%wide.region_22.24_spmd.clone.sunk | while | flops 511343104 | bytes 30055060 | solution.py:326
  638.1 60.1 %reduce-scatter.19.cloned.1.call-done = f32[64,192]{1,0:T(8,128)} async-done(((f32[512,192]{1,0:T(8,128)}), f32[64,192]{1,0:T(8,128)}) %reduce-scatter.19.cloned.1.call-update) | async-done | bytes 49168
  700.3 62.4 %reduce-scatter.21.cloned.1.call-done = f32[64,192]{1,0:T(8,128)} async-done(((f32[512,192]{1,0:T(8,128)}), f32[64,192]{1,0:T(8,128)}) %reduce-scatter.21.cloned.1.call-update) | async-done | bytes 49168
  764.6 26.0 %all-gather = f32[8,64,3]{1,2,0:T(4,128)S(1)} all-gather(f32[1,64,3]{1,2,0:T(4,128)S(1)} %copy-done.58), channel_id=1, replica_groups=mesh['tok'=8,'head'=4] {'tok'}, dimensions={0}, use_global_device_ids=true | all-gather | bytes 6912 | tf_op jit(solution)/shard_map/all_gather | solution.py:359
  790.7 5.7 all-reduce.14.cloned.1.call-done
  799.1 30.9 %all_gather.22 = bf16[512,192]{1,0:T(8,128)(2,1)S(1)} all-gather(bf16[64,192]{1,0:T(8,128)(2,1)S(1)} %get-tuple-element.596), channel_id=1, replica_groups=mesh['tok'=8,'head'=4] {'tok'}, dimensions={0}, use_global_device_ids=true | all-gather | bytes 221184 | tf_op jit(solution)/shard_map/all_gather | solution.py:357
  830.2 26.2 %all-gather.1 = f32[8,64,3]{1,2,0:T(4,128)S(1)} all-gather(f32[1,64,3]{1,2,0:T(4,128)S(1)} %bitcast.410), channel_id=1, replica_groups=mesh['tok'=8,'head'=4] {'tok'}, dimensions={0}, use_global_device_ids=true | all-gather | bytes 6912 | tf_op jit(solution)/shard_map/all_gather | solution.py:358
  856.5 7.9 fusion.17
  868.2 11.0 fusion.45
  879.2 5.0 fusion.44
  884.2 44.4 %reduce-scatter.23.cloned.1.call-done = f32[64,192]{1,0:T(8,128)} async-done(((f32[512,192]{1,0:T(8,128)}), f32[64,192]{1,0:T(8,128)}) %reduce-scatter.23.cloned.1.call-update) | async-done | bytes 49168
  931.1 9.5 fusion.81
  944.3 3.8 add_add_fusion.1
  948.2 5.1 convert_element_type.140
  955.7 4.8 copy.224
  965.3 2.8 reshape.827
  968.2 7.8 convolution_convert_fusion.5
  976.0 7.1 convolution_convert_fusion.4
  984.8 5.0 copy.227
  991.4 4.0 convolution_convert_fusion.6
  1001.8 2.7 fusion.100
  1006.0 8.9 concatenate.65.parts_ref
  1014.9 69.4 %grad_scatter.1 = f32[96,3072]{1,0:T(8,128)} custom-call(bf16[4,2,96,3072]{3,2,1,0:T(8,128)(2,1)} %concatenate.65.parts_ref), custom_call_target="tpu_custom_call" | custom-call | tf_op jit(solution)/shard_map/grad_scatter/pallas_call | solution.py:117
  1092.5 2.9 add_convert_fusion
  1100.0 2.8 add_add_fusion.4
  (396 shorter events, 151.0 us)
Async XLA Ops:
  7.2 433.2 %copy-start = (bf16[768,768]{1,0:T(8,128)(2,1)S(1)}, bf16[768,768]{1,0:T(8,128)(2,1)}, u32[]{:S(2)}) copy-start(bf16[768,768]{1,0:T(8,128)(2,1)} %param.33) | copy-start | bytes 3538948
  7.2 185.4 %all-reduce.6.cloned.1.call-start = ((), (), s32[]{:S(2)}) async-start(), calls=%async_computation.6 | async-start | bytes 1048576 | tf_op jit(solution)/shard_map/psum | solution.py:219
  12.2 58.8 %copy-start.56 = (f32[64]{0:T(128)}, f32[64]{0:T(128)S(1)}, u32[]{:S(2)}) copy-start(f32[64]{0:T(128)S(1)} %broadcast_multiply_fusion.5) | copy-start | bytes 772
  13.3 57.7 %copy-start.62 = (f32[64]{0:T(128)}, f32[64]{0:T(128)S(1)}, u32[]{:S(2)}) copy-start(f32[64]{0:T(128)S(1)} %add_rsqrt_fusion.1) | copy-start | bytes 772
  20.2 88.2 %copy-start.32 = (bf16[2048,192]{0,1:T(8,128)(2,1)}, bf16[2048,192]{0,1:T(8,128)(2,1)S(1)}, u32[]{:S(2)}) copy-start(bf16[2048,192]{0,1:T(8,128)(2,1)S(1)} %convolution_convert_fusion.1) | copy-start | bytes 2359300
  21.1 43.7 %copy-start.65 = (pred[2048]{0:T(1024)(128)(4,1)S(1)}, pred[2048]{0:T(1024)(128)(4,1)}, u32[]{:S(2)}) copy-start(pred[2048]{0:T(1024)(128)(4,1)} %constant.410) | copy-start | bytes 6148
  21.1 43.7 %copy-start.66 = (pred[2048]{0:T(1024)(128)(4,1)S(1)}, pred[2048]{0:T(1024)(128)(4,1)}, u32[]{:S(2)}) copy-start(pred[2048]{0:T(1024)(128)(4,1)} %constant.411) | copy-start | bytes 6148
  21.1 43.6 %copy-start.67 = (pred[2048]{0:T(1024)(128)(4,1)S(1)}, pred[2048]{0:T(1024)(128)(4,1)}, u32[]{:S(2)}) copy-start(pred[2048]{0:T(1024)(128)(4,1)} %constant.412) | copy-start | bytes 6148
  21.1 43.6 %copy-start.68 = (pred[2048]{0:T(1024)(128)(4,1)S(1)}, pred[2048]{0:T(1024)(128)(4,1)}, u32[]{:S(2)}) copy-start(pred[2048]{0:T(1024)(128)(4,1)} %constant.413) | copy-start | bytes 6148
  21.1 43.6 %copy-start.69 = (pred[2048]{0:T(1024)(128)(4,1)S(1)}, pred[2048]{0:T(1024)(128)(4,1)}, u32[]{:S(2)}) copy-start(pred[2048]{0:T(1024)(128)(4,1)} %constant.414) | copy-start | bytes 6148
  21.1 43.6 %copy-start.70 = (pred[2048]{0:T(1024)(128)(4,1)S(1)}, pred[2048]{0:T(1024)(128)(4,1)}, u32[]{:S(2)}) copy-start(pred[2048]{0:T(1024)(128)(4,1)} %constant.415) | copy-start | bytes 6148
  21.1 43.6 %copy-start.71 = (pred[2048]{0:T(1024)(128)(4,1)S(1)}, pred[2048]{0:T(1024)(128)(4,1)}, u32[]{:S(2)}) copy-start(pred[2048]{0:T(1024)(128)(4,1)} %constant.416) | copy-start | bytes 6148
  71.1 41.9 %copy-start.30 = (pred[512,2112]{0,1:T(8,128)(4,1)}, pred[512,2112]{0,1:T(8,128)(4,1)S(1)}, u32[]{:S(2)}) copy-start(pred[512,2112]{0,1:T(8,128)(4,1)S(1)} %broadcast_compare_fusion.2) | copy-start | bytes 3244036
  113.0 80.5 %copy-start.25 = (bf16[192,768]{1,0:T(8,128)(2,1)S(1)}, bf16[192,768]{1,0:T(8,128)(2,1)}, u32[]{:S(2)}) copy-start(bf16[192,768]{1,0:T(8,128)(2,1)} %param.28) | copy-start | bytes 884740
  119.0 107.6 %all-reduce.8.cloned.1.call-start = ((), (), s32[]{:S(2)}) async-start(), calls=%async_computation.7 | async-start | bytes 393216 | tf_op jit(solution)/shard_map/psum | solution.py:224
  194.4 36.5 %copy-start.27 = (bf16[768,192]{0,1:T(8,128)(2,1)S(1)}, bf16[768,192]{0,1:T(8,128)(2,1)}, u32[]{:S(2)}) copy-start(bf16[768,192]{0,1:T(8,128)(2,1)} %param.30) | copy-start | bytes 884740
  194.4 240.7 %all-reduce.10.cloned.1.call-start = ((), (), s32[]{:S(2)}) async-start(), calls=%async_computation.8 | async-start | bytes 12582912 | tf_op jit(solution)/shard_map/psum | solution.py:268
  197.5 64.6 %copy-start.28 = (bf16[768,192]{0,1:T(8,128)(2,1)S(1)}, bf16[768,192]{0,1:T(8,128)(2,1)}, u32[]{:S(2)}) copy-start(bf16[768,192]{0,1:T(8,128)(2,1)} %param.31) | copy-start | bytes 884740
  230.8 63.1 %copy-start.17 = (bf16[64,768]{1,0:T(8,128)(2,1)}, bf16[64,768]{1,0:T(8,128)(2,1)S(1)}, u32[]{:S(2)}) copy-start(bf16[64,768]{1,0:T(8,128)(2,1)S(1)} %multiply_convert_fusion.3) | copy-start | bytes 294916
  315.5 263.1 %all-reduce.12.cloned.1.call-start = ((), (), s32[]{:S(2)}) async-start(), calls=%async_computation.10 | async-start | bytes 12582912 | tf_op jit(solution)/shard_map/psum | solution.py:284
  439.4 12.9 %copy-start.2 = (f32[2048,768]{1,0:T(8,128)}, f32[2048,768]{1,0:T(8,128)S(1)}, u32[]{:S(2)}) copy-start(f32[2048,768]{1,0:T(8,128)S(1)} %get-tuple-element.576) | copy-start | bytes 18874372
  439.5 144.8 %copy-start.47 = (f32[2048]{0:T(1024)}, f32[2048]{0:T(1024)S(1)}, u32[]{:S(2)}) copy-start(f32[2048]{0:T(1024)S(1)} %broadcast_multiply_fusion) | copy-start | bytes 24580
  444.5 139.8 %copy-start.53 = (f32[2048]{0:T(1024)}, f32[2048]{0:T(1024)S(1)}, u32[]{:S(2)}) copy-start(f32[2048]{0:T(1024)S(1)} %fusion.68) | copy-start | bytes 24580
  458.6 239.6 %reduce-scatter.19.cloned.1.call-start = ((), (), s32[]{:S(2)}) async-start(), calls=%async_computation.14 | async-start | bytes 589824
  634.8 128.8 %copy-start.29 = (bf16[768,192]{0,1:T(8,128)(2,1)S(1)}, bf16[768,192]{0,1:T(8,128)(2,1)}, u32[]{:S(2)}) copy-start(bf16[768,192]{0,1:T(8,128)(2,1)} %param.31) | copy-start | bytes 884740
  634.8 129.8 %copy-start.58 = (f32[1,64,3]{1,2,0:T(4,128)S(1)}, f32[1,64,3]{1,2,0:T(4,128)}, u32[]{:S(2)}) copy-start(f32[1,64,3]{1,2,0:T(4,128)} %get-tuple-element.569) | copy-start | bytes 2308
  634.8 161.6 %copy-start.13 = (f32[64,768]{1,0:T(8,128)S(1)}, f32[64,768]{1,0:T(8,128)}, u32[]{:S(2)}) copy-start(f32[64,768]{1,0:T(8,128)} %all-reduce.8.cloned.1.call-done) | copy-start | bytes 589828
  634.8 161.6 %copy-start.61 = (f32[64]{0:T(128)S(1)}, f32[64]{0:T(128)}, u32[]{:S(2)}) copy-start(f32[64]{0:T(128)} %copy-done.60) | copy-start | bytes 772
  634.8 162.7 %copy-start.75 = (f32[64]{0:T(128)S(1)}, f32[64]{0:T(128)}, u32[]{:S(2)}) copy-start(f32[64]{0:T(128)} %copy-done.74) | copy-start | bytes 772
  634.8 162.7 %copy-start.73 = (f32[64]{0:T(128)S(1)}, f32[64]{0:T(128)}, u32[]{:S(2)}) copy-start(f32[64]{0:T(128)} %copy-done.72) | copy-start | bytes 772
  634.8 164.0 %copy-start.26 = (bf16[192,768]{1,0:T(8,128)(2,1)S(1)}, bf16[192,768]{1,0:T(8,128)(2,1)}, u32[]{:S(2)}) copy-start(bf16[192,768]{1,0:T(8,128)(2,1)} %param.28) | copy-start | bytes 884740
  635.9 126.8 %reduce-scatter.21.cloned.1.call-start = ((), (), s32[]{:S(2)}) async-start(), calls=%async_computation.15 | async-start | bytes 589824
  635.9 220.6 %copy-start.31 = (pred[512,2112]{0,1:T(8,128)(4,1)S(1)}, pred[512,2112]{0,1:T(8,128)(4,1)}, u32[]{:S(2)}) copy-start(pred[512,2112]{0,1:T(8,128)(4,1)} %copy-done.30) | copy-start | bytes 3244036
  635.9 220.5 %copy-start.52 = (bf16[64,192]{0,1:T(8,128)(2,1)S(1)}, bf16[64,192]{0,1:T(8,128)(2,1)}, u32[]{:S(2)}) copy-start(bf16[64,192]{0,1:T(8,128)(2,1)} %copy.204) | copy-start | bytes 73732
  638.0 158.3 %all-reduce.14.cloned.1.call-start = ((), (), s32[]{:S(2)}) async-start(), calls=%async_computation.11 | async-start | bytes 393216 | tf_op jit(solution)/shard_map/psum | solution.py:346
  764.6 164.0 %reduce-scatter.23.cloned.1.call-start = ((), (), s32[]{:S(2)}) async-start(), calls=%async_computation.16 | async-start | bytes 589824
  830.1 26.4 %copy-start.44 = (bf16[512,192]{0,1:T(8,128)(2,1)}, bf16[512,192]{0,1:T(8,128)(2,1)S(1)}, u32[]{:S(2)}) copy-start(bf16[512,192]{0,1:T(8,128)(2,1)S(1)} %copy.216) | copy-start | bytes 589828
  868.1 11.0 copy-start.35
  868.1 221.7 %reduce-scatter.17.cloned.1.call-start = ((), (), s32[]{:S(2)}) async-start(), calls=%async_computation.13 | async-start | bytes 245760 | tf_op jit(solution)/shard_map/reduce_scatter | solution.py:432
  879.1 50.4 %copy-start.40 = (bf16[768,192]{0,1:T(8,128)(2,1)S(1)}, bf16[768,192]{0,1:T(8,128)(2,1)}, u32[]{:S(2)}) copy-start(bf16[768,192]{0,1:T(8,128)(2,1)} %param.25) | copy-start | bytes 884740
  879.2 50.6 %copy-start.23 = (bf16[768,192]{0,1:T(8,128)(2,1)S(1)}, bf16[768,192]{0,1:T(8,128)(2,1)}, u32[]{:S(2)}) copy-start(bf16[768,192]{0,1:T(8,128)(2,1)} %param.26) | copy-start | bytes 884740
  879.2 50.8 %copy-start.21 = (bf16[768,192]{0,1:T(8,128)(2,1)S(1)}, bf16[768,192]{0,1:T(8,128)(2,1)}, u32[]{:S(2)}) copy-start(bf16[768,192]{0,1:T(8,128)(2,1)} %param.27) | copy-start | bytes 884740
  929.5 11.2 %copy-start.38 = (bf16[64,192]{0,1:T(8,128)(2,1)}, bf16[64,192]{0,1:T(8,128)(2,1)S(1)}, u32[]{:S(2)}) copy-start(bf16[64,192]{0,1:T(8,128)(2,1)S(1)} %copy.241) | copy-start | bytes 73732
  930.9 161.6 %reduce-scatter.13.cloned.1.call-start = ((), (), s32[]{:S(2)}) async-start(), calls=%async_computation.9 | async-start | bytes 7864320 | tf_op jit(solution)/shard_map/reduce_scatter | solution.py:276
  940.7 154.7 %reduce-scatter.15.cloned.1.call-start = ((), (), s32[]{:S(2)}) async-start(), calls=%async_computation.12 | async-start | bytes 7864320 | tf_op jit(solution)/shard_map/reduce_scatter | solution.py:431
  948.1 12.4 %copy-start.36 = (f32[64,768]{1,0:T(8,128)}, f32[64,768]{1,0:T(8,128)S(1)}, u32[]{:S(2)}) copy-start(f32[64,768]{1,0:T(8,128)S(1)} %convert_element_type.144) | copy-start | bytes 589828
  1014.9 75.0 %copy-start.37 = (f32[64,768]{1,0:T(8,128)S(1)}, f32[64,768]{1,0:T(8,128)}, u32[]{:S(2)}) copy-start(f32[64,768]{1,0:T(8,128)} %copy-done.36) | copy-start | bytes 589828
  1014.9 75.0 %copy-start.64 = (f32[16]{0:T(128)S(1)}, f32[16]{0:T(128)}, u32[]{:S(2)}) copy-start(f32[16]{0:T(128)} %broadcast_multiply_fusion.3) | copy-start | bytes 196
  (44 other events, 173.1 us)
Sparse Core Ops, SparseCore 0:
  119.1 73.4 all-reduce.5
  195.6 30.9 all-reduce.7
  315.6 119.4 all-reduce.9
  458.7 119.7 all-reduce.11
  636.0 62.1 reduce-scatter.18
  701.8 60.8 reduce-scatter.20
  765.6 30.7 all-reduce.13
  868.2 60.3 reduce-scatter.22
  931.0 18.6 reduce-scatter.16
  952.1 58.3 reduce-scatter.12
  1013.2 58.3 reduce-scatter.14

commit v2 on v1

--- a/solution.py
+++ b/solution.py
@@ -125,6 +125,427 @@
         ),
         name="grad_scatter",
     )(parts.reshape(outer, 2, rows, width))
+
+
+SUB = 64
+SCALE = 0.125
+LOG2E = 1.4426950408889634
+MASKED = -1e30
+GELU_A = 0.7978845608028654
+GELU_B = 0.044715
+
+
+def nn(left, right):
+    return lax.dot_general(left, right, (((1,), (0,)), ((), ())), preferred_element_type=jnp.float32)
+
+
+def nt(left, right):
+    return lax.dot_general(left, right, (((1,), (1,)), ((), ())), preferred_element_type=jnp.float32)
+
+
+def tn(left, right):
+    return lax.dot_general(left, right, (((0,), (0,)), ((), ())), preferred_element_type=jnp.float32)
+
+
+def norm_parts(values):
+    center = values - jnp.mean(values, axis=-1, keepdims=True)
+    scale = lax.rsqrt(jnp.mean(center * center, axis=-1, keepdims=True) + epsilon)
+    return center * scale, scale
+
+
+def norm_vjp(normed, scale, grad):
+    return scale * (
+        grad
+        - jnp.mean(grad, axis=-1, keepdims=True)
+        - normed * jnp.mean(grad * normed, axis=-1, keepdims=True)
+    )
+
+
+def middle_kernel(
+    tokens,
+    cotangent,
+    query_t,
+    key,
+    value,
+    key_t,
+    value_t,
+    latent_image,
+    token_image,
+    write_out,
+    mlp_in,
+    mlp_out,
+    layer_out,
+    grad_one,
+    grad_query_t,
+    grad_key,
+    grad_value,
+    grad_mlp_in,
+    grad_mlp_out,
+    grad_write_out,
+    update,
+    mixed_t,
+    log_total,
+    own_a,
+    send_a,
+    got_a,
+    half_a,
+    cross_a,
+    own_d,
+    send_d,
+    got_d,
+    half_d,
+    cross_d,
+    summed_d,
+    own_f,
+    send_f,
+    got_f,
+    half_f,
+    cross_f,
+    acc_in,
+    acc_out,
+    acc_write,
+    normed_s,
+    act_s,
+    inner_s,
+    wide_s,
+    send_sems,
+    recv_sems,
+):
+    chunks = query_t.shape[0]
+    heads = key.shape[0]
+    latents = key.shape[1]
+    width = tokens.shape[2]
+    block = min(512, latents)
+    blocks = latents // block
+    tok = lax.axis_index("tok")
+    head = lax.axis_index("head")
+    core = lax.rem(head, 2)
+    side = head // 2
+    other = 1 - core
+    core_peer = (tok, side * 2 + other)
+    side_peer = (tok, (1 - side) * 2 + core)
+    barrier = pltpu.get_barrier_semaphore()
+    for peer in (core_peer, side_peer):
+        pl.semaphore_signal(barrier, inc=1, device_id=peer, device_id_type=MESH)
+    pl.semaphore_wait(barrier, 2)
+
+    def copy(kind, chunk, source, target, peer):
+        slot = lax.rem(chunk, 2)
+        return pltpu.make_async_remote_copy(
+            src_ref=source,
+            dst_ref=target,
+            send_sem=send_sems.at[kind, slot],
+            recv_sem=recv_sems.at[kind, slot],
+            device_id=peer,
+            device_id_type=MESH,
+        )
+
+    def core_a(c):
+        return copy(0, c, send_a, got_a.at[lax.rem(c, 2)], core_peer)
+
+    def cross_copy_a(c):
+        return copy(1, c, half_a, cross_a.at[lax.rem(c, 2)], side_peer)
+
+    def core_u(c):
+        return copy(2, c, update.at[c, core], update.at[c, core], core_peer)
+
+    def core_d(c):
+        return copy(3, c, send_d, got_d.at[lax.rem(c, 2)], core_peer)
+
+    def cross_copy_d(c):
+        return copy(4, c, half_d, cross_d.at[lax.rem(c, 2)], side_peer)
+
+    def core_s(c):
+        half = summed_d.at[lax.rem(c, 2), core]
+        return copy(5, c, half, half, core_peer)
+
+    def core_f(c):
+        return copy(6, c, send_f, got_f.at[lax.rem(c, 2)], core_peer)
+
+    def cross_copy_f(c):
+        return copy(7, c, half_f.at[1 - side], cross_f.at[lax.rem(c, 2)], side_peer)
+
+    def rows_of(ref, c):
+        part = pl.ds(pl.multiple_of(c * SUB, SUB), SUB)
+        return jnp.concatenate([ref[q, part, :] for q in (0, 2, 1, 3)], axis=0)
+
+    def mask_of(c, start):
+        image = latent_image[pl.ds(start, block), :]
+        image = jnp.concatenate([image, image], axis=1)
+        return jnp.where(image == token_image[c], 0.0, MASKED)
+
+    def each_block(body, carry):
+        if blocks == 1:
+            return body(0, carry)
+        return lax.fori_loop(0, blocks, lambda b, kept: body(b * block, kept), carry)
+
+    def halve(wide, own, send):
+        wide_s[...] = wide.reshape(wide_s.shape)
+        own[...] = wide_s[core]
+        send[...] = wide_s[other].astype(jnp.bfloat16)
+
+    acc_in[...] = jnp.zeros_like(acc_in)
+    acc_out[...] = jnp.zeros_like(acc_out)
+    acc_write[...] = jnp.zeros_like(acc_write)
+    grad_key[...] = jnp.zeros_like(grad_key)
+    grad_value[...] = jnp.zeros_like(grad_value)
+
+    def head_rows(h):
+        return slice(h * HD, (h + 1) * HD)
+
+    def write_forward(c):
+        query = query_t[c]
+
+        def body(start, carry):
+            here = pl.ds(start, block)
+            bias = mask_of(c, start)
+            kept = []
+            for h in range(heads):
+                scores = nn(key[h, here, :], query[head_rows(h)])
+                weights = jnp.exp2(scores * (SCALE * LOG2E) + bias)
+                total = jnp.sum(weights, axis=0, keepdims=True)
+                mixed = nn(value_t[head_rows(h), here], weights.astype(jnp.bfloat16))
+                kept.append((carry[h][0] + total, carry[h][1] + mixed))
+            return tuple(kept)
+
+        zero = (jnp.zeros((1, query.shape[1]), jnp.float32), jnp.zeros((HD, query.shape[1]), jnp.float32))
+        totals = each_block(body, (zero,) * heads)
+        mixed = jnp.concatenate([part / total for total, part in totals], axis=0)
+        mixed = mixed.astype(jnp.bfloat16)
+        mixed_t[c] = mixed
+        for h in range(heads):
+            log_total[c, h : h + 1] = -jnp.log2(totals[h][0])
+        halve(tn(mixed, write_out[...]), own_a, send_a)
+        core_a(c).start()
+
+    def finish_update(c):
+        cross_copy_a(c).wait()
+        mine = half_a[...].astype(jnp.float32) + cross_a[lax.rem(c, 2)].astype(jnp.float32)
+        update[c, core] = mine.astype(jnp.bfloat16)
+        core_u(c).start()
+
+    def cross_update(c):
+        core_a(c).wait()
+        half_a[...] = (own_a[...] + got_a[lax.rem(c, 2)].astype(jnp.float32)).astype(jnp.bfloat16)
+        cross_copy_a(c).start()
+
+    def one_rows(c):
+        moved = update[c].reshape(4 * SUB, width).astype(jnp.float32)
+        return rows_of(tokens, c).astype(jnp.float32) + moved
+
+    def feed_forward(c):
+        core_u(c).wait()
+        normed, unused = norm_parts(one_rows(c))
+        normed = normed.astype(jnp.bfloat16)
+        normed_s[...] = normed
+        inner = nn(normed, mlp_in[...])
+        square = inner * inner
+        tanh = jnp.tanh(GELU_A * inner * (1.0 + GELU_B * square))
+        half = 0.5 + 0.5 * tanh
+        active = (inner * half).astype(jnp.bfloat16)
+        act_s[...] = active
+        slope = half + 0.5 * GELU_A * inner * (1.0 - tanh * tanh) * (1.0 + 3.0 * GELU_B * square)
+        grad_inner = (nt(rows_of(cotangent, c), mlp_out[...]) * slope).astype(jnp.bfloat16)
+        inner_s[...] = grad_inner
+        halve(nt(grad_inner, mlp_in[...]), own_d, send_d)
+        core_d(c).start()
+        halve(nn(active, mlp_out[...]), own_f, send_f)
+        core_f(c).start()
+
+    def finish_grad(c):
+        slot = lax.rem(c, 2)
+        cross_copy_d(c).wait()
+        mine = half_d[...].astype(jnp.float32) + cross_d[slot].astype(jnp.float32)
+        summed_d[slot, core] = mine.astype(jnp.bfloat16)
+        core_s(c).start()
+        cross_copy_f(c).wait()
+        part = pl.ds(pl.multiple_of(c * SUB, SUB), SUB)
+        moved = update[c].reshape(2, 2, SUB, width)
+        mine = jnp.where(core == 0, moved[0], moved[1])
+        mine = jnp.where(side == 0, mine[0], mine[1]).astype(jnp.float32)
+        total = tokens[head, part, :].astype(jnp.float32) + mine + half_f[side].astype(jnp.float32)
+        layer_out[part, :] = (total + cross_f[slot].astype(jnp.float32)).astype(jnp.bfloat16)
+
+    def cross_grad(c):
+        slot = lax.rem(c, 2)
+        core_d(c).wait()
+        half_d[...] = (own_d[...] + got_d[slot].astype(jnp.float32)).astype(jnp.bfloat16)
+        cross_copy_d(c).start()
+        core_f(c).wait()
+        total = own_f[...] + got_f[slot].astype(jnp.float32)
+        half_f[...] = total.astype(jnp.bfloat16).reshape(half_f.shape)
+        cross_copy_f(c).start()
+
+    def weight_grads(c):
+        acc_in[...] += tn(normed_s[...], inner_s[...])
+        acc_out[...] += tn(rows_of(cotangent, c), act_s[...])
+
+    def write_backward(c):
+        core_s(c).wait()
+        normed, scale = norm_parts(one_rows(c))
+        grad = summed_d[lax.rem(c, 2)].reshape(4 * SUB, width).astype(jnp.float32)
+        wide = rows_of(cotangent, c).astype(jnp.float32) + norm_vjp(normed, scale, grad)
+        wide_s[...] = wide.reshape(wide_s.shape)
+        part = pl.ds(pl.multiple_of(c * SUB, SUB), SUB)
+        mine = pl.ds(pl.multiple_of(side * SUB, SUB), SUB)
+        grad_one[part, :] = wide_s[core, mine, :]
+        narrow = wide.astype(jnp.bfloat16)
+        mixed = mixed_t[c]
+        acc_write[...] += nn(mixed, narrow)
+        grad_mixed = nt(write_out[...], narrow).astype(jnp.bfloat16)
+        query = query_t[c]
+        product = grad_mixed.astype(jnp.float32) * mixed.astype(jnp.float32)
+
+        def body(start, carry):
+            here = pl.ds(start, block)
+            bias = mask_of(c, start)
+            kept = []
+            for h in range(heads):
+                rows = head_rows(h)
+                scores = nn(key[h, here, :], query[rows])
+                weights = jnp.exp2(scores * (SCALE * LOG2E) + (bias + log_total[c, h : h + 1]))
+                grad_weights = nn(value[h, here, :], grad_mixed[rows])
+                delta = jnp.sum(product[rows], axis=0, keepdims=True)
+                grad_scores = (weights * (grad_weights - delta)).astype(jnp.bfloat16)
+                grad_key[h, here, :] += nt(grad_scores, query[rows])
+                grad_value[h, here, :] += nt(weights.astype(jnp.bfloat16), grad_mixed[rows])
+                kept.append(carry[h] + nn(key_t[rows, here], grad_scores))
+            return tuple(kept)
+
+        zero = jnp.zeros((HD, query.shape[1]), jnp.float32)
+        grads = each_block(body, (zero,) * heads)
+        grad_query_t[c] = (jnp.concatenate(grads, axis=0) * SCALE).astype(jnp.bfloat16)
+
+    def step(i, carry):
+        @pl.when(i < chunks)
+        def _():
+            write_forward(i)
+
+        @pl.when(jnp.logical_and(i >= 1, i <= chunks))
+        def _():
+            finish_update(i - 1)
+
+        @pl.when(i < chunks)
+        def _():
+            cross_update(i)
+
+        @pl.when(jnp.logical_and(i >= 1, i <= chunks))
+        def _():
+            feed_forward(i - 1)
+
+        @pl.when(i >= 2)
+        def _():
+            finish_grad(i - 2)
+
+        @pl.when(jnp.logical_and(i >= 1, i <= chunks))
+        def _():
+            cross_grad(i - 1)
+            weight_grads(i - 1)
+
+        @pl.when(i >= 2)
+        def _():
+            write_backward(i - 2)
+
+        return carry
+
+    lax.fori_loop(0, chunks + 2, step, 0)
+    grad_key[...] = grad_key[...] * SCALE
+    grad_mlp_in[...] = acc_in[...].astype(jnp.bfloat16)
+    grad_mlp_out[...] = acc_out[...].astype(jnp.bfloat16)
+    grad_write_out[...] = acc_write[...].T.astype(jnp.bfloat16)
+
+
+def middle(tokens, cotangent, query_write, keys, values, latent_image, token_image, write_out, mlp_in, mlp_out):
+    rows, width = tokens.shape
+    column = write_out.shape[0]
+    hidden = mlp_in.shape[1]
+    heads = column // HD
+    latents = keys.shape[0]
+    quarter = rows // 4
+    chunks = quarter // SUB
+    size = 4 * SUB
+    by_chunk = query_write.reshape(2, 2, chunks, SUB, column).transpose(2, 4, 1, 0, 3)
+    query_t = by_chunk.reshape(chunks, column, size)
+    images = token_image.reshape(2, 2, chunks, SUB).transpose(2, 1, 0, 3).reshape(chunks, 1, size)
+    latent_wide = jnp.broadcast_to(latent_image[:, None], (latents, 128))
+    key_heads = keys.reshape(latents, heads, HD).transpose(1, 0, 2)
+    value_heads = values.reshape(latents, heads, HD).transpose(1, 0, 2)
+    half = (2 * SUB, width)
+    low, wide = jnp.bfloat16, jnp.float32
+    vmem = pl.BlockSpec(memory_space=pltpu.VMEM)
+    exchange = [
+        pltpu.VMEM(half, wide),
+        pltpu.VMEM(half, low),
+        pltpu.VMEM((2, *half), low),
+        pltpu.VMEM(half, low),
+        pltpu.VMEM((2, *half), low),
+    ]
+    outs = pl.pallas_call(
+        middle_kernel,
+        out_shape=[
+            jax.ShapeDtypeStruct((quarter, width), low),
+            jax.ShapeDtypeStruct((quarter, width), wide),
+            jax.ShapeDtypeStruct((chunks, column, size), low),
+            jax.ShapeDtypeStruct((heads, latents, HD), wide),
+            jax.ShapeDtypeStruct((heads, latents, HD), wide),
+            jax.ShapeDtypeStruct((width, hidden), low),
+            jax.ShapeDtypeStruct((width, hidden), low),
+            jax.ShapeDtypeStruct((width, column), low),
+        ],
+        in_specs=[vmem] * 12,
+        out_specs=[vmem] * 8,
+        scratch_shapes=[
+            pltpu.VMEM((chunks, 2, *half), low),
+            pltpu.VMEM((chunks, column, size), low),
+            pltpu.VMEM((chunks, 8, size), wide),
+            *exchange,
+            *exchange,
+            pltpu.VMEM((2, 2, *half), low),
+            pltpu.VMEM(half, wide),
+            pltpu.VMEM(half, low),
+            pltpu.VMEM((2, *half), low),
+            pltpu.VMEM((2, SUB, width), low),
+            pltpu.VMEM((2, SUB, width), low),
+            pltpu.VMEM((width, hidden), wide),
+            pltpu.VMEM((width, hidden), wide),
+            pltpu.VMEM((column, width), wide),
+            pltpu.VMEM((size, width), low),
+            pltpu.VMEM((size, hidden), low),
+            pltpu.VMEM((size, hidden), low),
+            pltpu.VMEM((2, *half), wide),
+            pltpu.SemaphoreType.DMA((8, 2)),
+            pltpu.SemaphoreType.DMA((8, 2)),
+        ],
+        compiler_params=pltpu.CompilerParams(
+            collective_id=1, has_side_effects=True, vmem_limit_bytes=62 << 20
+        ),
+        name="middle",
+    )(
+        tokens.reshape(4, quarter, width),
+        cotangent.reshape(4, quarter, width),
+        query_t,
+        key_heads,
+        value_heads,
+        keys.T,
+        values.T,
+        latent_wide,
+        images,
+        write_out,
+        mlp_in,
+        mlp_out,
+    )
+    out, grad_one, grad_query_t, grad_key, grad_value, grad_in, grad_out, grad_write = outs
+    grad_query = grad_query_t.reshape(chunks, column, 2, 2, SUB).transpose(3, 2, 0, 4, 1)
+    return (
+        out,
+        grad_one,
+        grad_query.reshape(rows, column),
+        grad_key.transpose(1, 0, 2).reshape(latents, column),
+        grad_value.transpose(1, 0, 2).reshape(latents, column),
+        grad_in,
+        grad_out,
+        grad_write,
+    )
 
 
 def heads_view(values):
@@ -230,110 +651,12 @@
         lax.all_gather(wkey_own, "tok", axis=0, tiled=True),
         lax.all_gather(wvalue_own, "tok", axis=0, tiled=True),
     )
-    wkey_split = heads_view(wkey_all)
-    wvalue_split = heads_view(wvalue_all)
     query_write = matmul(normed_x, write_query).astype(jnp.bfloat16)
-    row_block = min(512, rows)
-    row_blocks = rows // row_block
-
-    def write_scores(query_block, image_block):
-        scores = (
-            jnp.einsum(
-                "qhd,khd->qhk",
-                heads_view(query_block),
-                wkey_split,
-                preferred_element_type=jnp.float32,
-            )
-            * 0.125
-        )
-        mask = (image_block[:, None] == latent_image[None, :])[:, None, :]
-        return (scores, mask)
-
-    def write_block(operands):
-        query_block, image_block = operands
-        scores, mask = write_scores(query_block, image_block)
-        weights = jnp.where(mask, jnp.exp(scores), 0.0)
-        totals_block = jnp.sum(weights, axis=-1, keepdims=True)
-        probs = (weights / totals_block).astype(jnp.bfloat16)
-        mixed = jnp.einsum("qhk,khd->qhd", probs, wvalue_split, preferred_element_type=jnp.float32)
-        return (
-            mixed.reshape(query_block.shape[0], column).astype(jnp.bfloat16),
-            jnp.log(totals_block[:, :, 0]),
-        )
-
-    wquery_blocks = query_write.reshape(row_blocks, row_block, column)
-    token_blocks = token_image.reshape(row_blocks, row_block)
-    write_mixed, write_logs = lax.map(write_block, (wquery_blocks, token_blocks))
-    write_mixed = write_mixed.reshape(rows, column)
-    tokens_one = tokens_full + lax.psum(matmul(write_mixed, write_out), "head")
-    normed_two, norm_two_back = jax.vjp(norm_rows, tokens_one)
-    normed_two = normed_two.astype(jnp.bfloat16)
-    inner = matmul(normed_two, mlp_in)
-    activated, gelu_back = jax.vjp(jax.nn.gelu, inner)
-    activated = activated.astype(jnp.bfloat16)
+    layer_out, grad_one_own, grad_wquery, grad_wkey_all, grad_wvalue_all, grad_mlp_in, grad_mlp_out, grad_write_out = middle(
+        tokens, cotangent, query_write, wkey_all, wvalue_all, latent_image, token_image, write_out, mlp_in, mlp_out
+    )
     quarter = rows // head_count
     row_start = head_index * quarter
-    branch = lax.psum_scatter(matmul(activated, mlp_out), "head", scatter_dimension=0, tiled=True)
-    layer_out = (lax.dynamic_slice_in_dim(tokens_one, row_start, quarter) + branch).astype(
-        jnp.bfloat16
-    )
-    grad_mlp_out = left_trans(cotangent, activated)
-    grad_act = right_trans(cotangent, mlp_out)
-    grad_inner = gelu_back(grad_act)[0].astype(jnp.bfloat16)
-    grad_mlp_in = left_trans(normed_two, grad_inner)
-    grad_normed_two = lax.psum(right_trans(grad_inner, mlp_in), "head")
-    grad_tokens_one = cotangent.astype(jnp.float32) + norm_two_back(grad_normed_two)[0]
-    grad_branch = grad_tokens_one.astype(jnp.bfloat16)
-    grad_write_out = left_trans(grad_branch, write_mixed)
-    grad_wmixed = right_trans(grad_branch, write_out).astype(jnp.bfloat16)
-
-    def write_back(carry, operands):
-        key_total, value_total = carry
-        query_block, image_block, grad_block, log_block = operands
-        scores, mask = write_scores(query_block, image_block)
-        probs = jnp.where(mask, jnp.exp(scores - log_block[:, :, None]), 0.0)
-        grad_probs = jnp.einsum(
-            "qhd,khd->qhk", heads_view(grad_block), wvalue_split, preferred_element_type=jnp.float32
-        )
-        delta = jnp.sum(probs * grad_probs, axis=-1, keepdims=True)
-        grad_scores = (probs * (grad_probs - delta)).astype(jnp.bfloat16)
-        grad_query = (
-            jnp.einsum("qhk,khd->qhd", grad_scores, wkey_split, preferred_element_type=jnp.float32)
-            * 0.125
-        )
-        key_total = (
-            key_total
-            + jnp.einsum(
-                "qhk,qhd->khd",
-                grad_scores,
-                heads_view(query_block),
-                preferred_element_type=jnp.float32,
-            ).reshape(all_latents, column)
-            * 0.125
-        )
-        value_total = value_total + jnp.einsum(
-            "qhk,qhd->khd",
-            probs.astype(jnp.bfloat16),
-            heads_view(grad_block),
-            preferred_element_type=jnp.float32,
-        ).reshape(all_latents, column)
-        return (
-            (key_total, value_total),
-            grad_query.reshape(query_block.shape[0], column).astype(jnp.bfloat16),
-        )
-
-    latent_zeros = jnp.zeros((all_latents, column), jnp.float32)
-    (grad_wkey_all, grad_wvalue_all), grad_wquery = lax.scan(
-        write_back,
-        (latent_zeros, latent_zeros),
-        (
-            wquery_blocks,
-            token_blocks,
-            grad_wmixed.reshape(row_blocks, row_block, column),
-            write_logs,
-        ),
-    )
-    grad_wquery = grad_wquery.reshape(rows, column)
     grad_wkey, grad_wvalue = (
         lax.psum_scatter(grad_wkey_all, "tok", scatter_dimension=0, tiled=True),
         lax.psum_scatter(grad_wvalue_all, "tok", scatter_dimension=0, tiled=True),
@@ -436,7 +759,7 @@
     token_rows = lax.dynamic_slice_in_dim(tokens_full, row_start, quarter)
     unused_x, norm_x_back = jax.vjp(norm_rows, token_rows)
     input_grad = (
-        lax.dynamic_slice_in_dim(grad_tokens_one, row_start, quarter) + norm_x_back(grad_x_rows)[0]
+        grad_one_own + norm_x_back(grad_x_rows)[0]
     )
     latent_rows = lax.dynamic_slice_in_dim(latents_full, latent_start, latent_quarter)
     unused_lat, norm_lat_back = jax.vjp(norm_rows, latent_rows)
@@ -446,19 +769,19 @@
     )
     partials = jnp.concatenate(
         [
-            grad_read_query,
-            grad_read_key,
-            grad_read_value,
-            grad_read_out,
-            grad_write_query,
-            grad_write_key,
-            grad_write_value,
+            grad_read_query.astype(jnp.bfloat16),
+            grad_read_key.astype(jnp.bfloat16),
+            grad_read_value.astype(jnp.bfloat16),
+            grad_read_out.astype(jnp.bfloat16),
+            grad_write_query.astype(jnp.bfloat16),
+            grad_write_key.astype(jnp.bfloat16),
+            grad_write_value.astype(jnp.bfloat16),
             grad_write_out,
             grad_mlp_in,
             grad_mlp_out,
         ],
         axis=1,
-    ).astype(jnp.bfloat16)
+    )
     grads = scatter_grads(partials, tok_count)
     summed = [grads[:, k * column : (k + 1) * column] for k in range(8)]
     hidden = mlp_in.shape[1]

time: 1120 us -> 852 us (0.76)
  waiting for transfers between devices: 482 us -> 250 us
  Pallas kernels: 69.4 us -> 171 us
  matrix products: 147 us -> 74.9 us
  other arithmetic: 114 us -> 77.9 us
  local copies, waits for them, and re-layouts: 80 us -> 54.3 us
    psum x2 -> x0, waiting for transfers between devices: 231 us -> none  [the longest x1 119 us: shards(): grad_normed_two = lax.psum(right_trans(grad_inner, mlp_in), 'head')]
    pallas_call x0 -> x1, Pallas kernels: none -> 104 us  [middle(): pl.pallas_call(middle_kernel, out_shape=[jax.ShapeDtypeStruct((quarter, w...]
    dot_general x28 -> x0, matrix products: 28.5 us -> none  [the longest x8 8.44 us: write_scores(): jnp.einsum('qhd,khd->qhk', heads_view(query_block), wkey_split, preferred...]
    dot_general x12 -> x9, matrix products: 33.2 us -> 9.19 us  [matmul(): return jnp.dot(left, right, preferred_element_type=jnp.float32)]
    dot_general x12 -> x9, matrix products: 28.4 us -> 15.2 us  [left_trans(): lax.dot_general(left, right, (((0,), (0,)), ((), ())), preferred_element_...]
    dynamic_slice x20 -> x0, local copies, waits for them, and re-layouts: 11.4 us -> none  [shards(): lax.map(write_block, (wquery_blocks, token_blocks))]
    unnamed x14 -> x11, waiting for transfers between devices: 167 us -> 176 us
  transfers between devices with their start and end apart: 11 -> 8, of which waited for: 8 -> 6; matrix products, arithmetic and copies ran while one was open for 11% -> 10% of each run, Pallas kernels for 6% -> 8%
where the time goes in v2:
time: 852 us; the launch traced here: 845 us
  waiting for transfers between devices  250 us (29%)
  blocking collectives  200 us (23%)
  Pallas kernels  171 us (20%)
  other arithmetic  77.9 us (9%)
  matrix products  74.9 us (9%)
  local copies, waits for them, and re-layouts  54.3 us (6%)
  between operations  15.8 us (2%)
    unnamed x11, waiting for transfers between devices  176 us
    pallas_call x1, Pallas kernels, middle(): pl.pallas_call(middle_kernel, out_shape=[jax.ShapeDtypeStruct((quarter, w...  104 us
    pallas_call x1, Pallas kernels, scatter_grads(): pl.pallas_call(partial(grad_kernel, outer), out_shape=jax.ShapeDtypeStruc...  67.4 us
    psum x1, waiting for transfers between devices, shards(): totals_all, sums_all = lax.psum((totals, sums), 'tok')  43.6 us
    select_n x1, other arithmetic, shards(): latent_image = jnp.repeat(group_image, LPG, total_repeat_length=all_latents)  36 us
    all_gather x1, blocking collectives, shards(): query_all = lax.all_gather(query_own, 'tok', axis=0, tiled=True)  33.1 us
    all_gather x1, blocking collectives, shards(): lax.all_gather(grad_rmixed_wide, 'tok', axis=0, tiled=True)  31.1 us
    all_gather x1, blocking collectives, shards(): lax.all_gather(wkey_own, 'tok', axis=0, tiled=True)  30.9 us
  transfers between devices with their start and end apart: 8, of which 6 were waited for; matrix products, arithmetic and copies ran while one was open for 10% of the time, Pallas kernels for 8%

profile of v2, /device:TPU:0, one launch (start us, length us, event | category | flops | bytes accessed | tf_op | source)
XLA Modules:
  0.0 844.5 jit_solution(11361151511325279154)
XLA Ops:
  13.9 2.4 convert_reduce_fusion
  20.2 2.1 convolution_convert_fusion.1
  22.3 4.3 compare_select_fusion.2
  27.8 36.0 %select_select_fusion.1 = s32[512]{0:T(512)S(1)} fusion(pred[512]{0:T(512)(128)(4,1)S(1)} %get-tuple-element.264, pred[512]{0:T(512)(128)(4,1)S(1)} %get-tuple-element.263, pred[512]{0:T(512)(128)(4,1)S(1)} %get-tuple-element.262, pred[512]{0:T(512)(128)(4,1)S(1)} %get-tuple-element.261, pred[512]{0:T(512)(128)(4,1)S(1)} %get-tuple-element.260, ...), kind=kLoop, calls=%fused_computation.170 | loop fusion | flops 33792 | bytes 35572 | tf_op jit(solution)/shard_map/jit(_take)/select_n | solution.py:585
  63.9 5.0 select_select_fusion
  70.3 33.1 %all_gather.18 = bf16[512,192]{1,0:T(8,128)(2,1)S(1)} all-gather(bf16[64,192]{1,0:T(8,128)(2,1)S(1)} %convolution_convert_fusion.11), channel_id=1, replica_groups=mesh['tok'=8,'head'=4] {'tok'}, dimensions={0}, use_global_device_ids=true | all-gather | bytes 221184 | tf_op jit(solution)/shard_map/all_gather | solution.py:596
  104.3 3.5 fusion.5
  107.9 7.1 fusion.6
  115.0 2.0 copy.213
  117.8 21.8 %psum.29 = f32[512,3]{0,1:T(4,128)S(1)} all-reduce(f32[512,3]{0,1:T(4,128)S(1)} %get-tuple-element.365), channel_id=1, replica_groups=mesh['tok'=8,'head'=4] {'tok'}, use_global_device_ids=true, to_apply=%region_8.9 | all-reduce | flops 1536 | bytes 12288 | tf_op jit(solution)/shard_map/psum | solution.py:640
  140.9 1.6 copy.214
  143.9 3.0 convolution_convert_fusion.2
  146.9 43.6 %all-reduce.4.cloned.1.call-done = f32[512,192]{1,0:T(8,128)} async-done(((f32[512,192]{1,0:T(8,128)}), f32[512,192]{1,0:T(8,128)}) %all-reduce.4.cloned.1.call-update) | async-done | bytes 393232 | tf_op jit(solution)/shard_map/psum | solution.py:640
  191.4 1.8 fusion.40
  197.8 26.8 %all-reduce.6.cloned.1.call-done = f32[64,768]{1,0:T(8,128)} async-done(((f32[64,768]{1,0:T(8,128)}), f32[64,768]{1,0:T(8,128)}) %all-reduce.6.cloned.1.call-update) | async-done | bytes 196624 | tf_op jit(solution)/shard_map/psum | solution.py:645
  228.0 30.9 %all_gather.19 = bf16[512,192]{1,0:T(8,128)(2,1)S(1)} all-gather(bf16[64,192]{1,0:T(8,128)(2,1)S(1)} %convolution_convert_fusion.10), channel_id=1, replica_groups=mesh['tok'=8,'head'=4] {'tok'}, dimensions={0}, use_global_device_ids=true | all-gather | bytes 221184 | tf_op jit(solution)/shard_map/all_gather | solution.py:651
  260.3 30.9 %all_gather.20 = bf16[512,192]{1,0:T(8,128)(2,1)S(1)} all-gather(bf16[64,192]{1,0:T(8,128)(2,1)S(1)} %convolution_convert_fusion.9), channel_id=1, replica_groups=mesh['tok'=8,'head'=4] {'tok'}, dimensions={0}, use_global_device_ids=true | all-gather | bytes 221184 | tf_op jit(solution)/shard_map/all_gather | solution.py:652
  293.1 103.5 %middle.1 = (bf16[512,768]{1,0:T(8,128)(2,1)}, f32[512,768]{1,0:T(8,128)}, bf16[8,192,256]{2,1,0:T(8,128)(2,1)}, f32[3,512,64]{2,1,0:T(8,128)}, f32[3,512,64]{2,...) custom-call(bf16[4,512,768]{2,1,0:T(8,128)(2,1)} %bitcast.221, ...), custom_call_target="tpu_custom_call" | custom-call | tf_op jit(solution)/shard_map/middle/pallas_call | solution.py:483
  400.6 60.5 %reduce-scatter.16.cloned.1.call-done = f32[64,192]{1,0:T(8,128)} async-done(((f32[512,192]{1,0:T(8,128)}), f32[64,192]{1,0:T(8,128)}) %reduce-scatter.16.cloned.1.call-update) | async-done | bytes 49168
  462.2 63.4 %reduce-scatter.18.cloned.1.call-done = f32[64,192]{1,0:T(8,128)} async-done(((f32[512,192]{1,0:T(8,128)}), f32[64,192]{1,0:T(8,128)}) %reduce-scatter.18.cloned.1.call-update) | async-done | bytes 49168
  527.6 26.0 %all-gather = f32[8,64,3]{1,2,0:T(4,128)S(1)} all-gather(f32[1,64,3]{1,2,0:T(4,128)S(1)} %copy-done.55), channel_id=1, replica_groups=mesh['tok'=8,'head'=4] {'tok'}, dimensions={0}, use_global_device_ids=true | all-gather | bytes 6912 | tf_op jit(solution)/shard_map/all_gather | solution.py:682
  555.3 3.8 all-reduce.8.cloned.1.call-done
  561.8 31.1 %all_gather.22 = bf16[512,192]{1,0:T(8,128)(2,1)S(1)} all-gather(bf16[64,192]{1,0:T(8,128)(2,1)S(1)} %get-tuple-element.286), channel_id=1, replica_groups=mesh['tok'=8,'head'=4] {'tok'}, dimensions={0}, use_global_device_ids=true | all-gather | bytes 221184 | tf_op jit(solution)/shard_map/all_gather | solution.py:680
  593.0 9.4 %fusion.22 = bf16[2112,3,64]{0,2,1:T(8,128)(2,1)S(1)} fusion(bf16[512,3,64]{0,2,1:T(8,128)(2,1)S(1)} %bitcast.257, f32[3,2112,512]{2,1,0:T(8,128)} %copy-done.67, f32[512,3]{0,1:T(4,128)S(1)} %reshape.689, pred[512,2112]{0,1:T(8,128)(4,1)} %copy-done.26), kind=kOutput, calls=%fused_computation.26 | convolution fusion | flops 1255845888 | bytes 15071232 | tf_op jit(solution)/shard_map/while/body/eval_jaxpr/qhk,qhd->khd/dot_general | solution.py:709
  603.4 26.0 %all-gather.1 = f32[8,64,3]{1,2,0:T(4,128)S(1)} all-gather(f32[1,64,3]{1,2,0:T(4,128)S(1)} %bitcast.261), channel_id=1, replica_groups=mesh['tok'=8,'head'=4] {'tok'}, dimensions={0}, use_global_device_ids=true | all-gather | bytes 6912 | tf_op jit(solution)/shard_map/all_gather | solution.py:681
  629.5 7.9 fusion.1
  637.5 2.0 fusion.21
  642.6 4.7 fusion.65
  647.3 3.7 fusion.64
  651.0 52.0 %reduce-scatter.20.cloned.1.call-done = f32[64,192]{1,0:T(8,128)} async-done(((f32[512,192]{1,0:T(8,128)}), f32[64,192]{1,0:T(8,128)}) %reduce-scatter.20.cloned.1.call-update) | async-done | bytes 49168
  705.7 8.3 add_add_fusion
  715.9 3.1 convert_element_type.97
  720.0 1.6 dynamic-slice_reduce_fusion
  721.6 3.9 convolution_convert_fusion.3
  725.4 1.9 copy.235
  727.3 1.9 convolution_convert_fusion.5
  729.2 1.9 copy.236
  731.1 1.9 convolution_convert_fusion.4
  732.9 1.9 copy.237
  734.9 2.0 fusion.67
  737.9 1.9 copy.232
  739.8 2.0 fusion.66
  745.0 9.0 %concatenate.39 = bf16[768,3072]{1,0:T(8,128)(2,1)} concatenate(bf16[768,192]{1,0:T(8,128)(2,1)S(1)} %copy.233, bf16[768,192]{1,0:T(8,128)(2,1)S(1)} %copy.231, bf16[768,192]{1,0:T(8,128)(2,1)S(1)} %copy-done.19, bf16[768,192]{1,0:T(8,128)(2,1)S(1)} %copy.234, bf16[768,192]{1,0:T(8,128)(2,1)S(1)} %copy-done.16, bf16[768,192]{1,0:T(8,128)(2,1)S(1)} %copy-done.17, ...), dimensions={1} | concatenate | bytes 9437184 | tf_op jit(solution)/shard_map/concatenate | solution.py:770
  754.1 67.4 %grad_scatter.1 = f32[96,3072]{1,0:T(8,128)} custom-call(bf16[4,2,96,3072]{3,2,1,0:T(8,128)(2,1)} %bitcast.222), custom_call_target="tpu_custom_call" | custom-call | tf_op jit(solution)/shard_map/grad_scatter/pallas_call | solution.py:117
  821.5 2.2 slice_bitcast_fusion.1
  825.2 1.9 slice_bitcast_fusion
  830.6 2.4 multiply_reduce_fusion.2
  833.1 2.1 fusion.56
  (262 shorter events, 61.4 us)
Async XLA Ops:
  7.2 11.1 %copy-start = (bf16[768,192]{0,1:T(8,128)(2,1)S(1)}, bf16[768,192]{0,1:T(8,128)(2,1)}, u32[]{:S(2)}) copy-start(bf16[768,192]{0,1:T(8,128)(2,1)} %param.22) | copy-start | bytes 884740
  7.2 9.1 %copy-start.1 = (bf16[2048,768]{1,0:T(8,128)(2,1)S(1)}, bf16[2048,768]{1,0:T(8,128)(2,1)}, u32[]{:S(2)}) copy-start(bf16[2048,768]{1,0:T(8,128)(2,1)} %param.18) | copy-start | bytes 9437188
  7.2 183.3 %all-reduce.4.cloned.1.call-start = ((), (), s32[]{:S(2)}) async-start(), calls=%async_computation.5 | async-start | bytes 1048576 | tf_op jit(solution)/shard_map/psum | solution.py:640
  12.7 57.2 %copy-start.52 = (f32[64]{0:T(128)}, f32[64]{0:T(128)S(1)}, u32[]{:S(2)}) copy-start(f32[64]{0:T(128)S(1)} %broadcast_multiply_fusion.4) | copy-start | bytes 772
  13.9 56.1 %copy-start.56 = (f32[64]{0:T(128)}, f32[64]{0:T(128)S(1)}, u32[]{:S(2)}) copy-start(f32[64]{0:T(128)S(1)} %add_rsqrt_fusion.1) | copy-start | bytes 772
  19.7 84.6 %copy-start.28 = (bf16[2048,192]{0,1:T(8,128)(2,1)}, bf16[2048,192]{0,1:T(8,128)(2,1)S(1)}, u32[]{:S(2)}) copy-start(bf16[2048,192]{0,1:T(8,128)(2,1)S(1)} %convolution_convert_fusion) | copy-start | bytes 2359300
  20.1 43.8 %copy-start.59 = (pred[2048]{0:T(1024)(128)(4,1)S(1)}, pred[2048]{0:T(1024)(128)(4,1)}, u32[]{:S(2)}) copy-start(pred[2048]{0:T(1024)(128)(4,1)} %constant.350) | copy-start | bytes 6148
  20.1 43.8 %copy-start.60 = (pred[2048]{0:T(1024)(128)(4,1)S(1)}, pred[2048]{0:T(1024)(128)(4,1)}, u32[]{:S(2)}) copy-start(pred[2048]{0:T(1024)(128)(4,1)} %constant.351) | copy-start | bytes 6148
  20.1 43.8 %copy-start.61 = (pred[2048]{0:T(1024)(128)(4,1)S(1)}, pred[2048]{0:T(1024)(128)(4,1)}, u32[]{:S(2)}) copy-start(pred[2048]{0:T(1024)(128)(4,1)} %constant.352) | copy-start | bytes 6148
  20.1 43.8 %copy-start.62 = (pred[2048]{0:T(1024)(128)(4,1)S(1)}, pred[2048]{0:T(1024)(128)(4,1)}, u32[]{:S(2)}) copy-start(pred[2048]{0:T(1024)(128)(4,1)} %constant.353) | copy-start | bytes 6148
  20.1 43.8 %copy-start.63 = (pred[2048]{0:T(1024)(128)(4,1)S(1)}, pred[2048]{0:T(1024)(128)(4,1)}, u32[]{:S(2)}) copy-start(pred[2048]{0:T(1024)(128)(4,1)} %constant.354) | copy-start | bytes 6148
  20.1 43.8 %copy-start.64 = (pred[2048]{0:T(1024)(128)(4,1)S(1)}, pred[2048]{0:T(1024)(128)(4,1)}, u32[]{:S(2)}) copy-start(pred[2048]{0:T(1024)(128)(4,1)} %constant.355) | copy-start | bytes 6148
  20.1 43.8 %copy-start.65 = (pred[2048]{0:T(1024)(128)(4,1)S(1)}, pred[2048]{0:T(1024)(128)(4,1)}, u32[]{:S(2)}) copy-start(pred[2048]{0:T(1024)(128)(4,1)} %constant.356) | copy-start | bytes 6148
  20.1 49.9 %copy-start.42 = (bf16[768,192]{0,1:T(8,128)(2,1)S(1)}, bf16[768,192]{0,1:T(8,128)(2,1)}, u32[]{:S(2)}) copy-start(bf16[768,192]{0,1:T(8,128)(2,1)} %param.21) | copy-start | bytes 884740
  70.0 37.8 %copy-start.26 = (pred[512,2112]{0,1:T(8,128)(4,1)}, pred[512,2112]{0,1:T(8,128)(4,1)S(1)}, u32[]{:S(2)}) copy-start(pred[512,2112]{0,1:T(8,128)(4,1)S(1)} %broadcast_compare_fusion) | copy-start | bytes 3244036
  107.9 36.0 %copy-start.4 = (bf16[2048,768]{1,0:T(8,128)(2,1)S(1)}, bf16[2048,768]{1,0:T(8,128)(2,1)}, u32[]{:S(2)}) copy-start(bf16[2048,768]{1,0:T(8,128)(2,1)} %copy-done.3) | copy-start | bytes 9437188
  117.0 107.5 %all-reduce.6.cloned.1.call-start = ((), (), s32[]{:S(2)}) async-start(), calls=%async_computation.6 | async-start | bytes 393216 | tf_op jit(solution)/shard_map/psum | solution.py:645
  143.9 49.5 %copy-start.47 = (s32[2,2,8,64]{3,2,1,0:T(8,128)S(1)}, s32[2,2,8,64]{3,2,1,0:T(8,128)}, u32[]{:S(2)}) copy-start(s32[2,2,8,64]{3,2,1,0:T(8,128)} %gather.12) | copy-start | bytes 24580
  191.4 370.1 %copy-start.27 = (f32[64,192]{1,0:T(8,128)}, f32[64,192]{1,0:T(8,128)S(1)}, u32[]{:S(2)}) copy-start(f32[64,192]{1,0:T(8,128)S(1)} %dynamic-slice_divide_fusion) | copy-start | bytes 147460
  193.3 267.8 %reduce-scatter.16.cloned.1.call-start = ((), (), s32[]{:S(2)}) async-start(), calls=%async_computation.10 | async-start | bytes 589824
  194.9 32.9 %copy-start.24 = (bf16[768,192]{0,1:T(8,128)(2,1)S(1)}, bf16[768,192]{0,1:T(8,128)(2,1)}, u32[]{:S(2)}) copy-start(bf16[768,192]{0,1:T(8,128)(2,1)} %param.26) | copy-start | bytes 884740
  196.4 63.7 %copy-start.25 = (bf16[768,192]{0,1:T(8,128)(2,1)S(1)}, bf16[768,192]{0,1:T(8,128)(2,1)}, u32[]{:S(2)}) copy-start(bf16[768,192]{0,1:T(8,128)(2,1)} %param.27) | copy-start | bytes 884740
  196.5 95.8 %copy-start.51 = (s32[512]{0:T(512)S(1)}, s32[512]{0:T(512)}, u32[]{:S(2)}) copy-start(s32[512]{0:T(512)} %copy-done.50) | copy-start | bytes 6148
  227.8 32.2 %copy-start.12 = (bf16[64,768]{1,0:T(8,128)(2,1)}, bf16[64,768]{1,0:T(8,128)(2,1)S(1)}, u32[]{:S(2)}) copy-start(bf16[64,768]{1,0:T(8,128)(2,1)S(1)} %multiply_convert_fusion.1) | copy-start | bytes 294916
  259.1 34.0 %copy-start.14 = (bf16[512,192]{0,1:T(8,128)(2,1)}, bf16[512,192]{0,1:T(8,128)(2,1)S(1)}, u32[]{:S(2)}) copy-start(bf16[512,192]{0,1:T(8,128)(2,1)S(1)} %copy.215) | copy-start | bytes 589828
  398.1 129.5 %copy-start.55 = (f32[1,64,3]{1,2,0:T(4,128)S(1)}, f32[1,64,3]{1,2,0:T(4,128)}, u32[]{:S(2)}) copy-start(f32[1,64,3]{1,2,0:T(4,128)} %get-tuple-element.269) | copy-start | bytes 2308
  399.2 126.5 %reduce-scatter.18.cloned.1.call-start = ((), (), s32[]{:S(2)}) async-start(), calls=%async_computation.11 | async-start | bytes 589824
  400.5 158.6 %copy-start.10 = (f32[64,768]{1,0:T(8,128)S(1)}, f32[64,768]{1,0:T(8,128)}, u32[]{:S(2)}) copy-start(f32[64,768]{1,0:T(8,128)} %all-reduce.6.cloned.1.call-done) | copy-start | bytes 589828
  400.5 158.6 %all-reduce.8.cloned.1.call-start = ((), (), s32[]{:S(2)}) async-start(), calls=%async_computation.7 | async-start | bytes 393216 | tf_op jit(solution)/shard_map/psum | solution.py:669
  462.0 99.4 %copy-start.39 = (bf16[64,192]{0,1:T(8,128)(2,1)}, bf16[64,192]{0,1:T(8,128)(2,1)S(1)}, u32[]{:S(2)}) copy-start(bf16[64,192]{0,1:T(8,128)(2,1)S(1)} %copy.241) | copy-start | bytes 73732
  526.6 34.8 %copy-start.40 = (bf16[64,192]{0,1:T(8,128)(2,1)}, bf16[64,192]{0,1:T(8,128)(2,1)S(1)}, u32[]{:S(2)}) copy-start(bf16[64,192]{0,1:T(8,128)(2,1)S(1)} %copy.243) | copy-start | bytes 73732
  526.6 34.9 %copy-start.23 = (bf16[192,768]{1,0:T(8,128)(2,1)S(1)}, bf16[192,768]{1,0:T(8,128)(2,1)}, u32[]{:S(2)}) copy-start(bf16[192,768]{1,0:T(8,128)(2,1)} %param.24) | copy-start | bytes 884740
  527.6 175.5 %reduce-scatter.20.cloned.1.call-start = ((), (), s32[]{:S(2)}) async-start(), calls=%async_computation.12 | async-start | bytes 589824
  555.3 150.4 %copy-start.11 = (bf16[2,2,8,64,192]{4,3,2,1,0:T(8,128)(2,1)}, bf16[2,2,8,64,192]{4,3,2,1,0:T(8,128)(2,1)S(1)}, u32[]{:S(2)}) copy-start(bf16[2,2,8,64,192]{4,3,2,1,0:T(8,128)(2,1)S(1)} %copy.230) | copy-start | bytes 2359300
  561.5 41.0 %copy-start.13 = (f32[64,768]{1,0:T(8,128)}, f32[64,768]{1,0:T(8,128)S(1)}, u32[]{:S(2)}) copy-start(f32[64,768]{1,0:T(8,128)S(1)} %broadcast_add_fusion) | copy-start | bytes 589828
  593.0 36.5 %copy-start.49 = (bf16[64,192]{0,1:T(8,128)(2,1)S(1)}, bf16[64,192]{0,1:T(8,128)(2,1)}, u32[]{:S(2)}) copy-start(bf16[64,192]{0,1:T(8,128)(2,1)} %copy.210) | copy-start | bytes 73732
  602.6 40.0 %copy-start.7 = (bf16[2048,3,64]{0,2,1:T(8,128)(2,1)}, bf16[2048,3,64]{0,2,1:T(8,128)(2,1)S(1)}, u32[]{:S(2)}) copy-start(bf16[2048,3,64]{0,2,1:T(8,128)(2,1)S(1)} %slice.179) | copy-start | bytes 2359300
  629.5 7.9 copy-start.33
  642.5 184.5 %reduce-scatter.14.cloned.1.call-start = ((), (), s32[]{:S(2)}) async-start(), calls=%async_computation.9 | async-start | bytes 245760 | tf_op jit(solution)/shard_map/reduce_scatter | solution.py:755
  647.3 56.7 %copy-start.43 = (bf16[768,192]{0,1:T(8,128)(2,1)S(1)}, bf16[768,192]{0,1:T(8,128)(2,1)}, u32[]{:S(2)}) copy-start(bf16[768,192]{0,1:T(8,128)(2,1)} %param.21) | copy-start | bytes 884740
  647.3 56.9 %copy-start.37 = (bf16[64,3,64]{0,2,1:T(8,128)(2,1)S(1)}, bf16[64,3,64]{0,2,1:T(8,128)(2,1)}, u32[]{:S(2)}) copy-start(bf16[64,3,64]{0,2,1:T(8,128)(2,1)} %slice.180) | copy-start | bytes 73732
  647.3 57.2 %copy-start.22 = (bf16[768,192]{0,1:T(8,128)(2,1)S(1)}, bf16[768,192]{0,1:T(8,128)(2,1)}, u32[]{:S(2)}) copy-start(bf16[768,192]{0,1:T(8,128)(2,1)} %param.23) | copy-start | bytes 884740
  647.3 57.2 %copy-start.35 = (bf16[64,3,64]{0,2,1:T(8,128)(2,1)S(1)}, bf16[64,3,64]{0,2,1:T(8,128)(2,1)}, u32[]{:S(2)}) copy-start(bf16[64,3,64]{0,2,1:T(8,128)(2,1)} %slice.181) | copy-start | bytes 73732
  647.3 58.4 %copy-start.44 = (bf16[768,192]{0,1:T(8,128)(2,1)S(1)}, bf16[768,192]{0,1:T(8,128)(2,1)}, u32[]{:S(2)}) copy-start(bf16[768,192]{0,1:T(8,128)(2,1)} %param.25) | copy-start | bytes 884740
  704.0 10.0 %copy-start.41 = (bf16[64,192]{0,1:T(8,128)(2,1)}, bf16[64,192]{0,1:T(8,128)(2,1)S(1)}, u32[]{:S(2)}) copy-start(bf16[64,192]{0,1:T(8,128)(2,1)S(1)} %copy.245) | copy-start | bytes 73732
  705.4 125.2 %reduce-scatter.12.cloned.1.call-start = ((), (), s32[]{:S(2)}) async-start(), calls=%async_computation.8 | async-start | bytes 7864320 | tf_op jit(solution)/shard_map/reduce_scatter | solution.py:754
  721.6 13.3 %copy-start.5 = (bf16[2048,768]{1,0:T(8,128)(2,1)S(1)}, bf16[2048,768]{1,0:T(8,128)(2,1)}, u32[]{:S(2)}) copy-start(bf16[2048,768]{1,0:T(8,128)(2,1)} %copy-done.3) | copy-start | bytes 9437188
  754.1 73.0 %copy-start.34 = (f32[64,768]{1,0:T(8,128)S(1)}, f32[64,768]{1,0:T(8,128)}, u32[]{:S(2)}) copy-start(f32[64,768]{1,0:T(8,128)} %convert_element_type.100) | copy-start | bytes 589828
  (28 other events, 94.1 us)
Sparse Core Ops, SparseCore 0:
  117.2 73.3 all-reduce.3
  193.6 30.9 all-reduce.5
  399.3 61.7 reduce-scatter.15
  464.7 60.9 reduce-scatter.17
  528.4 30.6 all-reduce.7
  642.6 60.3 reduce-scatter.19
  705.5 18.6 reduce-scatter.13
  726.8 58.3 reduce-scatter.11

commit v3 on v2

v3 whole, which is shorter than its diff:
```python
from functools import partial

import jax
import jax.numpy as jnp
from jax import lax
from jax.experimental import pallas as pl
from jax.experimental.pallas import tpu as pltpu
from jax.sharding import PartitionSpec as P

MESH = pl.DeviceIdType.MESH
HD = 64
GROUP = 256
LPG = 8
epsilon = 1e-05
SUB = 64
SCALE = 0.125
LOG2E = 1.4426950408889634
MASKED = -1e30
GELU_A = 0.7978845608028654
GELU_B = 0.044715


def nn(left, right):
    return lax.dot_general(left, right, (((1,), (0,)), ((), ())), preferred_element_type=jnp.float32)


def nt(left, right):
    return lax.dot_general(left, right, (((1,), (1,)), ((), ())), preferred_element_type=jnp.float32)


def tn(left, right):
    return lax.dot_general(left, right, (((0,), (0,)), ((), ())), preferred_element_type=jnp.float32)


def norm_parts(values):
    center = values - jnp.mean(values, axis=-1, keepdims=True)
    scale = lax.rsqrt(jnp.mean(center * center, axis=-1, keepdims=True) + epsilon)
    return center * scale, scale


def norm_vjp(normed, scale, grad):
    return scale * (
        grad
        - jnp.mean(grad, axis=-1, keepdims=True)
        - normed * jnp.mean(grad * normed, axis=-1, keepdims=True)
    )


def image_of(counts, group):
    bound = jnp.int32(0)
    image = jnp.zeros_like(group)
    for m in range(counts.shape[0]):
        bound = bound + counts[m]
        image = image + jnp.where(bound <= group, 1, 0)
    return image


def latent_row_image(counts, start, count):
    group = lax.shift_right_logical(lax.broadcasted_iota(jnp.int32, (1, count), 1) + start, 3)
    return image_of(counts, group)


def head_rows(h):
    return slice(h * HD, (h + 1) * HD)


def chunk_rows(ref, c):
    part = pl.ds(pl.multiple_of(c * SUB, SUB), SUB)
    return jnp.concatenate([ref[q, part, :] for q in (0, 2, 1, 3)], axis=0)


def greet_all(tok, head, tok_count, head_count):
    barrier = pltpu.get_barrier_semaphore()

    def greet(step, carry):
        peer = lax.rem(tok + step, tok_count)
        pl.semaphore_signal(barrier, inc=1, device_id=(peer, head), device_id_type=MESH)
        return carry

    lax.fori_loop(1, tok_count, greet, 0)
    for step in range(1, head_count):
        peer = lax.rem(head + step, head_count)
        pl.semaphore_signal(barrier, inc=1, device_id=(tok, peer), device_id_type=MESH)
    pl.semaphore_wait(barrier, tok_count + head_count - 2)


class Spread:
    def __init__(self, axis, tok, head, count, source, got, sems):
        self.axis, self.tok, self.head, self.count = axis, tok, head, count
        self.me = tok if axis == "tok" else head
        self.source, self.got, self.sems = source, got, sems

    def copy(self, peer, slot):
        return pltpu.make_async_remote_copy(
            src_ref=self.source(peer),
            dst_ref=self.got.at[slot],
            send_sem=self.sems.at[0, peer],
            recv_sem=self.sems.at[1, slot],
            device_id=(peer, self.head) if self.axis == "tok" else (self.tok, peer),
            device_id_type=MESH,
        )

    def start(self):
        def go(step, carry):
            self.copy(lax.rem(self.me + step, self.count), self.me).start()
            return carry

        lax.fori_loop(1, self.count, go, 0)

    def wait(self):
        def go(step, carry):
            peer = lax.rem(self.me + step, self.count)
            self.copy(peer, peer).wait()
            return carry

        lax.fori_loop(1, self.count, go, 0)


class Scatter:
    def __init__(self, tok, head, parts, got_one, sums, got_two, sems):
        self.head, self.mine, self.side = head, tok // 2, lax.rem(tok, 2)
        self.parts, self.got_one, self.sums, self.got_two, self.sems = parts, got_one, sums, got_two, sems
        self.outer = parts.shape[0]

    def first(self, block):
        return pltpu.make_async_remote_copy(
            src_ref=self.parts.at[block, 1 - self.side],
            dst_ref=self.got_one.at[block],
            send_sem=self.sems.at[0, block],
            recv_sem=self.sems.at[1, block],
            device_id=(self.mine * 2 + (1 - self.side), self.head),
            device_id_type=MESH,
        )

    def second(self, block, source):
        return pltpu.make_async_remote_copy(
            src_ref=self.sums.at[block],
            dst_ref=self.got_two.at[source],
            send_sem=self.sems.at[2, block],
            recv_sem=self.sems.at[3, source],
            device_id=(block * 2 + self.side, self.head),
            device_id_type=MESH,
        )

    def start(self):
        def go(step, carry):
            self.first(lax.rem(self.mine + step, self.outer)).start()
            return carry

        lax.fori_loop(1, self.outer + 1, go, 0)

    def forward(self, step):
        block = lax.rem(self.mine + step, self.outer)
        self.first(block).wait()
        total = self.parts[block, self.side].astype(jnp.float32) + self.got_one[block].astype(jnp.float32)
        self.sums[block] = total.astype(jnp.bfloat16)
        self.second(block, self.mine).start()

    def forward_all(self):
        def go(step, carry):
            self.forward(step)
            return carry

        lax.fori_loop(1, self.outer, go, 0)

    def finish(self):
        self.first(self.mine).wait()
        total = self.parts[self.mine, self.side].astype(jnp.float32) + self.got_one[self.mine].astype(jnp.float32)

        def go(step, total):
            peer = lax.rem(self.mine + step, self.outer)
            self.second(peer, peer).wait()
            return total + self.got_two[peer].astype(jnp.float32)

        return lax.fori_loop(1, self.outer, go, total)


def scatter_scratch(outer, rows, width):
    slots = pltpu.VMEM((outer, rows, width), jnp.bfloat16)
    return [slots, slots, slots, pltpu.SemaphoreType.DMA((4, outer))]


def split_three(value):
    high = value.astype(jnp.bfloat16).astype(jnp.float32)
    rest = value - high
    middle_part = rest.astype(jnp.bfloat16).astype(jnp.float32)
    return high, middle_part, rest - middle_part


def pick_lanes(shape, columns):
    lane = lax.broadcasted_iota(jnp.int32, shape, 1)
    value = jnp.zeros(shape, jnp.float32)
    for at, column in columns:
        value = jnp.where(lane == at, column, value)
    return value


def by_head(shape, columns):
    lane = lax.broadcasted_iota(jnp.int32, shape, 1)
    value = jnp.broadcast_to(columns[-1], shape)
    for h in range(len(columns) - 2, -1, -1):
        value = jnp.where(lane < (h + 1) * HD, columns[h], value)
    return value


def chunk_bias(counts, tok, groups_here, c, quarter, row_image, rows):
    kept = []
    for q in (0, 2, 1, 3):
        group = tok * groups_here + (q * quarter + c * SUB) // GROUP
        image = image_of(counts, group)
        kept.append([jnp.where(row_image == image, row, MASKED) for row in rows])
    return kept


def add_rows(values, rows):
    count = values.shape[0] // len(rows)
    return jnp.concatenate([values[k * count : (k + 1) * count] + row for k, row in enumerate(rows)], axis=0)


def front_kernel(
    counts, tokens, latents, rquery, rkey, rvalue, rout, wquery, wkey, wvalue,
    query_t, key, value, key_t, value_t, read_key, read_value, read_key_t, own_key, own_value, own_key_t,
    read_query_t, lat_one, mixed_out,
    normed_s, query_all, value_t_s, own_value_t, sums, sums_send, sums_got, head_parts, pair_all,
    query_sems, sums_sems, head_sems, pair_sems,
):
    tok_count, owned = query_all.shape[0], query_all.shape[1]
    head_count = head_parts.shape[0]
    chunks, column = query_t.shape[0], query_t.shape[1]
    heads = column // HD
    quarter = tokens.shape[1]
    groups_here = 4 * quarter // GROUP
    latent_count = tok_count * owned
    block = min(512, latent_count)
    blocks, per = latent_count // block, block // owned
    tok, head = lax.axis_index("tok"), lax.axis_index("head")
    low = jnp.bfloat16
    latents_wide = latents[...].astype(jnp.float32)
    normed_lat = norm_parts(latents_wide)[0].astype(low)
    query_all[tok] = nn(normed_lat, rquery[...]).astype(low)
    greet_all(tok, head, tok_count, head_count)
    queries = Spread("tok", tok, head, tok_count, lambda peer: query_all.at[tok], query_all, query_sems)
    queries.start()

    def keep_heads(ref, wide):
        for h in range(heads):
            ref[h] = wide[:, head_rows(h)]

    keys = nn(normed_lat, rkey[...]).astype(low)
    values = nn(normed_lat, rvalue[...]).astype(low)
    keep_heads(own_key, keys)
    keep_heads(own_value, values)
    own_key_t[...] = keys.T
    own_value_t[...] = values.T

    def project(c, carry):
        normed = norm_parts(chunk_rows(tokens, c).astype(jnp.float32))[0].astype(low)
        normed_s[c] = normed
        keys = nn(normed, rkey[...]).astype(low)
        values = nn(normed, rvalue[...]).astype(low)
        keep_heads(read_key.at[c], keys)
        keep_heads(read_value.at[c], values)
        read_key_t[c] = keys.T
        value_t_s[c] = values.T
        return carry

    lax.fori_loop(0, chunks, project, 0)
    sums[...] = jnp.zeros_like(sums)
    queries.wait()

    def attend(scores, rows, values_t, here, h):
        weights = jnp.exp2(add_rows(scores * (SCALE * LOG2E), rows))
        sums[column + h : column + h + 1, here] += jnp.sum(weights, axis=0, keepdims=True)
        sums[head_rows(h), here] += nn(values_t, weights.astype(low))

    def read_block(b, carry):
        start = pl.multiple_of(b * block, block)
        here = pl.ds(start, block)
        query = query_all[pl.ds(b * per, per)].reshape(block, column).T
        read_query_t[:, here] = query
        row_image = latent_row_image(counts, start, block)
        zero = jnp.zeros((1, block), jnp.float32)

        def read_chunk(c, carry):
            rows = chunk_bias(counts, tok, groups_here, c, quarter, row_image, [zero])
            rows = [row[0] for row in rows]
            for h in range(heads):
                scores = nn(read_key[c, h], query[head_rows(h)])
                attend(scores, rows, value_t_s[c, head_rows(h)], here, h)
            return carry

        lax.fori_loop(0, chunks, read_chunk, 0)
        rows = [
            jnp.where(row_image == image_of(counts, tok * groups_here + g), zero, MASKED)
            for g in range(owned // LPG)
        ]
        for h in range(heads):
            scores = nn(own_key[h], query[head_rows(h)])
            attend(scores, rows, own_value_t[head_rows(h), :], here, h)
        total = sums[column : column + heads, here]
        high = total.astype(low).astype(jnp.float32)
        sums[column : column + heads, here] = high
        sums[column + heads : column + 2 * heads, here] = total - high
        sums_send[pl.ds(b * per, per)] = sums[:, here].T.astype(low).reshape(per, owned, sums.shape[0])
        return carry

    lax.fori_loop(0, blocks, read_block, 0)
    totals = Spread("tok", tok, head, tok_count, lambda peer: sums_send.at[peer], sums_got, sums_sems)
    totals.start()

    def project_query(c, carry):
        query_t[c] = nn(normed_s[c], wquery[...]).astype(low).T
        return carry

    lax.fori_loop(0, chunks, project_query, 0)
    totals.wait()
    sums_got[tok] = sums_send[tok]
    summed = lax.fori_loop(
        1, tok_count, lambda s, kept: kept + sums_got[s].astype(jnp.float32), sums_got[0].astype(jnp.float32)
    )
    whole = [
        summed[:, column + h : column + h + 1] + summed[:, column + heads + h : column + heads + h + 1]
        for h in range(heads)
    ]
    mixed = summed[:, :column] / by_head((owned, column), whole)
    mixed_out[:, :column] = mixed
    mixed_out[:, column:] = pick_lanes(
        (owned, mixed_out.shape[1] - column), [(h, -jnp.log2(whole[h])) for h in range(heads)]
    )
    head_parts[head] = nn(mixed.astype(low), rout[...]).astype(low)
    moved = Spread("head", tok, head, head_count, lambda peer: head_parts.at[head], head_parts, head_sems)
    moved.start()
    moved.wait()
    latents_one = latents_wide
    for s in range(head_count):
        latents_one = latents_one + head_parts[s].astype(jnp.float32)
    lat_one[...] = latents_one
    normed_one = norm_parts(latents_one)[0].astype(low)
    pair_all[tok, 0] = nn(normed_one, wkey[...]).astype(low)
    pair_all[tok, 1] = nn(normed_one, wvalue[...]).astype(low)
    pairs = Spread("tok", tok, head, tok_count, lambda peer: pair_all.at[tok], pair_all, pair_sems)
    pairs.start()
    pairs.wait()

    def unpack(b, carry):
        start = pl.multiple_of(b * block, block)
        here = pl.ds(start, block)
        for k, (straight, turned) in enumerate(((key, key_t), (value, value_t))):
            wide = pair_all[pl.ds(b * per, per), k].reshape(block, column)
            for h in range(heads):
                straight[h, here, :] = wide[:, head_rows(h)]
            turned[:, here] = wide.T
        return carry

    lax.fori_loop(0, blocks, unpack, 0)


def front(counts, tokens, latents, rquery, rkey, rvalue, rout, wquery, wkey, wvalue, tok_count, head_count):
    rows, width = tokens.shape
    owned, column = latents.shape[0], rquery.shape[1]
    heads = column // HD
    quarter = rows // 4
    chunks, size = quarter // SUB, 4 * SUB
    latent_count = owned * tok_count
    low, wide = jnp.bfloat16, jnp.float32
    vmem = pl.BlockSpec(memory_space=pltpu.VMEM)
    packed = 256
    return pl.pallas_call(
        front_kernel,
        out_shape=[
            jax.ShapeDtypeStruct((chunks, column, size), low),
            jax.ShapeDtypeStruct((heads, latent_count, HD), low),
            jax.ShapeDtypeStruct((heads, latent_count, HD), low),
            jax.ShapeDtypeStruct((column, latent_count), low),
            jax.ShapeDtypeStruct((column, latent_count), low),
            jax.ShapeDtypeStruct((chunks, heads, size, HD), low),
            jax.ShapeDtypeStruct((chunks, heads, size, HD), low),
            jax.ShapeDtypeStruct((chunks, column, size), low),
            jax.ShapeDtypeStruct((heads, owned, HD), low),
            jax.ShapeDtypeStruct((heads, owned, HD), low),
            jax.ShapeDtypeStruct((column, owned), low),
            jax.ShapeDtypeStruct((column, latent_count), low),
            jax.ShapeDtypeStruct((owned, width), wide),
            jax.ShapeDtypeStruct((owned, packed), wide),
        ],
        in_specs=[pl.BlockSpec(memory_space=pltpu.SMEM)] + [vmem] * 9,
        out_specs=[vmem] * 14,
        scratch_shapes=[
            pltpu.VMEM((chunks, size, width), low),
            pltpu.VMEM((tok_count, owned, column), low),
            pltpu.VMEM((chunks, column, size), low),
            pltpu.VMEM((column, owned), low),
            pltpu.VMEM((packed, latent_count), wide),
            pltpu.VMEM((tok_count, owned, packed), low),
            pltpu.VMEM((tok_count, owned, packed), low),
            pltpu.VMEM((head_count, owned, width), low),
            pltpu.VMEM((tok_count, 2, owned, column), low),
            pltpu.SemaphoreType.DMA((2, tok_count)),
            pltpu.SemaphoreType.DMA((2, tok_count)),
            pltpu.SemaphoreType.DMA((2, head_count)),
            pltpu.SemaphoreType.DMA((2, tok_count)),
        ],
        compiler_params=pltpu.CompilerParams(collective_id=2, has_side_effects=True, vmem_limit_bytes=62 << 20),
        name="front",
    )(counts, tokens.reshape(4, quarter, width), latents, rquery, rkey, rvalue, rout, wquery, wkey, wvalue)


def middle_kernel(
    counts,
    tokens,
    cotangent,
    query_t,
    key,
    value,
    key_t,
    value_t,
    write_out,
    mlp_in,
    mlp_out,
    layer_out,
    grad_one,
    grad_query_t,
    grad_pairs,
    grad_mlp_in,
    grad_mlp_out,
    grad_write_out,
    update,
    mixed_t,
    log_total,
    own_a,
    send_a,
    got_a,
    half_a,
    cross_a,
    own_d,
    send_d,
    got_d,
    half_d,
    cross_d,
    summed_d,
    own_f,
    send_f,
    got_f,
    half_f,
    cross_f,
    acc_in,
    acc_out,
    acc_write,
    normed_s,
    act_s,
    inner_s,
    wide_s,
    latent_image,
    grad_key,
    grad_value,
    send_sems,
    recv_sems,
):
    chunks = query_t.shape[0]
    heads = key.shape[0]
    latents = key.shape[1]
    width = tokens.shape[2]
    block = min(512, latents)
    blocks = latents // block
    tok = lax.axis_index("tok")
    head = lax.axis_index("head")
    core = lax.rem(head, 2)
    side = head // 2
    other = 1 - core
    core_peer = (tok, side * 2 + other)
    side_peer = (tok, (1 - side) * 2 + core)
    barrier = pltpu.get_barrier_semaphore()
    for peer in (core_peer, side_peer):
        pl.semaphore_signal(barrier, inc=1, device_id=peer, device_id_type=MESH)
    pl.semaphore_wait(barrier, 2)

    def copy(kind, chunk, source, target, peer):
        slot = lax.rem(chunk, 2)
        return pltpu.make_async_remote_copy(
            src_ref=source,
            dst_ref=target,
            send_sem=send_sems.at[kind, slot],
            recv_sem=recv_sems.at[kind, slot],
            device_id=peer,
            device_id_type=MESH,
        )

    def core_a(c):
        return copy(0, c, send_a, got_a.at[lax.rem(c, 2)], core_peer)

    def cross_copy_a(c):
        return copy(1, c, half_a, cross_a.at[lax.rem(c, 2)], side_peer)

    def core_u(c):
        return copy(2, c, update.at[c, core], update.at[c, core], core_peer)

    def core_d(c):
        return copy(3, c, send_d, got_d.at[lax.rem(c, 2)], core_peer)

    def cross_copy_d(c):
        return copy(4, c, half_d, cross_d.at[lax.rem(c, 2)], side_peer)

    def core_s(c):
        half = summed_d.at[lax.rem(c, 2), core]
        return copy(5, c, half, half, core_peer)

    def core_f(c):
        return copy(6, c, send_f, got_f.at[lax.rem(c, 2)], core_peer)

    def cross_copy_f(c):
        return copy(7, c, half_f.at[1 - side], cross_f.at[lax.rem(c, 2)], side_peer)

    group = lax.shift_right_logical(lax.broadcasted_iota(jnp.int32, latent_image.shape, 0), 3)
    latent_image[...] = image_of(counts, group)
    quarter = tokens.shape[1]

    def mask_of(c, start):
        image = latent_image[pl.ds(start, block), :]
        image = jnp.concatenate([image, image], axis=1)
        lane = lax.broadcasted_iota(jnp.int32, (1, 4 * SUB), 1)
        part = lax.shift_right_logical(lane, 6)
        part = 2 * lax.rem(part, 2) + part // 2
        row = part * quarter + c * SUB
        group = tok * (4 * quarter // GROUP) + lax.shift_right_logical(row, 8)
        return jnp.where(image == image_of(counts, group), 0.0, MASKED)

    def each_block(body, carry):
        if blocks == 1:
            return body(0, carry)
        return lax.fori_loop(0, blocks, lambda b, kept: body(b * block, kept), carry)

    def halve(wide, own, send):
        wide_s[...] = wide.reshape(wide_s.shape)
        own[...] = wide_s[core]
        send[...] = wide_s[other].astype(jnp.bfloat16)

    acc_in[...] = jnp.zeros_like(acc_in)
    acc_out[...] = jnp.zeros_like(acc_out)
    acc_write[...] = jnp.zeros_like(acc_write)
    grad_key[...] = jnp.zeros_like(grad_key)
    grad_value[...] = jnp.zeros_like(grad_value)

    def write_forward(c):
        query = query_t[c]

        def body(start, carry):
            here = pl.ds(start, block)
            bias = mask_of(c, start)
            kept = []
            for h in range(heads):
                scores = nn(key[h, here, :], query[head_rows(h)])
                weights = jnp.exp2(scores * (SCALE * LOG2E) + bias)
                total = jnp.sum(weights, axis=0, keepdims=True)
                mixed = nn(value_t[head_rows(h), here], weights.astype(jnp.bfloat16))
                kept.append((carry[h][0] + total, carry[h][1] + mixed))
            return tuple(kept)

        zero = (jnp.zeros((1, query.shape[1]), jnp.float32), jnp.zeros((HD, query.shape[1]), jnp.float32))
        totals = each_block(body, (zero,) * heads)
        mixed = jnp.concatenate([part / total for total, part in totals], axis=0)
        mixed = mixed.astype(jnp.bfloat16)
        mixed_t[c] = mixed
        for h in range(heads):
            log_total[c, h : h + 1] = -jnp.log2(totals[h][0])
        halve(tn(mixed, write_out[...]), own_a, send_a)
        core_a(c).start()

    def finish_update(c):
        cross_copy_a(c).wait()
        mine = half_a[...].astype(jnp.float32) + cross_a[lax.rem(c, 2)].astype(jnp.float32)
        update[c, core] = mine.astype(jnp.bfloat16)
        core_u(c).start()

    def cross_update(c):
        core_a(c).wait()
        half_a[...] = (own_a[...] + got_a[lax.rem(c, 2)].astype(jnp.float32)).astype(jnp.bfloat16)
        cross_copy_a(c).start()

    def one_rows(c):
        moved = update[c].reshape(4 * SUB, width).astype(jnp.float32)
        return chunk_rows(tokens, c).astype(jnp.float32) + moved

    def feed_forward(c):
        core_u(c).wait()
        normed, unused = norm_parts(one_rows(c))
        normed = normed.astype(jnp.bfloat16)
        normed_s[...] = normed
        inner = nn(normed, mlp_in[...])
        square = inner * inner
        tanh = jnp.tanh(GELU_A * inner * (1.0 + GELU_B * square))
        half = 0.5 + 0.5 * tanh
        active = (inner * half).astype(jnp.bfloat16)
        act_s[...] = active
        slope = half + 0.5 * GELU_A * inner * (1.0 - tanh * tanh) * (1.0 + 3.0 * GELU_B * square)
        grad_inner = (nt(chunk_rows(cotangent, c), mlp_out[...]) * slope).astype(jnp.bfloat16)
        inner_s[...] = grad_inner
        halve(nt(grad_inner, mlp_in[...]), own_d, send_d)
        core_d(c).start()
        halve(nn(active, mlp_out[...]), own_f, send_f)
        core_f(c).start()

    def finish_grad(c):
        slot = lax.rem(c, 2)
        cross_copy_d(c).wait()
        mine = half_d[...].astype(jnp.float32) + cross_d[slot].astype(jnp.float32)
        summed_d[slot, core] = mine.astype(jnp.bfloat16)
        core_s(c).start()
        cross_copy_f(c).wait()
        part = pl.ds(pl.multiple_of(c * SUB, SUB), SUB)
        moved = update[c].reshape(2, 2, SUB, width)
        mine = jnp.where(core == 0, moved[0], moved[1])
        mine = jnp.where(side == 0, mine[0], mine[1]).astype(jnp.float32)
        total = tokens[head, part, :].astype(jnp.float32) + mine + half_f[side].astype(jnp.float32)
        layer_out[part, :] = (total + cross_f[slot].astype(jnp.float32)).astype(jnp.bfloat16)

    def cross_grad(c):
        slot = lax.rem(c, 2)
        core_d(c).wait()
        half_d[...] = (own_d[...] + got_d[slot].astype(jnp.float32)).astype(jnp.bfloat16)
        cross_copy_d(c).start()
        core_f(c).wait()
        total = own_f[...] + got_f[slot].astype(jnp.float32)
        half_f[...] = total.astype(jnp.bfloat16).reshape(half_f.shape)
        cross_copy_f(c).start()

    def weight_grads(c):
        acc_in[...] += tn(normed_s[...], inner_s[...])
        acc_out[...] += tn(chunk_rows(cotangent, c), act_s[...])

    def write_backward(c):
        core_s(c).wait()
        normed, scale = norm_parts(one_rows(c))
        grad = summed_d[lax.rem(c, 2)].reshape(4 * SUB, width).astype(jnp.float32)
        wide = chunk_rows(cotangent, c).astype(jnp.float32) + norm_vjp(normed, scale, grad)
        wide_s[...] = wide.reshape(wide_s.shape)
        part = pl.ds(pl.multiple_of(c * SUB, SUB), SUB)
        mine = pl.ds(pl.multiple_of(side * SUB, SUB), SUB)
        grad_one[part, :] = wide_s[core, mine, :]
        narrow = wide.astype(jnp.bfloat16)
        mixed = mixed_t[c]
        acc_write[...] += nn(mixed, narrow)
        grad_mixed = nt(write_out[...], narrow).astype(jnp.bfloat16)
        query = query_t[c]
        product = grad_mixed.astype(jnp.float32) * mixed.astype(jnp.float32)

        def body(start, carry):
            here = pl.ds(start, block)
            bias = mask_of(c, start)
            kept = []
            for h in range(heads):
                rows = head_rows(h)
                scores = nn(key[h, here, :], query[rows])
                weights = jnp.exp2(scores * (SCALE * LOG2E) + (bias + log_total[c, h : h + 1]))
                grad_weights = nn(value[h, here, :], grad_mixed[rows])
                delta = jnp.sum(product[rows], axis=0, keepdims=True)
                grad_scores = (weights * (grad_weights - delta)).astype(jnp.bfloat16)
                grad_key[h, here, :] += nt(grad_scores, query[rows])
                grad_value[h, here, :] += nt(weights.astype(jnp.bfloat16), grad_mixed[rows])
                kept.append(carry[h] + nn(key_t[rows, here], grad_scores))
            return tuple(kept)

        zero = jnp.zeros((HD, query.shape[1]), jnp.float32)
        grads = each_block(body, (zero,) * heads)
        grad_query_t[c] = (jnp.concatenate(grads, axis=0) * SCALE).astype(jnp.bfloat16)

    def step(i, carry):
        @pl.when(i < chunks)
        def _():
            write_forward(i)

        @pl.when(jnp.logical_and(i >= 1, i <= chunks))
        def _():
            finish_update(i - 1)

        @pl.when(i < chunks)
        def _():
            cross_update(i)

        @pl.when(jnp.logical_and(i >= 1, i <= chunks))
        def _():
            feed_forward(i - 1)

        @pl.when(i >= 2)
        def _():
            finish_grad(i - 2)

        @pl.when(jnp.logical_and(i >= 1, i <= chunks))
        def _():
            cross_grad(i - 1)
            weight_grads(i - 1)

        @pl.when(i >= 2)
        def _():
            write_backward(i - 2)

        return carry

    lax.fori_loop(0, chunks + 2, step, 0)
    owned = grad_pairs.shape[2]

    def pack(b, carry):
        here = pl.ds(pl.multiple_of(b * block, block), block)
        there = pl.ds(b * (block // owned), block // owned)
        shape = (block // owned, owned, heads * HD)
        keys = jnp.concatenate([grad_key[h, here, :] for h in range(heads)], axis=1)
        values = jnp.concatenate([grad_value[h, here, :] for h in range(heads)], axis=1)
        grad_pairs[there, 0] = (keys * SCALE).astype(jnp.bfloat16).reshape(shape)
        grad_pairs[there, 1] = values.astype(jnp.bfloat16).reshape(shape)
        return carry

    lax.fori_loop(0, blocks, pack, 0)
    grad_mlp_in[...] = acc_in[...].astype(jnp.bfloat16)
    grad_mlp_out[...] = acc_out[...].astype(jnp.bfloat16)
    grad_write_out[...] = acc_write[...].T.astype(jnp.bfloat16)


def middle(counts, tokens, cotangent, query_t, key, value, key_t, value_t, write_out, mlp_in, mlp_out, tok_count):
    rows, width = tokens.shape
    column = write_out.shape[0]
    hidden = mlp_in.shape[1]
    heads = column // HD
    latents = key.shape[1]
    owned = latents // tok_count
    quarter = rows // 4
    chunks = quarter // SUB
    size = 4 * SUB
    half = (2 * SUB, width)
    low, wide = jnp.bfloat16, jnp.float32
    vmem = pl.BlockSpec(memory_space=pltpu.VMEM)
    exchange = [
        pltpu.VMEM(half, wide),
        pltpu.VMEM(half, low),
        pltpu.VMEM((2, *half), low),
        pltpu.VMEM(half, low),
        pltpu.VMEM((2, *half), low),
    ]
    return pl.pallas_call(
        middle_kernel,
        out_shape=[
            jax.ShapeDtypeStruct((quarter, width), low),
            jax.ShapeDtypeStruct((quarter, width), wide),
            jax.ShapeDtypeStruct((chunks, column, size), low),
            jax.ShapeDtypeStruct((tok_count, 2, owned, column), low),
            jax.ShapeDtypeStruct((width, hidden), low),
            jax.ShapeDtypeStruct((width, hidden), low),
            jax.ShapeDtypeStruct((width, column), low),
        ],
        in_specs=[pl.BlockSpec(memory_space=pltpu.SMEM)] + [vmem] * 10,
        out_specs=[vmem] * 7,
        scratch_shapes=[
            pltpu.VMEM((chunks, 2, *half), low),
            pltpu.VMEM((chunks, column, size), low),
            pltpu.VMEM((chunks, 8, size), wide),
            *exchange,
            *exchange,
            pltpu.VMEM((2, 2, *half), low),
            pltpu.VMEM(half, wide),
            pltpu.VMEM(half, low),
            pltpu.VMEM((2, *half), low),
            pltpu.VMEM((2, SUB, width), low),
            pltpu.VMEM((2, SUB, width), low),
            pltpu.VMEM((width, hidden), wide),
            pltpu.VMEM((width, hidden), wide),
            pltpu.VMEM((column, width), wide),
            pltpu.VMEM((size, width), low),
            pltpu.VMEM((size, hidden), low),
            pltpu.VMEM((size, hidden), low),
            pltpu.VMEM((2, *half), wide),
            pltpu.VMEM((latents, 128), jnp.int32),
            pltpu.VMEM((heads, latents, HD), wide),
            pltpu.VMEM((heads, latents, HD), wide),
            pltpu.SemaphoreType.DMA((8, 2)),
            pltpu.SemaphoreType.DMA((8, 2)),
        ],
        compiler_params=pltpu.CompilerParams(
            collective_id=1, has_side_effects=True, vmem_limit_bytes=62 << 20
        ),
        name="middle",
    )(
        counts,
        tokens.reshape(4, quarter, width),
        cotangent.reshape(4, quarter, width),
        query_t,
        key,
        value,
        key_t,
        value_t,
        write_out,
        mlp_in,
        mlp_out,
    )


def back_kernel(
    counts, tokens, latents, grad_one, lat_one, mixed_in, read_key, read_value, read_key_t, own_key, own_value,
    own_key_t, query_t, grad_query_t, grad_pairs, parts_in, parts_out, grad_write, rquery, rkey, rvalue, rout,
    wquery, wkey, wvalue,
    input_grad, latent_grad, out_in, out_out, out_early, out_late, out_query,
    got_pairs, head_parts, output_all, output_t, rows_s, acc_query, acc_read, grad_own, query_sum, query_send,
    query_got, own_f, send_f, got_f, half_f, cross_f, wide_s, lat_parts, lat_got,
    in_one, in_sums, in_two, in_sems, out_one, out_sums, out_two, out_sems,
    parts_early, early_one, early_sums, early_two, early_sems,
    parts_late, late_one, late_sums, late_two, late_sems,
    parts_query, q_one, q_sums, q_two, q_sems,
    pair_sems, head_sems, output_sems, query_sems, lat_sems, send_sems, recv_sems,
):
    tok_count, owned, column = query_got.shape
    head_count = head_parts.shape[0]
    chunks = read_key.shape[0]
    heads = column // HD
    quarter, width = tokens.shape[1], tokens.shape[2]
    groups_here = 4 * quarter // GROUP
    latent_count = tok_count * owned
    block = min(512, latent_count)
    blocks, per = latent_count // block, block // owned
    tok, head = lax.axis_index("tok"), lax.axis_index("head")
    core, side = lax.rem(head, 2), head // 2
    other = 1 - core
    low, wide = jnp.bfloat16, jnp.float32
    greet_all(tok, head, tok_count, head_count)
    pairs = Spread("tok", tok, head, tok_count, lambda peer: grad_pairs.at[peer], got_pairs, pair_sems)
    pairs.start()
    by_in = Scatter(tok, head, parts_in, in_one, in_sums, in_two, in_sems)
    by_out = Scatter(tok, head, parts_out, out_one, out_sums, out_two, out_sems)
    by_in.start()
    by_out.start()
    early = Scatter(tok, head, parts_early, early_one, early_sums, early_two, early_sems)
    late = Scatter(tok, head, parts_late, late_one, late_sums, late_two, late_sems)
    final = Scatter(tok, head, parts_query, q_one, q_sums, q_two, q_sems)

    def put_parts(ref, at, value):
        share = value.shape[0] // tok_count
        for b in range(tok_count):
            ref[b // 2, b % 2, :, at : at + value.shape[1]] = value[b * share : (b + 1) * share].astype(low)

    def normed_chunk(c):
        return norm_parts(chunk_rows(tokens, c).astype(wide))[0].astype(low)

    acc_query[...] = jnp.zeros_like(acc_query)

    def query_weights(c, carry):
        acc_query[...] += tn(normed_chunk(c), grad_query_t[c].T)
        return carry

    lax.fori_loop(0, chunks, query_weights, 0)
    put_parts(parts_early, 0, acc_query[...])
    put_parts(parts_early, column, grad_write[...])
    pairs.wait()
    got_pairs[tok] = grad_pairs[tok]
    summed = lax.fori_loop(
        1, tok_count, lambda s, kept: kept + got_pairs[s].astype(wide), got_pairs[0].astype(wide)
    )
    grad_key, grad_value = summed[0].astype(low), summed[1].astype(low)
    head_parts[head] = (nt(grad_key, wkey[...]) + nt(grad_value, wvalue[...])).astype(low)
    moved = Spread("head", tok, head, head_count, lambda peer: head_parts.at[head], head_parts, head_sems)
    moved.start()
    normed_one, scale_one = norm_parts(lat_one[...])
    narrow_one = normed_one.astype(low)
    put_parts(parts_early, 2 * column, tn(narrow_one, grad_key))
    put_parts(parts_early, 3 * column, tn(narrow_one, grad_value))
    moved.wait()
    grad = head_parts[0].astype(wide)
    for s in range(1, head_count):
        grad = grad + head_parts[s].astype(wide)
    grad_lat_one = norm_vjp(normed_one, scale_one, grad)
    grad_own[...] = grad_lat_one
    narrow = grad_lat_one.astype(low)
    grad_mixed = nt(narrow, rout[...]).astype(low)
    mixed = mixed_in[:, :column]
    product = grad_mixed.astype(wide) * mixed
    extra = []
    for h in range(heads):
        delta = jnp.sum(product[:, head_rows(h)], axis=1, keepdims=True)
        logs = mixed_in[:, column + h : column + h + 1]
        for k, (first, second) in enumerate(zip(split_three(delta), split_three(logs), strict=True)):
            extra.append((3 * h + k, first))
            extra.append((3 * (heads + h) + k, second))
    output_all[tok, :, :column] = grad_mixed
    output_all[tok, :, column:] = pick_lanes((owned, output_all.shape[2] - column), extra).astype(low)
    outputs = Spread("tok", tok, head, tok_count, lambda peer: output_all.at[tok], output_all, output_sems)
    outputs.start()
    put_parts(parts_early, 4 * column, tn(narrow, mixed.astype(low)))
    early.start()
    acc_read[...] = jnp.zeros_like(acc_read)
    query_sum[...] = jnp.zeros_like(query_sum)
    by_in.forward_all()
    outputs.wait()

    def turn(b, carry):
        here = pl.ds(pl.multiple_of(b * block, block), block)
        turned = output_all[pl.ds(b * per, per)].reshape(block, output_all.shape[2]).astype(wide).T
        output_t[:, here] = turned[:column].astype(low)
        for h in range(2 * heads):
            at = column + 3 * h
            rows_s[h : h + 1, here] = turned[at : at + 1] + turned[at + 1 : at + 2] + turned[at + 2 : at + 3]
        return carry

    lax.fori_loop(0, blocks, turn, 0)

    def read_back(keys, values, keys_t, rows_for, here, h):
        hr = head_rows(h)
        query, output = query_t[hr, here], output_t[hr, here]
        scores = nn(keys, query)
        weights = jnp.exp2(add_rows(scores * (SCALE * LOG2E), rows_for(h)))
        grad_weights = nn(values, output)
        grad_scores = (weights * (grad_weights - rows_s[h : h + 1, here])).astype(low)
        query_sum[hr, here] += nn(keys_t, grad_scores)
        return nt(grad_scores, query), nt(weights.astype(low), output)

    def each_block(body, carry):
        if blocks == 1:
            return body(0, carry)
        return lax.fori_loop(0, blocks, body, carry)

    def key_grads(count, key_of, value_of, key_t_of, images):
        def body(b, carry):
            start = b * block
            here = pl.ds(start, block)
            row_image = latent_row_image(counts, start, block)

            def rows_for(h):
                logs = rows_s[heads + h : heads + h + 1, here]
                return [jnp.where(row_image == image, logs, MASKED) for image in images]

            kept = []
            for h in range(heads):
                dk, dv = read_back(key_of(h), value_of(h), key_t_of(h), rows_for, here, h)
                kept.append((carry[h][0] + dk, carry[h][1] + dv))
            return tuple(kept)

        zero = jnp.zeros((count, HD), wide)
        grads = each_block(body, ((zero, zero),) * heads)
        keys = jnp.concatenate([grads[h][0] for h in range(heads)], axis=1) * SCALE
        values = jnp.concatenate([grads[h][1] for h in range(heads)], axis=1)
        return keys.astype(low), values.astype(low)

    own_images = [image_of(counts, tok * groups_here + g) for g in range(owned // LPG)]
    own_dk, own_dv = key_grads(
        owned, lambda h: own_key[h], lambda h: own_value[h], lambda h: own_key_t[head_rows(h), :], own_images
    )

    def copy(kind, chunk, source, target, peer):
        slot = lax.rem(chunk, 2)
        return pltpu.make_async_remote_copy(
            src_ref=source,
            dst_ref=target,
            send_sem=send_sems.at[kind, slot],
            recv_sem=recv_sems.at[kind, slot],
            device_id=(tok, peer),
            device_id_type=MESH,
        )

    def core_copy(c):
        return copy(0, c, send_f, got_f.at[lax.rem(c, 2)], side * 2 + other)

    def cross_copy(c):
        return copy(1, c, half_f.at[1 - side], cross_f.at[lax.rem(c, 2)], (1 - side) * 2 + core)

    def compute(c):
        images = [
            image_of(counts, tok * groups_here + (q * quarter + c * SUB) // GROUP) for q in (0, 2, 1, 3)
        ]
        dk, dv = key_grads(
            4 * SUB,
            lambda h: read_key[c, h],
            lambda h: read_value[c, h],
            lambda h: read_key_t[c, head_rows(h), :],
            images,
        )
        moved = nt(dk, rkey[...]) + nt(dv, rvalue[...]) + tn(grad_query_t[c], wquery_t_of(wquery))
        wide_s[...] = moved.reshape(wide_s.shape)
        own_f[...] = wide_s[core]
        send_f[...] = wide_s[other].astype(low)
        core_copy(c).start()
        normed = normed_chunk(c)
        acc_read[0] += tn(normed, dk)
        acc_read[1] += tn(normed, dv)

    def wquery_t_of(ref):
        return ref[...].T

    def cross(c):
        core_copy(c).wait()
        total = own_f[...] + got_f[lax.rem(c, 2)].astype(wide)
        half_f[...] = total.astype(low).reshape(half_f.shape)
        cross_copy(c).start()

    def finish(c):
        cross_copy(c).wait()
        part = pl.ds(pl.multiple_of(c * SUB, SUB), SUB)
        total = half_f[side].astype(wide) + cross_f[lax.rem(c, 2)].astype(wide)
        normed, scale = norm_parts(tokens[head, part, :].astype(wide))
        input_grad[part, :] = grad_one[part, :] + norm_vjp(normed, scale, total)

    def step(c, carry):
        @pl.when(c >= 1)
        def _():
            @pl.when(c >= 2)
            def _():
                finish(c - 2)

            cross(c - 1)

        @pl.when(c < chunks)
        def _():
            compute(c)

        return carry

    half_way = chunks // 2
    lax.fori_loop(0, half_way, step, 0)
    by_out.forward_all()
    lax.fori_loop(half_way, chunks, step, 0)
    early.forward_all()

    def turn_query(b, carry):
        here = pl.ds(pl.multiple_of(b * block, block), block)
        turned = (query_sum[:, here] * SCALE).T.astype(low)
        query_send[pl.ds(b * per, per)] = turned.reshape(per, owned, column)
        return carry

    lax.fori_loop(0, blocks, turn_query, 0)
    queries = Spread("tok", tok, head, tok_count, lambda peer: query_send.at[peer], query_got, query_sems)
    queries.start()
    normed_lat, scale_lat = norm_parts(latents[...].astype(wide))
    narrow_lat = normed_lat.astype(low)
    put_parts(parts_late, 0, acc_read[0] + tn(narrow_lat, own_dk))
    put_parts(parts_late, column, acc_read[1] + tn(narrow_lat, own_dv))
    late.start()
    step(chunks, 0)
    queries.wait()
    query_got[tok] = query_send[tok]
    summed = lax.fori_loop(
        1, tok_count, lambda s, kept: kept + query_got[s].astype(wide), query_got[0].astype(wide)
    )
    grad_query = summed.astype(low)
    lat_total = nt(grad_query, rquery[...]) + nt(own_dk, rkey[...]) + nt(own_dv, rvalue[...])
    lat_parts[...] = lat_total.astype(low).reshape(lat_parts.shape)
    lats = Spread("head", tok, head, head_count, lambda peer: lat_parts.at[peer], lat_got, lat_sems)
    lats.start()
    put_parts(parts_query, 0, tn(narrow_lat, grad_query))
    final.start()
    late.forward_all()
    finish(chunks - 1)
    out_in[...] = by_in.finish()
    final.forward_all()
    lats.wait()
    lat_got[head] = lat_parts[head]
    total = lat_got[0].astype(wide)
    for s in range(1, head_count):
        total = total + lat_got[s].astype(wide)
    share = owned // head_count
    mine = pl.ds(pl.multiple_of(head * share, share), share)
    normed, scale = norm_parts(latents[mine, :].astype(wide))
    latent_grad[...] = grad_own[mine, :] + norm_vjp(normed, scale, total)
    out_out[...] = by_out.finish()
    out_early[...] = early.finish()
    out_late[...] = late.finish()
    out_query[...] = final.finish()


def back(
    counts, tokens, latents, grad_one, lat_one, mixed, read_key, read_value, read_key_t, own_key, own_value,
    own_key_t, query_t, grad_query_t, grad_pairs, grad_in, grad_out, grad_write, rquery, rkey, rvalue, rout,
    wquery, wkey, wvalue, tok_count, head_count,
):
    rows, width = tokens.shape
    owned, column = latents.shape[0], rquery.shape[1]
    hidden = grad_in.shape[1]
    quarter = rows // 4
    chunks, size = quarter // SUB, 4 * SUB
    latent_count = owned * tok_count
    outer, share = tok_count // 2, width // tok_count
    low, wide = jnp.bfloat16, jnp.float32
    vmem = pl.BlockSpec(memory_space=pltpu.VMEM)
    packed = 256
    half = (2 * SUB, width)

    def with_parts(columns):
        return [pltpu.VMEM((outer, 2, share, columns), low)] + scatter_scratch(outer, share, columns)

    return pl.pallas_call(
        back_kernel,
        out_shape=[
            jax.ShapeDtypeStruct((quarter, width), wide),
            jax.ShapeDtypeStruct((owned // head_count, width), wide),
            jax.ShapeDtypeStruct((share, hidden), wide),
            jax.ShapeDtypeStruct((share, hidden), wide),
            jax.ShapeDtypeStruct((share, 5 * column), wide),
            jax.ShapeDtypeStruct((share, 2 * column), wide),
            jax.ShapeDtypeStruct((share, column), wide),
        ],
        in_specs=[pl.BlockSpec(memory_space=pltpu.SMEM)] + [vmem] * 24,
        out_specs=[vmem] * 7,
        scratch_shapes=[
            pltpu.VMEM((tok_count, 2, owned, column), low),
            pltpu.VMEM((head_count, owned, width), low),
            pltpu.VMEM((tok_count, owned, packed), low),
            pltpu.VMEM((column, latent_count), low),
            pltpu.VMEM((8, latent_count), wide),
            pltpu.VMEM((width, column), wide),
            pltpu.VMEM((2, width, column), wide),
            pltpu.VMEM((owned, width), wide),
            pltpu.VMEM((column, latent_count), wide),
            pltpu.VMEM((tok_count, owned, column), low),
            pltpu.VMEM((tok_count, owned, column), low),
            pltpu.VMEM(half, wide),
            pltpu.VMEM(half, low),
            pltpu.VMEM((2, *half), low),
            pltpu.VMEM((2, SUB, width), low),
            pltpu.VMEM((2, SUB, width), low),
            pltpu.VMEM((2, *half), wide),
            pltpu.VMEM((head_count, owned // head_count, width), low),
            pltpu.VMEM((head_count, owned // head_count, width), low),
            *scatter_scratch(outer, share, hidden),
            *scatter_scratch(outer, share, hidden),
            *with_parts(5 * column),
            *with_parts(2 * column),
            *with_parts(column),
            pltpu.SemaphoreType.DMA((2, tok_count)),
            pltpu.SemaphoreType.DMA((2, head_count)),
            pltpu.SemaphoreType.DMA((2, tok_count)),
            pltpu.SemaphoreType.DMA((2, tok_count)),
            pltpu.SemaphoreType.DMA((2, head_count)),
            pltpu.SemaphoreType.DMA((2, 2)),
            pltpu.SemaphoreType.DMA((2, 2)),
        ],
        compiler_params=pltpu.CompilerParams(collective_id=3, has_side_effects=True, vmem_limit_bytes=62 << 20),
        name="back",
    )(
        counts, tokens.reshape(4, quarter, width), latents, grad_one, lat_one, mixed, read_key, read_value,
        read_key_t, own_key, own_value, own_key_t, query_t, grad_query_t, grad_pairs,
        grad_in.reshape(outer, 2, share, hidden), grad_out.reshape(outer, 2, share, hidden), grad_write,
        rquery, rkey, rvalue, rout, wquery, wkey, wvalue,
    )


def shards(
    tokens,
    latents,
    image_groups,
    read_query,
    read_key,
    read_value,
    read_out,
    write_query,
    write_key,
    write_value,
    write_out,
    mlp_in,
    mlp_out,
    cotangent,
):
    column = read_query.shape[1]
    tok_count = lax.axis_size("tok")
    head_count = lax.axis_size("head")
    (
        wquery_t, wkey, wvalue, wkey_t, wvalue_t, rkey, rvalue, rkey_t, own_key, own_value, own_key_t,
        rquery_t, lat_one, mixed,
    ) = front(
        image_groups, tokens, latents, read_query, read_key, read_value, read_out, write_query, write_key,
        write_value, tok_count, head_count,
    )
    layer_out, grad_one, grad_wquery_t, grad_pairs, grad_in, grad_out, grad_write = middle(
        image_groups, tokens, cotangent, wquery_t, wkey, wvalue, wkey_t, wvalue_t, write_out, mlp_in, mlp_out,
        tok_count,
    )
    input_grad, latent_grad, grad_mlp_in, grad_mlp_out, early, late, grad_read_query = back(
        image_groups, tokens, latents, grad_one, lat_one, mixed, rkey, rvalue, rkey_t, own_key, own_value,
        own_key_t, rquery_t, grad_wquery_t, grad_pairs, grad_in, grad_out, grad_write, read_query, read_key,
        read_value, read_out, write_query, write_key, write_value, tok_count, head_count,
    )

    def part(array, k):
        return array[:, k * column : (k + 1) * column]

    return (
        layer_out,
        input_grad,
        latent_grad,
        grad_read_query,
        part(late, 0),
        part(late, 1),
        part(early, 4).T,
        part(early, 0),
        part(early, 2),
        part(early, 3),
        part(early, 1).T,
        grad_mlp_in,
        grad_mlp_out.T,
    )
def solution(mesh):
    return jax.shard_map(
        shards,
        mesh=mesh,
        in_specs=(
            P("tok", None),
            P("tok", None),
            P(),
            P(None, "head"),
            P(None, "head"),
            P(None, "head"),
            P("head", None),
            P(None, "head"),
            P(None, "head"),
            P(None, "head"),
            P("head", None),
            P(None, "head"),
            P("head", None),
            P("tok", None),
        ),
        out_specs=(
            P(("tok", "head"), None),
            P(("tok", "head"), None),
            P(("tok", "head"), None),
            P("tok", "head"),
            P("tok", "head"),
            P("tok", "head"),
            P("head", "tok"),
            P("tok", "head"),
            P("tok", "head"),
            P("tok", "head"),
            P("head", "tok"),
            P("tok", "head"),
            P("head", "tok"),
        ),
        check_vma=False,
    )
```

time: 852 us -> 286 us (0.34)
  waiting for transfers between devices: 250 us -> 0 us
  blocking collectives: 200 us -> 0 us
  Pallas kernels: 171 us -> 269 us
  other arithmetic: 77.9 us -> 0 us
  matrix products: 74.9 us -> 0 us
  local copies, waits for them, and re-layouts: 54.3 us -> 16 us
  between operations: 15.8 us -> 0.74 us
    all_gather x6 -> x0, blocking collectives: 178 us -> none  [the longest x1 33.1 us: shards(): query_all = lax.all_gather(query_own, 'tok', axis=0, tiled=True)]
    unnamed x11 -> x0, waiting for transfers between devices: 176 us -> none
    pallas_call x1 -> x2, Pallas kernels: 67.4 us -> 166 us  [the longest x1 118 us: back(): pl.pallas_call(back_kernel, out_shape=[jax.ShapeDtypeStruct((quarter, wid...]
    dot_general x33 -> x0, matrix products: 74.9 us -> none  [the longest x9 19.3 us: right_trans(): lax.dot_general(left, right, (((1,), (1,)), ((), ())), preferred_element_...]
    psum x3 -> x0, waiting for transfers between devices: 74.3 us -> none  [the longest x1 43.6 us: shards(): totals_all, sums_all = lax.psum((totals, sums), 'tok')]
    select_n x1 -> x0, other arithmetic: 36 us -> none  [shards(): latent_image = jnp.repeat(group_image, LPG, total_repeat_length=all_latents)]
    psum x1 -> x0, blocking collectives: 21.8 us -> none  [shards(): totals_all, sums_all = lax.psum((totals, sums), 'tok')]
    reduce_sum x16 -> x0, other arithmetic: 19.1 us -> none  [the longest x8 11.1 us: norm_rows(): center = values - jnp.mean(values, axis=-1, keepdims=True)]
  transfers between devices with their start and end apart: 8 -> 0, of which waited for: 6 -> 0; matrix products, arithmetic and copies ran while one was open for 10% -> 0% of each run, Pallas kernels for 8% -> 0%
where the time goes in v3:
time: 286 us
  Pallas kernels  269 us (94%)
  local copies, waits for them, and re-layouts  16 us (6%)
    pallas_call x1, Pallas kernels, back(): pl.pallas_call(back_kernel, out_shape=[jax.ShapeDtypeStruct((quarter, wid...  118 us
    pallas_call x1, Pallas kernels, middle(): pl.pallas_call(middle_kernel, out_shape=[jax.ShapeDtypeStruct((quarter, w...  103 us
    pallas_call x1, Pallas kernels, front(): pl.pallas_call(front_kernel, out_shape=[jax.ShapeDtypeStruct((chunks, col...  47.8 us
    unnamed x34, local copies, waits for them, and re-layouts  13.8 us

profile of v3, /device:TPU:0, one launch (start us, length us, event | category | flops | bytes accessed | tf_op | source)
XLA Modules:
  0.0 285.7 jit_solution(3488158176794769052)
XLA Ops:
  0.6 0.0 copy-start.4
  0.7 0.0 copy-start.5
  0.7 0.0 copy-start.6
  0.7 0.0 copy-start.7
  0.7 2.0 copy.27.rquery
  2.7 1.9 copy.28.rkey
  4.5 0.0 copy-done.4
  4.5 0.9 copy.29.rvalue
  5.4 0.0 copy-done.5
  5.4 0.9 copy.30.wquery
  6.4 0.0 copy-done.6
  6.4 0.9 copy.31.wkey
  7.3 0.0 copy-done.7
  7.3 0.9 copy.32.wvalue
  8.3 47.8 %front.1 = (bf16[8,192,256]{2,1,0:T(8,128)(2,1)}, bf16[3,512,64]{2,1,0:T(8,128)(2,1)}, bf16[3,512,64]{2,1,0:T(8,128)(2,1)}, bf16[192,512]{1,0:T(8,128)(2,1)}, bf...) custom-call(s32[5]{0:T(128)} %counts.5, ...), custom_call_target="tpu_custom_call" | custom-call | tf_op jit(solution)/shard_map/front/pallas_call | solution.py:368
  56.1 103.4 %middle.1 = (bf16[512,768]{1,0:T(8,128)(2,1)}, f32[512,768]{1,0:T(8,128)}, bf16[8,192,256]{2,1,0:T(8,128)(2,1)}, bf16[8,2,64,192]{3,2,1,0:T(8,128)(2,1)}, bf16[7...) custom-call(s32[5]{0:T(128)} %counts.5, bf16[4,512,768]{2,1,0:T(8,128)(2,1)} %bitcast.10, ...), custom_call_target="tpu_custom_call" | custom-call | tf_op jit(solution)/shard_map/middle/pallas_call | solution.py:737
  159.5 117.8 %back.1 = (f32[512,768]{1,0:T(8,128)}, f32[16,768]{1,0:T(8,128)}, f32[96,768]{1,0:T(8,128)}, f32[96,768]{1,0:T(8,128)}, f32[96,960]{1,0:T(8,128)}, /*index=5*/f32[96,384]{1,0:T(8,128)}, f32[96,192]{1,0:T(8,128)}) custom-call(s32[5]{0:T(128)} %counts.5, bf16[4,512,768]{2,1,0:T(8,128)(2,1)} %bitcast.11, bf16[64,768]{1,0:T(8,128)(2,1)} %latents.3, ...), custom_call_target="tpu_custom_call" | custom-call | tf_op jit(solution)/shard_map/back/pallas_call | solution.py:1082
  277.3 0.0 copy-start.1
  277.3 0.0 copy-start
  277.3 2.2 slice_bitcast_fusion
  279.5 0.7 copy.39
  280.3 0.7 copy.40
  281.0 0.0 copy-done.1
  281.0 0.9 copy.47
  281.9 0.0 copy-done
  281.9 0.0 copy-start.9
  281.9 0.0 copy-start.8
  281.9 0.0 copy-start.3
  281.9 0.0 copy-start.2
  281.9 1.1 copy.48
  283.0 0.0 copy-done.9
  283.0 0.6 copy.49
  283.7 0.0 copy-done.8
  283.7 0.6 copy.50
  284.3 0.0 copy-done.3
  284.3 0.7 copy.51
  285.0 0.0 copy-done.2
  285.0 0.7 copy.52
Async XLA Ops:
  0.6 3.9 %copy-start.4 = (bf16[768,192]{0,1:T(8,128)(2,1)S(1)}, bf16[768,192]{0,1:T(8,128)(2,1)}, u32[]{:S(2)}) copy-start(bf16[768,192]{0,1:T(8,128)(2,1)} %param.19) | copy-start | bytes 884740
  0.7 4.8 %copy-start.5 = (bf16[768,192]{0,1:T(8,128)(2,1)S(1)}, bf16[768,192]{0,1:T(8,128)(2,1)}, u32[]{:S(2)}) copy-start(bf16[768,192]{0,1:T(8,128)(2,1)} %param.21) | copy-start | bytes 884740
  0.7 5.7 %copy-start.6 = (bf16[768,192]{0,1:T(8,128)(2,1)S(1)}, bf16[768,192]{0,1:T(8,128)(2,1)}, u32[]{:S(2)}) copy-start(bf16[768,192]{0,1:T(8,128)(2,1)} %param.22) | copy-start | bytes 884740
  0.7 6.6 %copy-start.7 = (bf16[768,192]{0,1:T(8,128)(2,1)S(1)}, bf16[768,192]{0,1:T(8,128)(2,1)}, u32[]{:S(2)}) copy-start(bf16[768,192]{0,1:T(8,128)(2,1)} %param.23) | copy-start | bytes 884740
  277.3 3.7 %copy-start.1 = (bf16[512,768]{1,0:T(8,128)(2,1)S(1)}, bf16[512,768]{1,0:T(8,128)(2,1)}, u32[]{:S(2)}) copy-start(bf16[512,768]{1,0:T(8,128)(2,1)} %get-tuple-element.104) | copy-start | bytes 2359300
  277.3 4.6 %copy-start = (f32[512,768]{1,0:T(8,128)S(1)}, f32[512,768]{1,0:T(8,128)}, u32[]{:S(2)}) copy-start(f32[512,768]{1,0:T(8,128)} %get-tuple-element.105) | copy-start | bytes 4718596
  281.9 1.2 copy-start.9
  281.9 1.8 copy-start.8
  281.9 2.4 copy-start.3
  281.9 3.1 %copy-start.2 = (f32[96,768]{1,0:T(8,128)S(1)}, f32[96,768]{1,0:T(8,128)}, u32[]{:S(2)}) copy-start(f32[96,768]{1,0:T(8,128)} %get-tuple-element.68) | copy-start | bytes 884740

commit v4 on v0

v4 whole, which is shorter than its diff:
```python
from functools import partial
from types import SimpleNamespace

import jax
import jax.numpy as jnp
from jax import lax
from jax.experimental import pallas as pl
from jax.experimental.pallas import tpu as pltpu
from jax.sharding import PartitionSpec as P

MESH = pl.DeviceIdType.MESH
HD = 64
GROUP = 256
LPG = 8
epsilon = 1e-05
SUB = 64
SCALE = 0.125
LOG2E = 1.4426950408889634
MASKED = -1e30
GELU_A = 0.7978845608028654
GELU_B = 0.044715


def nn(left, right):
    return lax.dot_general(left, right, (((1,), (0,)), ((), ())), preferred_element_type=jnp.float32)


def nt(left, right):
    return lax.dot_general(left, right, (((1,), (1,)), ((), ())), preferred_element_type=jnp.float32)


def tn(left, right):
    return lax.dot_general(left, right, (((0,), (0,)), ((), ())), preferred_element_type=jnp.float32)


def norm_parts(values):
    center = values - jnp.mean(values, axis=-1, keepdims=True)
    scale = lax.rsqrt(jnp.mean(center * center, axis=-1, keepdims=True) + epsilon)
    return center * scale, scale


def norm_vjp(normed, scale, grad):
    return scale * (
        grad
        - jnp.mean(grad, axis=-1, keepdims=True)
        - normed * jnp.mean(grad * normed, axis=-1, keepdims=True)
    )


def image_of(counts, group):
    bound = jnp.int32(0)
    image = jnp.zeros_like(group)
    for m in range(counts.shape[0]):
        bound = bound + counts[m]
        image = image + jnp.where(bound <= group, 1, 0)
    return image


def latent_row_image(counts, start, count):
    group = lax.shift_right_logical(lax.broadcasted_iota(jnp.int32, (1, count), 1) + start, 3)
    return image_of(counts, group)


def head_rows(h):
    return slice(h * HD, (h + 1) * HD)


def chunk_rows(ref, c):
    part = pl.ds(pl.multiple_of(c * SUB, SUB), SUB)
    return jnp.concatenate([ref[q, part, :] for q in (0, 2, 1, 3)], axis=0)


def greet_all(r, d):
    barrier = pltpu.get_barrier_semaphore()

    def greet(step, carry):
        peer = lax.rem(r.tok + step, d.tok_count)
        pl.semaphore_signal(barrier, inc=1, device_id=(peer, r.head), device_id_type=MESH)
        return carry

    lax.fori_loop(1, d.tok_count, greet, 0)
    for step in range(1, d.head_count):
        peer = lax.rem(r.head + step, d.head_count)
        pl.semaphore_signal(barrier, inc=1, device_id=(r.tok, peer), device_id_type=MESH)
    pl.semaphore_wait(barrier, d.tok_count + d.head_count - 2)


class Spread:
    def __init__(self, axis, tok, head, count, source, got, sems):
        self.axis, self.tok, self.head, self.count = axis, tok, head, count
        self.me = tok if axis == "tok" else head
        self.source, self.got, self.sems = source, got, sems

    def copy(self, peer, slot):
        return pltpu.make_async_remote_copy(
            src_ref=self.source(peer),
            dst_ref=self.got.at[slot],
            send_sem=self.sems.at[0, peer],
            recv_sem=self.sems.at[1, slot],
            device_id=(peer, self.head) if self.axis == "tok" else (self.tok, peer),
            device_id_type=MESH,
        )

    def start(self):
        def go(step, carry):
            self.copy(lax.rem(self.me + step, self.count), self.me).start()
            return carry

        lax.fori_loop(1, self.count, go, 0)

    def wait(self):
        def go(step, carry):
            peer = lax.rem(self.me + step, self.count)
            self.copy(peer, peer).wait()
            return carry

        lax.fori_loop(1, self.count, go, 0)


class Scatter:
    def __init__(self, r, parts, got_one, got_two, sems):
        self.head, self.mine, self.side = r.head, r.tok // 2, lax.rem(r.tok, 2)
        self.parts, self.got_one, self.got_two, self.sems = parts, got_one, got_two, sems
        self.outer = parts.shape[0]

    def first(self, block):
        return pltpu.make_async_remote_copy(
            src_ref=self.parts.at[block, 1 - self.side],
            dst_ref=self.got_one.at[block],
            send_sem=self.sems.at[0, block],
            recv_sem=self.sems.at[1, block],
            device_id=(self.mine * 2 + (1 - self.side), self.head),
            device_id_type=MESH,
        )

    def second(self, block, source):
        return pltpu.make_async_remote_copy(
            src_ref=self.got_one.at[block],
            dst_ref=self.got_two.at[source],
            send_sem=self.sems.at[2, block],
            recv_sem=self.sems.at[3, source],
            device_id=(block * 2 + self.side, self.head),
            device_id_type=MESH,
        )

    def start(self):
        def go(step, carry):
            self.first(lax.rem(self.mine + step, self.outer)).start()
            return carry

        lax.fori_loop(1, self.outer + 1, go, 0)

    def total(self, block):
        self.first(block).wait()
        both = self.parts[block, self.side].astype(jnp.float32) + self.got_one[block].astype(jnp.float32)
        return both.astype(jnp.bfloat16)

    def forward(self):
        def go(step, carry):
            block = lax.rem(self.mine + step, self.outer)
            self.got_one[block] = self.total(block)
            self.second(block, self.mine).start()
            return carry

        lax.fori_loop(1, self.outer, go, 0)

    def finish(self):
        self.got_two[self.mine] = self.total(self.mine)

        def go(step, carry):
            peer = lax.rem(self.mine + step, self.outer)
            self.second(peer, peer).wait()
            return carry

        lax.fori_loop(1, self.outer, go, 0)


def split_three(value):
    high = value.astype(jnp.bfloat16).astype(jnp.float32)
    rest = value - high
    middle_part = rest.astype(jnp.bfloat16).astype(jnp.float32)
    return high, middle_part, rest - middle_part


def pick_lanes(shape, columns):
    lane = lax.broadcasted_iota(jnp.int32, shape, 1)
    value = jnp.zeros(shape, jnp.float32)
    for at, column in columns:
        value = jnp.where(lane == at, column, value)
    return value


def by_head(shape, columns):
    lane = lax.broadcasted_iota(jnp.int32, shape, 1)
    value = jnp.broadcast_to(columns[-1], shape)
    for h in range(len(columns) - 2, -1, -1):
        value = jnp.where(lane < (h + 1) * HD, columns[h], value)
    return value


def chunk_bias(counts, tok, groups_here, c, quarter, row_image, rows):
    kept = []
    for q in (0, 2, 1, 3):
        group = tok * groups_here + (q * quarter + c * SUB) // GROUP
        image = image_of(counts, group)
        kept.append([jnp.where(row_image == image, row, MASKED) for row in rows])
    return kept


def add_rows(values, rows):
    count = values.shape[0] // len(rows)
    return jnp.concatenate([values[k * count : (k + 1) * count] + row for k, row in enumerate(rows)], axis=0)


def token_images(r, d, c):
    return [
        image_of(r.counts, r.tok * d.groups_here + (q * d.quarter + c * SUB) // GROUP) for q in (0, 2, 1, 3)
    ]


def spread_of(r, d, axis, source, got, sems):
    count = d.tok_count if axis == "tok" else d.head_count
    return Spread(axis, r.tok, r.head, count, source, got, sems)


def sum_slots(ref, count):
    first = ref[0].astype(jnp.float32)
    return lax.fori_loop(1, count, lambda s, kept: kept + ref[s].astype(jnp.float32), first)


def each_block(d, body, carry):
    if d.blocks == 1:
        return body(0, carry)
    return lax.fori_loop(0, d.blocks, lambda b, kept: body(b, kept), carry)


def block_at(d, b):
    start = b * d.block if d.blocks == 1 else pl.multiple_of(b * d.block, d.block)
    return start, pl.ds(start, d.block)


def keep_heads(ref, wide, heads):
    for h in range(heads):
        ref[h] = wide[:, head_rows(h)]


def chunk_core_side(r):
    return lax.rem(r.head, 2), r.head // 2


def loads(r):
    pairs = (
        (r.write_out_hbm, r.write_out),
        (r.mlp_in_hbm, r.mlp_in),
        (r.mlp_out_hbm, r.mlp_out),
        (r.cotangent_hbm, r.cotangent),
    )
    return [pltpu.make_async_copy(source, target, r.load_sems.at[k]) for k, (source, target) in enumerate(pairs)]


def front_phase(r, d):
    low = jnp.bfloat16
    heads, column, chunks, owned = d.heads, d.column, d.chunks, d.owned
    latents_wide = r.latents[...].astype(jnp.float32)
    normed_lat = norm_parts(latents_wide)[0].astype(low)
    r.query_all[r.tok] = nt(normed_lat, r.rquery[...]).astype(low)
    greet_all(r, d)
    queries = spread_of(r, d, "tok", lambda peer: r.query_all.at[r.tok], r.query_all, r.query_sems)
    queries.start()
    keys = nt(normed_lat, r.rkey[...]).astype(low)
    values = nt(normed_lat, r.rvalue[...]).astype(low)
    keep_heads(r.own_key, keys, heads)
    keep_heads(r.own_value, values, heads)
    r.own_key_t[...] = keys.T
    r.own_value_t[...] = values.T

    def project(c, carry):
        normed = norm_parts(chunk_rows(r.tokens, c).astype(jnp.float32))[0].astype(low)
        r.update[c] = normed.reshape(r.update.shape[1:])
        keys = nt(normed, r.rkey[...]).astype(low)
        values = nt(normed, r.rvalue[...]).astype(low)
        keep_heads(r.read_key.at[c], keys, heads)
        keep_heads(r.read_value.at[c], values, heads)
        r.read_key_t[c] = keys.T
        r.read_value_t[c] = values.T
        return carry

    lax.fori_loop(0, chunks, project, 0)
    r.sums[...] = jnp.zeros_like(r.sums)
    queries.wait()

    def attend(scores, rows, values_t, here, h):
        weights = jnp.exp2(add_rows(scores * (SCALE * LOG2E), rows))
        r.sums[column + h : column + h + 1, here] += jnp.sum(weights, axis=0, keepdims=True)
        r.sums[head_rows(h), here] += nn(values_t, weights.astype(low))

    def read_block(b, carry):
        start, here = block_at(d, b)
        query = r.query_all[pl.ds(b * d.per, d.per)].reshape(d.block, column).T
        r.read_query_t[:, here] = query
        row_image = latent_row_image(r.counts, start, d.block)

        def masks(images):
            return [jnp.where(row_image == image, 0.0, MASKED) for image in images]

        def read_chunk(c, carry):
            rows = masks(token_images(r, d, c))
            for h in range(heads):
                attend(nn(r.read_key[c, h], query[head_rows(h)]), rows, r.read_value_t[c, head_rows(h)], here, h)
            return carry

        lax.fori_loop(0, chunks, read_chunk, 0)
        rows = masks([image_of(r.counts, r.tok * d.groups_here + g) for g in range(d.groups_here)])
        for h in range(heads):
            attend(nn(r.own_key[h], query[head_rows(h)]), rows, r.own_value_t[head_rows(h), :], here, h)
        total = r.sums[column : column + heads, here]
        high = total.astype(low).astype(jnp.float32)
        r.sums[column : column + heads, here] = high
        r.sums[column + heads : column + 2 * heads, here] = total - high
        r.sums_send[pl.ds(b * d.per, d.per)] = r.sums[:, here].T.astype(low).reshape(d.per, owned, d.packed)
        return carry

    each_block(d, read_block, 0)
    totals = spread_of(r, d, "tok", lambda peer: r.sums_send.at[peer], r.sums_got, r.sums_sems)
    totals.start()

    def project_query(c, carry):
        r.query_t[c] = nt(r.wquery[...], r.update[c].reshape(4 * SUB, d.width)).astype(low)
        return carry

    lax.fori_loop(0, chunks, project_query, 0)
    totals.wait()
    r.sums_got[r.tok] = r.sums_send[r.tok]
    summed = sum_slots(r.sums_got, d.tok_count)
    whole = [
        summed[:, column + h : column + h + 1] + summed[:, column + heads + h : column + heads + h + 1]
        for h in range(heads)
    ]
    mixed = summed[:, :column] / by_head((owned, column), whole)
    r.mixed[:, :column] = mixed
    r.mixed[:, column:] = pick_lanes(
        (owned, d.packed - column), [(h, -jnp.log2(whole[h])) for h in range(heads)]
    )
    r.head_parts[r.head] = nn(mixed.astype(low), r.rout[...]).astype(low)
    moved = spread_of(r, d, "head", lambda peer: r.head_parts.at[r.head], r.head_parts, r.head_sems)
    moved.start()
    moved.wait()
    latents_one = latents_wide
    for s in range(d.head_count):
        latents_one = latents_one + r.head_parts[s].astype(jnp.float32)
    r.lat_one[...] = latents_one
    normed_one = norm_parts(latents_one)[0].astype(low)
    r.pair_all[r.tok, :, :column] = nt(normed_one, r.wkey[...]).astype(low)
    r.pair_all[r.tok, :, column:] = nt(normed_one, r.wvalue[...]).astype(low)
    pairs = spread_of(r, d, "tok", lambda peer: r.pair_all.at[r.tok], r.pair_all, r.pair_sems)
    pairs.start()
    pairs.wait()

    def unpack(b, carry):
        start, here = block_at(d, b)
        wide = r.pair_all[pl.ds(b * d.per, d.per)].reshape(d.block, 2 * column)
        for h in range(heads):
            r.key[h, here, :] = wide[:, head_rows(h)]
            r.value[h, here, :] = wide[:, head_rows(heads + h)]
        turned = wide.T
        r.key_t[:, here] = turned[:column]
        r.value_t[:, here] = turned[column:]
        return carry

    each_block(d, unpack, 0)


def mlp_scatters(r):
    return (
        Scatter(r, r.parts_in, r.in_one, r.in_two, r.in_sems),
        Scatter(r, r.parts_out, r.out_one, r.out_two, r.out_sems),
    )


def cross_f(r, c):
    core, side = chunk_core_side(r)
    return pltpu.make_async_remote_copy(
        src_ref=r.f_half.at[c, 1 - side],
        dst_ref=r.f_cross.at[c],
        send_sem=r.f_sems.at[0, c],
        recv_sem=r.f_sems.at[1, c],
        device_id=(r.tok, (1 - side) * 2 + core),
        device_id_type=MESH,
    )


def middle_phase(r, d, merged):
    chunks, heads, width = d.chunks, d.heads, d.width
    core, side = chunk_core_side(r)
    other = 1 - core
    core_peer = (r.tok, side * 2 + other)
    side_peer = (r.tok, (1 - side) * 2 + core)
    for load in loads(r):
        load.wait()

    def copy(kind, chunk, source, target, peer):
        slot = lax.rem(chunk, 2)
        return pltpu.make_async_remote_copy(
            src_ref=source,
            dst_ref=target,
            send_sem=r.send_sems.at[kind, slot],
            recv_sem=r.recv_sems.at[kind, slot],
            device_id=peer,
            device_id_type=MESH,
        )

    def core_a(c):
        return copy(0, c, r.send_a, r.got_a.at[lax.rem(c, 2)], core_peer)

    def cross_copy_a(c):
        return copy(1, c, r.half_a, r.cross_a.at[lax.rem(c, 2)], side_peer)

    def core_u(c):
        return copy(2, c, r.update.at[c, core], r.update.at[c, core], core_peer)

    def core_d(c):
        return copy(3, c, r.send_d, r.got_d.at[lax.rem(c, 2)], core_peer)

    def cross_copy_d(c):
        return copy(4, c, r.half_d, r.cross_d.at[lax.rem(c, 2)], side_peer)

    def core_s(c):
        half = r.summed_d.at[lax.rem(c, 2), core]
        return copy(5, c, half, half, core_peer)

    def core_f(c):
        return copy(6, c, r.send_f, r.got_f.at[lax.rem(c, 2)], core_peer)

    group = lax.shift_right_logical(lax.broadcasted_iota(jnp.int32, r.latent_image.shape, 0), 3)
    r.latent_image[...] = image_of(r.counts, group)

    def mask_of(c, here):
        image = r.latent_image[here, :]
        image = jnp.concatenate([image, image], axis=1)
        lane = lax.broadcasted_iota(jnp.int32, (1, 4 * SUB), 1)
        part = lax.shift_right_logical(lane, 6)
        part = 2 * lax.rem(part, 2) + part // 2
        row = part * d.quarter + c * SUB
        group = r.tok * d.groups_here + lax.shift_right_logical(row, 8)
        return jnp.where(image == image_of(r.counts, group), 0.0, MASKED)

    def halve(wide, own, send):
        r.wide_s[...] = wide.reshape(r.wide_s.shape)
        own[...] = r.wide_s[core]
        send[...] = r.wide_s[other].astype(jnp.bfloat16)

    r.acc_in[...] = jnp.zeros_like(r.acc_in)
    r.acc_out[...] = jnp.zeros_like(r.acc_out)
    r.acc_write[...] = jnp.zeros_like(r.acc_write)
    r.grad_key[...] = jnp.zeros_like(r.grad_key)
    r.grad_value[...] = jnp.zeros_like(r.grad_value)

    def write_forward(c):
        query = r.query_t[c]

        def body(b, carry):
            here = block_at(d, b)[1]
            bias = mask_of(c, here)
            kept = []
            for h in range(heads):
                scores = nn(r.key[h, here, :], query[head_rows(h)])
                weights = jnp.exp2(scores * (SCALE * LOG2E) + bias)
                total = jnp.sum(weights, axis=0, keepdims=True)
                mixed = nn(r.value_t[head_rows(h), here], weights.astype(jnp.bfloat16))
                kept.append((carry[h][0] + total, carry[h][1] + mixed))
            return tuple(kept)

        size = 4 * SUB
        zero = (jnp.zeros((1, size), jnp.float32), jnp.zeros((HD, size), jnp.float32))
        totals = each_block(d, body, (zero,) * heads)
        mixed = jnp.concatenate([part / total for total, part in totals], axis=0)
        mixed = mixed.astype(jnp.bfloat16)
        r.mixed_t[c] = mixed
        for h in range(heads):
            r.log_total[c, h : h + 1] = -jnp.log2(totals[h][0])
        halve(tn(mixed, r.write_out[...]), r.own_a, r.send_a)
        core_a(c).start()

    def finish_update(c):
        cross_copy_a(c).wait()
        mine = r.half_a[...].astype(jnp.float32) + r.cross_a[lax.rem(c, 2)].astype(jnp.float32)
        r.update[c, core] = mine.astype(jnp.bfloat16)
        core_u(c).start()

    def cross_update(c):
        core_a(c).wait()
        r.half_a[...] = (r.own_a[...] + r.got_a[lax.rem(c, 2)].astype(jnp.float32)).astype(jnp.bfloat16)
        cross_copy_a(c).start()

    def one_rows(c):
        moved = r.update[c].reshape(4 * SUB, width).astype(jnp.float32)
        return chunk_rows(r.tokens, c).astype(jnp.float32) + moved

    def feed_forward(c):
        core_u(c).wait()
        normed = norm_parts(one_rows(c))[0].astype(jnp.bfloat16)
        r.normed_s[...] = normed
        inner = nn(normed, r.mlp_in[...])
        square = inner * inner
        tanh = jnp.tanh(GELU_A * inner * (1.0 + GELU_B * square))
        half = 0.5 + 0.5 * tanh
        active = (inner * half).astype(jnp.bfloat16)
        r.act_s[...] = active
        slope = half + 0.5 * GELU_A * inner * (1.0 - tanh * tanh) * (1.0 + 3.0 * GELU_B * square)
        grad_inner = (nt(chunk_rows(r.cotangent, c), r.mlp_out[...]) * slope).astype(jnp.bfloat16)
        r.inner_s[...] = grad_inner
        halve(nt(grad_inner, r.mlp_in[...]), r.own_d, r.send_d)
        core_d(c).start()
        halve(nn(active, r.mlp_out[...]), r.own_f, r.send_f)
        core_f(c).start()

    def finish_grad(c):
        slot = lax.rem(c, 2)
        cross_copy_d(c).wait()
        mine = r.half_d[...].astype(jnp.float32) + r.cross_d[slot].astype(jnp.float32)
        r.summed_d[slot, core] = mine.astype(jnp.bfloat16)
        core_s(c).start()

    def cross_grad(c):
        slot = lax.rem(c, 2)
        core_d(c).wait()
        r.half_d[...] = (r.own_d[...] + r.got_d[slot].astype(jnp.float32)).astype(jnp.bfloat16)
        cross_copy_d(c).start()

    def keep_forward(c):
        slot = lax.rem(c, 2)
        core_f(c).wait()
        total = (r.own_f[...] + r.got_f[slot].astype(jnp.float32)).reshape(2, SUB, width)
        r.f_half[c] = total.astype(jnp.bfloat16)
        part = pl.ds(pl.multiple_of(c * SUB, SUB), SUB)
        rows = pl.ds(pl.multiple_of(side * SUB, SUB), SUB)
        mine = jnp.where(side == 0, total[0], total[1]) + r.update[c, core, rows, :].astype(jnp.float32)
        r.f_half[c, side] = (mine + r.tokens[r.head, part, :].astype(jnp.float32)).astype(jnp.bfloat16)

    def weight_grads(c):
        r.acc_in[...] += tn(r.normed_s[...], r.inner_s[...])
        r.acc_out[...] += tn(chunk_rows(r.cotangent, c), r.act_s[...])

    def write_backward(c):
        core_s(c).wait()
        normed, scale = norm_parts(one_rows(c))
        grad = r.summed_d[lax.rem(c, 2)].reshape(4 * SUB, width).astype(jnp.float32)
        wide = chunk_rows(r.cotangent, c).astype(jnp.float32) + norm_vjp(normed, scale, grad)
        r.wide_s[...] = wide.reshape(r.wide_s.shape)
        part = pl.ds(pl.multiple_of(c * SUB, SUB), SUB)
        mine = pl.ds(pl.multiple_of(side * SUB, SUB), SUB)
        r.grad_one[part, :] = r.wide_s[core, mine, :]
        narrow = wide.astype(jnp.bfloat16)
        mixed = r.mixed_t[c]
        r.acc_write[...] += nn(mixed, narrow)
        grad_mixed = nt(r.write_out[...], narrow).astype(jnp.bfloat16)
        query = r.query_t[c]
        product = grad_mixed.astype(jnp.float32) * mixed.astype(jnp.float32)

        def body(b, carry):
            here = block_at(d, b)[1]
            bias = mask_of(c, here)
            kept = []
            for h in range(heads):
                rows = head_rows(h)
                scores = nn(r.key[h, here, :], query[rows])
                weights = jnp.exp2(scores * (SCALE * LOG2E) + (bias + r.log_total[c, h : h + 1]))
                grad_weights = nn(r.value[h, here, :], grad_mixed[rows])
                delta = jnp.sum(product[rows], axis=0, keepdims=True)
                grad_scores = (weights * (grad_weights - delta)).astype(jnp.bfloat16)
                r.grad_key[h, here, :] += nt(grad_scores, query[rows])
                r.grad_value[h, here, :] += nt(weights.astype(jnp.bfloat16), grad_mixed[rows])
                kept.append(carry[h] + nn(r.key_t[rows, here], grad_scores))
            return tuple(kept)

        zero = jnp.zeros((HD, 4 * SUB), jnp.float32)
        grads = each_block(d, body, (zero,) * heads)
        r.grad_query_t[c] = (jnp.concatenate(grads, axis=0) * SCALE).astype(jnp.bfloat16)

    def step(i, carry):
        @pl.when(i < chunks)
        def _():
            write_forward(i)

        @pl.when(jnp.logical_and(i >= 1, i <= chunks))
        def _():
            finish_update(i - 1)

        @pl.when(i < chunks)
        def _():
            cross_update(i)

        @pl.when(jnp.logical_and(i >= 1, i <= chunks))
        def _():
            feed_forward(i - 1)

        @pl.when(i >= 2)
        def _():
            finish_grad(i - 2)

        @pl.when(jnp.logical_and(i >= 1, i <= chunks))
        def _():
            cross_grad(i - 1)
            weight_grads(i - 1)
            keep_forward(i - 1)

        @pl.when(i >= 2)
        def _():
            write_backward(i - 2)

        return carry

    lax.fori_loop(0, chunks + 1, step, 0)
    put_parts(d, r.parts_in, 0, r.acc_in)
    put_parts(d, r.parts_out, 0, r.acc_out)
    if merged:
        mlp_scatters(r)[0].start()
    finish_grad(chunks - 1)
    if merged:
        for c in range(chunks):
            cross_f(r, c).start()
    write_backward(chunks - 1)

    def pack(b, carry):
        here = block_at(d, b)[1]
        there = pl.ds(b * d.per, d.per)
        both = [r.grad_key[h, here, :] * SCALE for h in range(heads)]
        both += [r.grad_value[h, here, :] for h in range(heads)]
        wide = jnp.concatenate(both, axis=1).astype(jnp.bfloat16)
        r.grad_pairs[there] = wide.reshape(d.per, d.owned, 2 * d.column)
        return carry

    each_block(d, pack, 0)
    r.grad_write[...] = r.acc_write[...].T.astype(jnp.bfloat16)


def put_parts(d, ref, at, value):
    width = value.shape[1]
    for b in range(d.tok_count):
        rows = slice(b * d.share, (b + 1) * d.share)
        ref[b // 2, b % 2, :, at : at + width] = value[rows, :].astype(jnp.bfloat16)


def back_phase(r, d, merged):
    chunks, heads, width, column, owned = d.chunks, d.heads, d.width, d.column, d.owned
    low, wide = jnp.bfloat16, jnp.float32
    core, side = chunk_core_side(r)
    other = 1 - core
    pairs = spread_of(r, d, "tok", lambda peer: r.grad_pairs.at[peer], r.got_pairs, r.pairs_sems)
    pairs.start()
    by_in, by_out = mlp_scatters(r)
    early = Scatter(r, r.parts_early, r.early_one, r.early_two, r.early_sems)
    late = Scatter(r, r.parts_late, r.late_one, r.late_two, r.late_sems)
    final = Scatter(r, r.parts_final, r.final_one, r.final_two, r.final_sems)
    if not merged:
        by_in.start()
        for c in range(chunks):
            cross_f(r, c).start()
    r.acc_in[...] = jnp.zeros_like(r.acc_in)
    r.acc_out[...] = jnp.zeros_like(r.acc_out)
    at_key, at_value = slice(0, column), slice(256, 256 + column)

    def query_weights(c, carry):
        normed = norm_parts(chunk_rows(r.tokens, c).astype(wide))[0].astype(low)
        r.update[c] = normed.reshape(r.update.shape[1:])
        r.acc_in[:, :column] += tn(normed, r.grad_query_t[c].T)
        return carry

    lax.fori_loop(0, chunks, query_weights, 0)
    put_parts(d, r.parts_early, 0, r.acc_in[:, :column])
    put_parts(d, r.parts_early, column, r.grad_write)
    pairs.wait()
    by_out.start()
    by_in.forward()
    r.got_pairs[r.tok] = r.grad_pairs[r.tok]
    summed = sum_slots(r.got_pairs, d.tok_count).astype(low)
    grad_key, grad_value = summed[:, :column], summed[:, column:]
    r.head_parts[r.head] = (nn(grad_key, r.wkey[...]) + nn(grad_value, r.wvalue[...])).astype(low)
    moved = spread_of(r, d, "head", lambda peer: r.head_parts.at[r.head], r.head_parts, r.heads_sems)
    moved.start()
    normed_one, scale_one = norm_parts(r.lat_one[...])
    put_parts(d, r.parts_early, 2 * column, tn(normed_one.astype(low), summed))
    moved.wait()
    grad_lat_one = norm_vjp(normed_one, scale_one, sum_slots(r.head_parts, d.head_count))
    r.grad_own[...] = grad_lat_one
    narrow = grad_lat_one.astype(low)
    grad_mixed = nt(narrow, r.rout[...]).astype(low)
    mixed = r.mixed[:, :column]
    product = grad_mixed.astype(wide) * mixed
    extra = []
    for h in range(heads):
        delta = jnp.sum(product[:, head_rows(h)], axis=1, keepdims=True)
        logs = r.mixed[:, column + h : column + h + 1]
        for k, (first, second) in enumerate(zip(split_three(delta), split_three(logs), strict=True)):
            extra.append((3 * h + k, first))
            extra.append((3 * (heads + h) + k, second))
    r.output_all[r.tok, :, :column] = grad_mixed
    r.output_all[r.tok, :, column:] = pick_lanes((owned, d.packed - column), extra).astype(low)
    outputs = spread_of(r, d, "tok", lambda peer: r.output_all.at[r.tok], r.output_all, r.output_sems)
    outputs.start()
    put_parts(d, r.parts_early, 4 * column, tn(narrow, mixed.astype(low)))
    r.query_sum[...] = jnp.zeros_like(r.query_sum)
    outputs.wait()
    early.start()
    by_out.forward()

    def turn(b, carry):
        here = block_at(d, b)[1]
        turned = r.output_all[pl.ds(b * d.per, d.per)].reshape(d.block, d.packed).astype(wide).T
        r.output_t[:, here] = turned[:column].astype(low)
        for h in range(2 * heads):
            at = column + 3 * h
            r.rows[h : h + 1, here] = turned[at : at + 1] + turned[at + 1 : at + 2] + turned[at + 2 : at + 3]
        return carry

    each_block(d, turn, 0)

    def key_grads(count, key_of, value_of, key_t_of, images):
        def body(b, carry):
            start, here = block_at(d, b)
            row_image = latent_row_image(r.counts, start, d.block)
            kept = []
            for h in range(heads):
                hr = head_rows(h)
                logs = r.rows[heads + h : heads + h + 1, here]
                rows = [jnp.where(row_image == image, logs, MASKED) for image in images]
                query, output = r.read_query_t[hr, here], r.output_t[hr, here]
                weights = jnp.exp2(add_rows(nn(key_of(h), query) * (SCALE * LOG2E), rows))
                grad_weights = nn(value_of(h), output)
                grad_scores = (weights * (grad_weights - r.rows[h : h + 1, here])).astype(low)
                r.query_sum[hr, here] += nn(key_t_of(h), grad_scores)
                kept.append(
                    (carry[h][0] + nt(grad_scores, query), carry[h][1] + nt(weights.astype(low), output))
                )
            return tuple(kept)

        zero = jnp.zeros((count, HD), wide)
        grads = each_block(d, body, ((zero, zero),) * heads)
        keys = jnp.concatenate([grads[h][0] for h in range(heads)], axis=1) * SCALE
        values = jnp.concatenate([grads[h][1] for h in range(heads)], axis=1)
        return keys.astype(low), values.astype(low)

    def core_copy(c):
        slot = lax.rem(c, 2)
        return pltpu.make_async_remote_copy(
            src_ref=r.send_f,
            dst_ref=r.got_f.at[slot],
            send_sem=r.core_sems.at[0, slot],
            recv_sem=r.core_sems.at[1, slot],
            device_id=(r.tok, side * 2 + other),
            device_id_type=MESH,
        )

    def cross_copy(c):
        return pltpu.make_async_remote_copy(
            src_ref=r.x_half.at[c, 1 - side],
            dst_ref=r.x_cross.at[c],
            send_sem=r.x_sems.at[0, c],
            recv_sem=r.x_sems.at[1, c],
            device_id=(r.tok, (1 - side) * 2 + core),
            device_id_type=MESH,
        )

    def compute(c):
        dk, dv = key_grads(
            4 * SUB,
            lambda h: r.read_key[c, h],
            lambda h: r.read_value[c, h],
            lambda h: r.read_key_t[c, head_rows(h), :],
            token_images(r, d, c),
        )
        moved = nn(dk, r.rkey[...]) + nn(dv, r.rvalue[...]) + tn(r.grad_query_t[c], r.wquery[...])
        r.wide_s[...] = moved.reshape(r.wide_s.shape)
        r.own_f[...] = r.wide_s[core]
        r.send_f[...] = r.wide_s[other].astype(low)
        core_copy(c).start()
        normed = r.update[c].reshape(4 * SUB, width)
        r.acc_out[:, at_key] += tn(normed, dk)
        r.acc_out[:, at_value] += tn(normed, dv)

    def cross(c):
        core_copy(c).wait()
        total = r.own_f[...] + r.got_f[lax.rem(c, 2)].astype(wide)
        r.x_half[c] = total.astype(low).reshape(2, SUB, width)
        cross_copy(c).start()

    def step(c, carry):
        @pl.when(c >= 1)
        def _():
            cross(c - 1)

        compute(c)
        return carry

    lax.fori_loop(0, chunks // 2, step, 0)
    early.forward()
    lax.fori_loop(chunks // 2, chunks, step, 0)
    own_dk, own_dv = key_grads(
        owned,
        lambda h: r.own_key[h],
        lambda h: r.own_value[h],
        lambda h: r.own_key_t[head_rows(h), :],
        [image_of(r.counts, r.tok * d.groups_here + g) for g in range(d.groups_here)],
    )

    def turn_query(b, carry):
        here = block_at(d, b)[1]
        turned = (r.query_sum[:, here] * SCALE).T.astype(low)
        r.query_send[pl.ds(b * d.per, d.per)] = turned.reshape(d.per, owned, column)
        return carry

    each_block(d, turn_query, 0)
    queries = spread_of(r, d, "tok", lambda peer: r.query_send.at[peer], r.query_got, r.back_query_sems)
    queries.start()
    cross(chunks - 1)
    normed_lat, scale_lat = norm_parts(r.latents[...].astype(wide))
    narrow_lat = normed_lat.astype(low)
    put_parts(d, r.parts_late, 0, r.acc_out[:, at_key] + tn(narrow_lat, own_dk))
    put_parts(d, r.parts_late, column, r.acc_out[:, at_value] + tn(narrow_lat, own_dv))
    late.start()
    queries.wait()
    r.query_got[r.tok] = r.query_send[r.tok]
    grad_query = sum_slots(r.query_got, d.tok_count).astype(low)
    lat_total = nn(grad_query, r.rquery[...]) + nn(own_dk, r.rkey[...]) + nn(own_dv, r.rvalue[...])
    r.lat_parts[...] = lat_total.astype(low).reshape(r.lat_parts.shape)
    lats = spread_of(r, d, "head", lambda peer: r.lat_parts.at[peer], r.lat_got, r.lat_sems)
    lats.start()
    put_parts(d, r.parts_final, 0, tn(narrow_lat, grad_query))
    final.start()
    late.forward()
    by_in.finish()
    final.forward()
    lats.wait()
    r.lat_got[r.head] = r.lat_parts[r.head]
    total = sum_slots(r.lat_got, d.head_count)
    count = owned // d.head_count
    mine = pl.ds(pl.multiple_of(r.head * count, count), count)
    normed, scale = norm_parts(r.latents[mine, :].astype(wide))
    r.lat_grad[...] = r.grad_own[mine, :] + norm_vjp(normed, scale, total)
    by_out.finish()
    early.finish()

    def wait_cross(c, carry):
        cross_copy(c).wait()
        cross_f(r, c).wait()
        return carry

    lax.fori_loop(0, chunks, wait_cross, 0)
    late.finish()
    final.finish()


FRONT, MIDDLE, BACK = 1, 2, 4
OWN, CARRY, OUT = 0, 1, 2


def buffers(d):
    low, wide = jnp.bfloat16, jnp.float32
    size, half = 4 * SUB, (2 * SUB, d.width)
    n, h = d.tok_count, d.head_count
    front, middle, back = FRONT, MIDDLE, BACK
    every = front | middle | back
    by_chunk = (d.chunks, d.column, size)
    by_head, by_column = (d.heads, d.latent_count, HD), (d.column, d.latent_count)
    key_heads, own_heads = (d.chunks, d.heads, size, HD), (d.heads, d.owned, HD)
    pairs, queries, wide_rows = (n, d.owned, 2 * d.column), (n, d.owned, d.column), (n, d.owned, d.packed)
    halves, quarters = (d.chunks, 2, SUB, d.width), (d.chunks, SUB, d.width)
    tok_sems, head_sems, sum_sems = (2, n), (2, h), (4, d.outer)

    def slots(columns):
        return (d.outer, d.share, columns)

    def parts(columns):
        return (d.outer, 2, d.share, columns)

    return dict(
        query_t=(by_chunk, low, front | middle, CARRY),
        key=(by_head, low, front | middle, CARRY),
        value=(by_head, low, front | middle, CARRY),
        key_t=(by_column, low, front | middle, CARRY),
        value_t=(by_column, low, front | middle, CARRY),
        read_key=(key_heads, low, front | back, CARRY),
        read_value=(key_heads, low, front | back, CARRY),
        read_key_t=(by_chunk, low, front | back, CARRY),
        read_value_t=(by_chunk, low, front, OWN),
        own_key=(own_heads, low, front | back, CARRY),
        own_value=(own_heads, low, front | back, CARRY),
        own_key_t=((d.column, d.owned), low, front | back, CARRY),
        own_value_t=((d.column, d.owned), low, front, OWN),
        read_query_t=(by_column, low, front | back, CARRY),
        lat_one=((d.owned, d.width), wide, front | back, CARRY),
        mixed=((d.owned, d.packed), wide, front | back, CARRY),
        update=((d.chunks, 2, *half), low, every, OWN),
        query_all=(queries, low, front, OWN),
        sums=((d.packed, d.latent_count), wide, front, OWN),
        sums_send=(wide_rows, low, front, OWN),
        sums_got=(wide_rows, low, front, OWN),
        head_parts=((h, d.owned, d.width), low, front | back, OWN),
        pair_all=(pairs, low, front, OWN),
        query_sems=(tok_sems, None, front, OWN),
        sums_sems=(tok_sems, None, front, OWN),
        head_sems=(head_sems, None, front, OWN),
        pair_sems=(tok_sems, None, front, OWN),
        grad_one=((d.quarter, d.width), wide, middle, OUT),
        grad_query_t=(by_chunk, low, middle | back, CARRY),
        grad_pairs=(pairs, low, middle | back, CARRY),
        parts_in=(parts(d.hidden), low, middle | back, CARRY),
        parts_out=(parts(d.hidden), low, middle | back, CARRY),
        grad_write=((d.width, d.column), low, middle | back, CARRY),
        f_half=(halves, low, middle | back, OUT),
        write_out=((d.column, d.width), low, middle, OWN),
        mlp_in=((d.width, d.hidden), low, middle, OWN),
        mlp_out=((d.hidden, d.width), low, middle, OWN),
        cotangent=((4, d.quarter, d.width), low, middle, OWN),
        mixed_t=(by_chunk, low, middle, OWN),
        log_total=((d.chunks, 8, size), wide, middle, OWN),
        own_a=(half, wide, middle, OWN),
        send_a=(half, low, middle, OWN),
        got_a=((2, *half), low, middle, OWN),
        half_a=(half, low, middle, OWN),
        cross_a=((2, *half), low, middle, OWN),
        own_d=(half, wide, middle, OWN),
        send_d=(half, low, middle, OWN),
        got_d=((2, *half), low, middle, OWN),
        half_d=(half, low, middle, OWN),
        cross_d=((2, *half), low, middle, OWN),
        summed_d=((2, 2, *half), low, middle, OWN),
        own_f=(half, wide, middle | back, OWN),
        send_f=(half, low, middle | back, OWN),
        got_f=((2, *half), low, middle | back, OWN),
        acc_in=((d.width, d.hidden), wide, middle | back, OWN),
        acc_out=((d.width, d.hidden), wide, middle | back, OWN),
        acc_write=((d.column, d.width), wide, middle, OWN),
        normed_s=((size, d.width), low, middle, OWN),
        act_s=((size, d.hidden), low, middle, OWN),
        inner_s=((size, d.hidden), low, middle, OWN),
        wide_s=((2, *half), wide, middle | back, OWN),
        latent_image=((d.latent_count, 128), jnp.int32, middle, OWN),
        grad_key=(by_head, wide, middle, OWN),
        grad_value=(by_head, wide, middle, OWN),
        send_sems=((7, 2), None, middle, OWN),
        recv_sems=((7, 2), None, middle, OWN),
        load_sems=((4,), None, middle, OWN),
        f_cross=(quarters, low, back, OUT),
        x_half=(halves, low, back, OUT),
        x_cross=(quarters, low, back, OUT),
        in_two=(slots(d.hidden), low, back, OUT),
        out_two=(slots(d.hidden), low, back, OUT),
        early_two=(slots(5 * d.column), low, back, OUT),
        late_two=(slots(2 * d.column), low, back, OUT),
        final_two=(slots(d.column), low, back, OUT),
        lat_grad=((d.owned // h, d.width), wide, back, OUT),
        in_one=(slots(d.hidden), low, back, OWN),
        out_one=(slots(d.hidden), low, back, OWN),
        early_one=(slots(5 * d.column), low, back, OWN),
        late_one=(slots(2 * d.column), low, back, OWN),
        final_one=(slots(d.column), low, back, OWN),
        parts_early=(parts(5 * d.column), low, back, OWN),
        parts_late=(parts(2 * d.column), low, back, OWN),
        parts_final=(parts(d.column), low, back, OWN),
        got_pairs=(pairs, low, back, OWN),
        output_all=(wide_rows, low, back, OWN),
        output_t=(by_column, low, back, OWN),
        rows=((8, d.latent_count), wide, back, OWN),
        grad_own=((d.owned, d.width), wide, back, OWN),
        query_sum=(by_column, wide, back, OWN),
        query_send=(queries, low, back, OWN),
        query_got=(queries, low, back, OWN),
        lat_parts=((h, d.owned // h, d.width), low, back, OWN),
        lat_got=((h, d.owned // h, d.width), low, back, OWN),
        in_sems=(sum_sems, None, back, OWN),
        out_sems=(sum_sems, None, back, OWN),
        early_sems=(sum_sems, None, back, OWN),
        late_sems=(sum_sems, None, back, OWN),
        final_sems=(sum_sems, None, back, OWN),
        pairs_sems=(tok_sems, None, back, OWN),
        heads_sems=(head_sems, None, back, OWN),
        output_sems=(tok_sems, None, back, OWN),
        back_query_sems=(tok_sems, None, back, OWN),
        lat_sems=(head_sems, None, back, OWN),
        core_sems=((2, 2), None, back, OWN),
        x_sems=((2, d.chunks), None, back, OWN),
        f_sems=((2, d.chunks), None, back, OWN),
    )


def run(d, number, phases, inputs, made):
    table = buffers(d)
    later = (FRONT | MIDDLE | BACK) & ~(2 * phases - 1) if phases != FRONT | MIDDLE | BACK else 0
    given = {x: (array, memory) for x, (array, uses, memory) in inputs.items() if uses & phases}
    given |= {x: (made[x], pltpu.VMEM) for x in made if table[x][2] & phases}
    wanted, inside = [], []
    for x, (shape, kind, uses, keep) in table.items():
        if x in given or not uses & phases:
            continue
        (wanted if keep == OUT or (keep == CARRY and uses & later) else inside).append(x)
    names = [*given, *wanted, *inside]
    merged = phases == FRONT | MIDDLE | BACK

    def kernel(*refs):
        r = SimpleNamespace(**dict(zip(names, refs, strict=True)))
        r.tok, r.head = lax.axis_index("tok"), lax.axis_index("head")
        if phases & MIDDLE:
            for load in loads(r):
                load.start()
        if not phases & FRONT:
            greet_all(r, d)
        if phases & FRONT:
            front_phase(r, d)
        if phases & MIDDLE:
            middle_phase(r, d, merged)
        if phases & BACK:
            back_phase(r, d, merged)

    def scratch(x):
        shape, kind = table[x][:2]
        return pltpu.SemaphoreType.DMA(shape) if kind is None else pltpu.VMEM(shape, kind)

    out = pl.pallas_call(
        kernel,
        out_shape=[jax.ShapeDtypeStruct(*table[x][:2]) for x in wanted],
        in_specs=[pl.BlockSpec(memory_space=memory) for array, memory in given.values()],
        out_specs=[pl.BlockSpec(memory_space=pltpu.VMEM) for x in wanted],
        scratch_shapes=[scratch(x) for x in inside],
        compiler_params=pltpu.CompilerParams(
            collective_id=number, has_side_effects=True, vmem_limit_bytes=63 << 20
        ),
        name="phases%d" % phases,
    )(*[array for array, memory in given.values()])
    return dict(zip(wanted, out, strict=True))


def finish_kernel(
    index, tokens, grad_one, f_own, f_cross, x_own, x_cross, in_two, out_two, early_two, early_all, late_two, final_two, lat,
    layer_out, input_grad, latent_grad, g_rquery, g_rkey, g_rvalue, g_rout, g_wquery, g_wkey, g_wvalue, g_wout,
    g_in, g_out,
):
    wide = jnp.float32
    column = final_two.shape[2]
    rows, width = grad_one.shape

    def both(own, cross):
        return (own[...].astype(wide).reshape(rows, width)) + cross[...].astype(wide).reshape(rows, width)

    layer_out[...] = both(f_own, f_cross).astype(jnp.bfloat16)
    normed, scale = norm_parts(tokens[0].astype(wide))
    input_grad[...] = grad_one[...] + norm_vjp(normed, scale, both(x_own, x_cross))
    latent_grad[...] = lat[...]

    def total(ref):
        kept = ref[0].astype(wide)
        for s in range(1, ref.shape[0]):
            kept = kept + ref[s].astype(wide)
        return kept

    g_in[...] = total(in_two)
    g_out[...] = total(out_two)
    g_rquery[...] = total(final_two)
    late = total(late_two)
    g_rkey[...] = late[:, :column]
    g_rvalue[...] = late[:, column:]
    early = total(early_two)
    g_wquery[...] = early[:, :column]
    g_wkey[...] = early[:, 2 * column : 3 * column]
    g_wvalue[...] = early[:, 3 * column : 4 * column]

    @pl.when(pl.program_id(0) == 0)
    def _():
        early = total(early_all)
        g_wout[...] = early[:, column : 2 * column].T
        g_rout[...] = early[:, 4 * column :].T


def finish(d, tokens, m):
    steps = 2 if d.share % 32 == 0 else 1
    rows, share, parts = d.quarter // steps, d.share // steps, d.chunks // steps
    head = lax.axis_index("head")
    index = jnp.stack([head, head // 2]).astype(jnp.int32)
    half = pl.BlockSpec((parts, None, SUB, d.width), lambda i, at: (i, at[1], 0, 0))
    cross = pl.BlockSpec((parts, SUB, d.width), lambda i, at: (i, 0, 0))
    strip = pl.BlockSpec((rows, d.width), lambda i, at: (i, 0))
    whole = pl.BlockSpec((d.owned // d.head_count, d.width), lambda i, at: (0, 0))

    def slots(columns):
        return pl.BlockSpec((d.outer, share, columns), lambda i, at: (0, i, 0))

    def part(columns):
        return pl.BlockSpec((share, columns), lambda i, at: (i, 0))

    wide, column = jnp.float32, d.column
    grads = [column] * 8 + [d.hidden] * 2
    turned = (column, d.share)
    return pl.pallas_call(
        finish_kernel,
        out_shape=[
            jax.ShapeDtypeStruct((d.quarter, d.width), jnp.bfloat16),
            jax.ShapeDtypeStruct((d.quarter, d.width), wide),
            jax.ShapeDtypeStruct((d.owned // d.head_count, d.width), wide),
            *[jax.ShapeDtypeStruct(turned if k in (3, 7) else (d.share, columns), wide) for k, columns in enumerate(grads)],
        ],
        grid_spec=pltpu.PrefetchScalarGridSpec(
            num_scalar_prefetch=1,
            grid=(steps,),
            in_specs=[
                pl.BlockSpec((1, rows, d.width), lambda i, at: (at[0], i, 0)),
                strip,
                half,
                cross,
                half,
                cross,
                slots(d.hidden),
                slots(d.hidden),
                slots(5 * column),
                pl.BlockSpec((d.outer, d.share, 5 * column), lambda i, at: (0, 0, 0)),
                slots(2 * column),
                slots(column),
                whole,
            ],
            out_specs=[
                strip,
                strip,
                whole,
                *[
                    pl.BlockSpec(turned, lambda i, at: (0, 0)) if k in (3, 7) else part(columns)
                    for k, columns in enumerate(grads)
                ],
            ],
        ),
        compiler_params=pltpu.CompilerParams(vmem_limit_bytes=62 << 20),
        name="finish",
    )(
        index, tokens, m.grad_one, m.f_half, m.f_cross, m.x_half, m.x_cross, m.in_two, m.out_two, m.early_two,
        m.early_two, m.late_two, m.final_two, m.lat_grad,
    )


def shards(
    tokens,
    latents,
    image_groups,
    read_query,
    read_key,
    read_value,
    read_out,
    write_query,
    write_key,
    write_value,
    write_out,
    mlp_in,
    mlp_out,
    cotangent,
):
    d = SimpleNamespace(tok_count=lax.axis_size("tok"), head_count=lax.axis_size("head"))
    rows, d.width = tokens.shape
    d.owned, d.column, d.hidden, d.packed = latents.shape[0], read_query.shape[1], mlp_in.shape[1], 256
    d.heads, d.quarter, d.groups_here = d.column // HD, rows // 4, rows // GROUP
    d.chunks, d.latent_count = d.quarter // SUB, d.owned * d.tok_count
    d.block = min(512, d.latent_count)
    d.blocks, d.per = d.latent_count // d.block, d.block // d.owned
    d.outer, d.share = d.tok_count // 2, d.width // d.tok_count
    tokens = tokens.reshape(4, d.quarter, d.width)
    every, vmem = FRONT | MIDDLE | BACK, pltpu.VMEM
    inputs = dict(
        counts=(image_groups, every, pltpu.SMEM),
        tokens=(tokens, every, vmem),
        latents=(latents, FRONT | BACK, vmem),
        rquery=(read_query.T, FRONT | BACK, vmem),
        rkey=(read_key.T, FRONT | BACK, vmem),
        rvalue=(read_value.T, FRONT | BACK, vmem),
        rout=(read_out, FRONT | BACK, vmem),
        wquery=(write_query.T, FRONT | BACK, vmem),
        wkey=(write_key.T, FRONT | BACK, vmem),
        wvalue=(write_value.T, FRONT | BACK, vmem),
        write_out_hbm=(write_out, MIDDLE, pl.ANY),
        mlp_in_hbm=(mlp_in, MIDDLE, pl.ANY),
        mlp_out_hbm=(mlp_out, MIDDLE, pl.ANY),
        cotangent_hbm=(cotangent.reshape(4, d.quarter, d.width), MIDDLE, pl.ANY),
    )
    made = {}
    for number, phases in enumerate([every] if d.latent_count <= 512 else [FRONT, MIDDLE, BACK]):
        made |= run(d, number, phases, inputs, made)
    (
        layer_out, input_grad, latent_grad, g_rquery, g_rkey, g_rvalue, g_rout, g_wquery, g_wkey, g_wvalue, g_wout,
        g_in, g_out,
    ) = finish(d, tokens, SimpleNamespace(**made))
    return (
        layer_out,
        input_grad,
        latent_grad,
        g_rquery,
        g_rkey,
        g_rvalue,
        g_rout,
        g_wquery,
        g_wkey,
        g_wvalue,
        g_wout,
        g_in,
        g_out.T,
    )


def solution(mesh):
    return jax.shard_map(
        shards,
        mesh=mesh,
        in_specs=(
            P("tok", None),
            P("tok", None),
            P(),
            P(None, "head"),
            P(None, "head"),
            P(None, "head"),
            P("head", None),
            P(None, "head"),
            P(None, "head"),
            P(None, "head"),
            P("head", None),
            P(None, "head"),
            P("head", None),
            P("tok", None),
        ),
        out_specs=(
            P(("tok", "head"), None),
            P(("tok", "head"), None),
            P(("tok", "head"), None),
            P("tok", "head"),
            P("tok", "head"),
            P("tok", "head"),
            P("head", "tok"),
            P("tok", "head"),
            P("tok", "head"),
            P("tok", "head"),
            P("head", "tok"),
            P("tok", "head"),
            P("head", "tok"),
        ),
        check_vma=False,
    )
```

time: 1760 us -> 222 us (0.13)
  waiting for transfers between devices: 1210 us -> 0 us
  Pallas kernels: 0 us -> 221 us
  blocking collectives: 199 us -> 0 us
  matrix products: 155 us -> 0 us
  other arithmetic: 112 us -> 0.67 us
  local copies, waits for them, and re-layouts: 58.3 us -> 0 us
    reduce_scatter x11 -> x0, waiting for transfers between devices: 667 us -> none  [the longest x1 72.5 us: shards(): lax.psum_scatter(grad_mlp_out, 'tok', scatter_dimension=1, tiled=True)]
    psum x5 -> x0, waiting for transfers between devices: 315 us -> none  [the longest x1 119 us: shards(): grad_normed_two = lax.psum(right_trans(grad_inner, mlp_in), 'head')]
    unnamed x26 -> x0, waiting for transfers between devices: 231 us -> none
    pallas_call x0 -> x2, Pallas kernels: none -> 221 us  [the longest x1 214 us: run(): pl.pallas_call(kernel, out_shape=[jax.ShapeDtypeStruct(*table[x][:2]) for...]
    all_gather x6 -> x0, blocking collectives: 177 us -> none  [the longest x1 32.7 us: shards(): query_all = lax.all_gather(query_own, 'tok', axis=0, tiled=True)]
    dot_general x68 -> x0, matrix products: 149 us -> none  [the longest x10 32.2 us: left_trans(): lax.dot_general(left, right, (((0,), (0,)), ((), ())), preferred_element_...]
    select_n x1 -> x0, other arithmetic: 35.8 us -> none  [shards(): latent_image = jnp.repeat(group_image, LPG, total_repeat_length=all_latents)]
    reduce_sum x20 -> x0, other arithmetic: 35.7 us -> none  [the longest x10 19.3 us: norm_rows(): center = values - jnp.mean(values, axis=-1, keepdims=True)]
  transfers between devices with their start and end apart: 21 -> 0, of which waited for: 21 -> 0; matrix products, arithmetic and copies ran while one was open for 6% -> 0% of each run, Pallas kernels for 0% -> 0%
where the time goes in v4:
time: 222 us
  Pallas kernels  221 us (100%)
    pallas_call x1, Pallas kernels, run(): pl.pallas_call(kernel, out_shape=[jax.ShapeDtypeStruct(*table[x][:2]) for...  214 us
    pallas_call x1, Pallas kernels, finish(): pl.pallas_call(finish_kernel, out_shape=[jax.ShapeDtypeStruct((d.quarter,...  6.4 us

profile of v4, /device:TPU:0, one launch (start us, length us, event | category | flops | bytes accessed | tf_op | source)
XLA Modules:
  0.0 222.3 jit_solution(13064677268798380710)
XLA Ops:
  0.7 0.7 pad_add_fusion.index
  1.3 214.4 %phases7.1 = (f32[512,768]{1,0:T(8,128)}, bf16[8,2,64,768]{3,2,1,0:T(8,128)(2,1)}, bf16[8,64,768]{2,1,0:T(8,128)(2,1)}, bf16[8,2,64,768]{3,2,1,0:T(8,128)(2,1)},...) custom-call(s32[5]{0:T(128)} %refs_0_.1, ...), custom_call_target="tpu_custom_call" | custom-call | tf_op jit(solution)/shard_map/phases7/pallas_call | solution.py:1019
  215.7 6.4 %finish.1 = (bf16[512,768]{1,0:T(8,128)(2,1)}, f32[512,768]{1,0:T(8,128)}, f32[16,768]{1,0:T(8,128)}, f32[96,192]{1,0:T(8,128)}, f32[96,192]{1,0:T(8,128)}, /*in...) custom-call(s32[2]{0:T(128)} %pad_add_fusion.index, ...), custom_call_target="tpu_custom_call" | custom-call | tf_op jit(solution)/shard_map/finish/pallas_call | solution.py:1093

commit v5 on v4

--- a/solution.py
+++ b/solution.py
@@ -19,6 +19,8 @@
 MASKED = -1e30
 GELU_A = 0.7978845608028654
 GELU_B = 0.044715
+LAG = 2
+DEPTH = 3
 
 
 def nn(left, right):
@@ -143,12 +145,20 @@
             device_id_type=MESH,
         )
 
+    def start_block(self, k):
+        self.first(lax.rem(self.mine + k + 1, self.outer)).start()
+
+    def forward_block(self, k):
+        block = lax.rem(self.mine + k + 1, self.outer)
+        self.got_one[block] = self.total(block)
+        self.second(block, self.mine).start()
+
     def start(self):
-        def go(step, carry):
-            self.first(lax.rem(self.mine + step, self.outer)).start()
+        def go(k, carry):
+            self.start_block(k)
             return carry
 
-        lax.fori_loop(1, self.outer + 1, go, 0)
+        lax.fori_loop(0, self.outer, go, 0)
 
     def total(self, block):
         self.first(block).wait()
@@ -156,13 +166,11 @@
         return both.astype(jnp.bfloat16)
 
     def forward(self):
-        def go(step, carry):
-            block = lax.rem(self.mine + step, self.outer)
-            self.got_one[block] = self.total(block)
-            self.second(block, self.mine).start()
+        def go(k, carry):
+            self.forward_block(k)
             return carry
 
-        lax.fori_loop(1, self.outer, go, 0)
+        lax.fori_loop(0, self.outer - 1, go, 0)
 
     def finish(self):
         self.got_two[self.mine] = self.total(self.mine)
@@ -253,7 +261,7 @@
         (r.write_out_hbm, r.write_out),
         (r.mlp_in_hbm, r.mlp_in),
         (r.mlp_out_hbm, r.mlp_out),
-        (r.cotangent_hbm, r.cotangent),
+        (r.cotangent_hbm, r.store.at[0:4]),
     )
     return [pltpu.make_async_copy(source, target, r.load_sems.at[k]) for k, (source, target) in enumerate(pairs)]
 
@@ -399,12 +407,11 @@
         load.wait()
 
     def copy(kind, chunk, source, target, peer):
-        slot = lax.rem(chunk, 2)
         return pltpu.make_async_remote_copy(
             src_ref=source,
             dst_ref=target,
-            send_sem=r.send_sems.at[kind, slot],
-            recv_sem=r.recv_sems.at[kind, slot],
+            send_sem=r.send_sems.at[kind, chunk],
+            recv_sem=r.recv_sems.at[kind, chunk],
             device_id=peer,
             device_id_type=MESH,
         )
@@ -413,7 +420,7 @@
         return copy(0, c, r.send_a, r.got_a.at[lax.rem(c, 2)], core_peer)
 
     def cross_copy_a(c):
-        return copy(1, c, r.half_a, r.cross_a.at[lax.rem(c, 2)], side_peer)
+        return copy(1, c, r.half_a.at[lax.rem(c, 3)], r.cross_a.at[c], side_peer)
 
     def core_u(c):
         return copy(2, c, r.update.at[c, core], r.update.at[c, core], core_peer)
@@ -421,21 +428,33 @@
     def core_d(c):
         return copy(3, c, r.send_d, r.got_d.at[lax.rem(c, 2)], core_peer)
 
+    def half_d(c):
+        rows = pl.ds(pl.multiple_of(lax.rem(c, 4) * 2 * SUB, 2 * SUB), 2 * SUB)
+        return r.store.at[4 + c // 4, rows, :]
+
+    def cross_d(c):
+        rows = pl.ds(pl.multiple_of(lax.rem(c, 4) * 2 * SUB, 2 * SUB), 2 * SUB)
+        return r.store.at[6 + c // 4, rows, :]
+
     def cross_copy_d(c):
-        return copy(4, c, r.half_d, r.cross_d.at[lax.rem(c, 2)], side_peer)
+        return copy(4, c, half_d(c), cross_d(c), side_peer)
 
     def core_s(c):
-        half = r.summed_d.at[lax.rem(c, 2), core]
+        half = r.summed_d.at[lax.rem(c, 4), core]
         return copy(5, c, half, half, core_peer)
 
     def core_f(c):
         return copy(6, c, r.send_f, r.got_f.at[lax.rem(c, 2)], core_peer)
 
-    group = lax.shift_right_logical(lax.broadcasted_iota(jnp.int32, r.latent_image.shape, 0), 3)
-    r.latent_image[...] = image_of(r.counts, group)
-
-    def mask_of(c, here):
-        image = r.latent_image[here, :]
+    def latent_images(start):
+        row = lax.broadcasted_iota(jnp.int32, r.latent_image.shape, 0) + start
+        return image_of(r.counts, lax.shift_right_logical(row, 3))
+
+    if d.blocks == 1:
+        r.latent_image[...] = latent_images(0)
+
+    def mask_of(c, b):
+        image = r.latent_image[...] if d.blocks == 1 else latent_images(b * d.block)
         image = jnp.concatenate([image, image], axis=1)
         lane = lax.broadcasted_iota(jnp.int32, (1, 4 * SUB), 1)
         part = lax.shift_right_logical(lane, 6)
@@ -460,7 +479,7 @@
 
         def body(b, carry):
             here = block_at(d, b)[1]
-            bias = mask_of(c, here)
+            bias = mask_of(c, b)
             kept = []
             for h in range(heads):
                 scores = nn(r.key[h, here, :], query[head_rows(h)])
@@ -483,13 +502,14 @@
 
     def finish_update(c):
         cross_copy_a(c).wait()
-        mine = r.half_a[...].astype(jnp.float32) + r.cross_a[lax.rem(c, 2)].astype(jnp.float32)
+        mine = r.half_a[lax.rem(c, 3)].astype(jnp.float32) + r.cross_a[c].astype(jnp.float32)
         r.update[c, core] = mine.astype(jnp.bfloat16)
         core_u(c).start()
 
     def cross_update(c):
         core_a(c).wait()
-        r.half_a[...] = (r.own_a[...] + r.got_a[lax.rem(c, 2)].astype(jnp.float32)).astype(jnp.bfloat16)
+        half = r.own_a[...] + r.got_a[lax.rem(c, 2)].astype(jnp.float32)
+        r.half_a[lax.rem(c, 3)] = half.astype(jnp.bfloat16)
         cross_copy_a(c).start()
 
     def one_rows(c):
@@ -507,7 +527,7 @@
         active = (inner * half).astype(jnp.bfloat16)
         r.act_s[...] = active
         slope = half + 0.5 * GELU_A * inner * (1.0 - tanh * tanh) * (1.0 + 3.0 * GELU_B * square)
-        grad_inner = (nt(chunk_rows(r.cotangent, c), r.mlp_out[...]) * slope).astype(jnp.bfloat16)
+        grad_inner = (nt(chunk_rows(r.store, c), r.mlp_out[...]) * slope).astype(jnp.bfloat16)
         r.inner_s[...] = grad_inner
         halve(nt(grad_inner, r.mlp_in[...]), r.own_d, r.send_d)
         core_d(c).start()
@@ -515,17 +535,15 @@
         core_f(c).start()
 
     def finish_grad(c):
-        slot = lax.rem(c, 2)
         cross_copy_d(c).wait()
-        mine = r.half_d[...].astype(jnp.float32) + r.cross_d[slot].astype(jnp.float32)
-        r.summed_d[slot, core] = mine.astype(jnp.bfloat16)
+        mine = half_d(c)[...].astype(jnp.float32) + cross_d(c)[...].astype(jnp.float32)
+        r.summed_d[lax.rem(c, 4), core] = mine.astype(jnp.bfloat16)
         core_s(c).start()
 
     def cross_grad(c):
         slot = lax.rem(c, 2)
         core_d(c).wait()
-        r.half_d[...] = (r.own_d[...] + r.got_d[slot].astype(jnp.float32)).astype(jnp.bfloat16)
-        cross_copy_d(c).start()
+        half_d(c)[...] = (r.own_d[...] + r.got_d[slot].astype(jnp.float32)).astype(jnp.bfloat16)
 
     def keep_forward(c):
         slot = lax.rem(c, 2)
@@ -539,13 +557,13 @@
 
     def weight_grads(c):
         r.acc_in[...] += tn(r.normed_s[...], r.inner_s[...])
-        r.acc_out[...] += tn(chunk_rows(r.cotangent, c), r.act_s[...])
+        r.acc_out[...] += tn(chunk_rows(r.store, c), r.act_s[...])
 
     def write_backward(c):
         core_s(c).wait()
         normed, scale = norm_parts(one_rows(c))
-        grad = r.summed_d[lax.rem(c, 2)].reshape(4 * SUB, width).astype(jnp.float32)
-        wide = chunk_rows(r.cotangent, c).astype(jnp.float32) + norm_vjp(normed, scale, grad)
+        grad = r.summed_d[lax.rem(c, 4)].reshape(4 * SUB, width).astype(jnp.float32)
+        wide = chunk_rows(r.store, c).astype(jnp.float32) + norm_vjp(normed, scale, grad)
         r.wide_s[...] = wide.reshape(r.wide_s.shape)
         part = pl.ds(pl.multiple_of(c * SUB, SUB), SUB)
         mine = pl.ds(pl.multiple_of(side * SUB, SUB), SUB)
@@ -559,7 +577,7 @@
 
         def body(b, carry):
             here = block_at(d, b)[1]
-            bias = mask_of(c, here)
+            bias = mask_of(c, b)
             kept = []
             for h in range(heads):
                 rows = head_rows(h)
@@ -578,49 +596,60 @@
         r.grad_query_t[c] = (jnp.concatenate(grads, axis=0) * SCALE).astype(jnp.bfloat16)
 
     def step(i, carry):
+        @pl.when(jnp.logical_and(i >= DEPTH, i < chunks + DEPTH))
+        def _():
+            finish_update(i - DEPTH)
+
         @pl.when(i < chunks)
         def _():
             write_forward(i)
 
-        @pl.when(jnp.logical_and(i >= 1, i <= chunks))
+        @pl.when(i > DEPTH)
         def _():
-            finish_update(i - 1)
+            weight_grads(i - DEPTH - 1)
+            keep_forward(i - DEPTH - 1)
+            cross_grad(i - DEPTH - 1)
 
         @pl.when(i < chunks)
         def _():
             cross_update(i)
 
-        @pl.when(jnp.logical_and(i >= 1, i <= chunks))
+        @pl.when(i >= chunks)
         def _():
-            feed_forward(i - 1)
-
-        @pl.when(i >= 2)
+            cross_copy_d(i - chunks).start()
+
+        @pl.when(jnp.logical_and(i >= DEPTH, i < chunks + DEPTH))
         def _():
-            finish_grad(i - 2)
-
-        @pl.when(jnp.logical_and(i >= 1, i <= chunks))
-        def _():
-            cross_grad(i - 1)
-            weight_grads(i - 1)
-            keep_forward(i - 1)
-
-        @pl.when(i >= 2)
-        def _():
-            write_backward(i - 2)
+            feed_forward(i - DEPTH)
 
         return carry
 
-    lax.fori_loop(0, chunks + 1, step, 0)
+    ahead = DEPTH + 1
+    lax.fori_loop(0, chunks + ahead, step, 0)
     put_parts(d, r.parts_in, 0, r.acc_in)
     put_parts(d, r.parts_out, 0, r.acc_out)
-    if merged:
-        mlp_scatters(r)[0].start()
-    finish_grad(chunks - 1)
-    if merged:
-        for c in range(chunks):
-            cross_f(r, c).start()
-    write_backward(chunks - 1)
-
+    by_in, by_out = mlp_scatters(r) if merged else (None, None)
+
+    def back_step(c, carry):
+        @pl.when(c < chunks)
+        def _():
+            finish_grad(c)
+
+        @pl.when(c + ahead < chunks)
+        def _():
+            cross_copy_d(c + ahead).start()
+
+        if merged:
+            trickle(by_in, c)
+            trickle(by_out, c - d.outer)
+
+        @pl.when(c >= 1)
+        def _():
+            write_backward(c - 1)
+
+        return carry
+
+    lax.fori_loop(0, chunks + 1, back_step, 0)
     def pack(b, carry):
         here = block_at(d, b)[1]
         there = pl.ds(b * d.per, d.per)
@@ -632,6 +661,11 @@
 
     each_block(d, pack, 0)
     r.grad_write[...] = r.acc_write[...].T.astype(jnp.bfloat16)
+
+
+def trickle(scatter, k):
+    pl.when(jnp.logical_and(k >= 0, k < scatter.outer))(partial(scatter.start_block, k))
+    pl.when(jnp.logical_and(k >= LAG, k < LAG + scatter.outer - 1))(partial(scatter.forward_block, k - LAG))
 
 
 def put_parts(d, ref, at, value):
@@ -650,15 +684,53 @@
     pairs.start()
     by_in, by_out = mlp_scatters(r)
     early = Scatter(r, r.parts_early, r.early_one, r.early_two, r.early_sems)
+    later = Scatter(r, r.parts_second, r.second_one, r.second_two, r.second_sems)
     late = Scatter(r, r.parts_late, r.late_one, r.late_two, r.late_sems)
     final = Scatter(r, r.parts_final, r.final_one, r.final_two, r.final_sems)
     if not merged:
         by_in.start()
-        for c in range(chunks):
-            cross_f(r, c).start()
+        by_out.start()
+    first_f = chunks // 2
+    for c in range(first_f):
+        cross_f(r, c).start()
     r.acc_in[...] = jnp.zeros_like(r.acc_in)
     r.acc_out[...] = jnp.zeros_like(r.acc_out)
     at_key, at_value = slice(0, column), slice(256, 256 + column)
+
+    def plain_weights(key, h, here, masks):
+        scores = nn(key, r.read_query_t[head_rows(h), here]) * (SCALE * LOG2E)
+        return jnp.exp2(add_rows(scores, masks))
+
+    def masks_of(b, images):
+        start, here = block_at(d, b)
+        row_image = latent_row_image(r.counts, start, d.block)
+        return [jnp.where(row_image == image, 0.0, MASKED) for image in images]
+
+    def keep_weights(first, last):
+        def keep(c, carry):
+            masks = masks_of(0, token_images(r, d, c))
+            top, low_rows = slice(0, 4 * SUB), slice(4 * SUB, 8 * SUB)
+            for h in range(heads):
+                weights = plain_weights(r.read_key[c, h], h, slice(0, d.block), masks).astype(low)
+                if h == 0:
+                    r.store[c, top, 0:512] = weights
+                elif h == 1:
+                    r.store[c, top, 512:768] = weights[:, 0:256]
+                    r.store[c, low_rows, 0:256] = weights[:, 256:512]
+                else:
+                    r.store[c, low_rows, 256:768] = weights
+            return carry
+
+        if keeps_weights(d):
+            lax.fori_loop(first, last, keep, 0)
+
+    def kept_weights(c, h):
+        top, low_rows = slice(0, 4 * SUB), slice(4 * SUB, 8 * SUB)
+        if h == 0:
+            return r.store[c, top, 0:512]
+        if h == 1:
+            return jnp.concatenate([r.store[c, top, 512:768], r.store[c, low_rows, 0:256]], axis=1)
+        return r.store[c, low_rows, 256:768]
 
     def query_weights(c, carry):
         normed = norm_parts(chunk_rows(r.tokens, c).astype(wide))[0].astype(low)
@@ -669,17 +741,21 @@
     lax.fori_loop(0, chunks, query_weights, 0)
     put_parts(d, r.parts_early, 0, r.acc_in[:, :column])
     put_parts(d, r.parts_early, column, r.grad_write)
+    keep_weights(0, chunks // 2)
     pairs.wait()
-    by_out.start()
-    by_in.forward()
+    early.start()
+    if not merged:
+        by_in.forward()
+        by_out.forward()
     r.got_pairs[r.tok] = r.grad_pairs[r.tok]
     summed = sum_slots(r.got_pairs, d.tok_count).astype(low)
     grad_key, grad_value = summed[:, :column], summed[:, column:]
     r.head_parts[r.head] = (nn(grad_key, r.wkey[...]) + nn(grad_value, r.wvalue[...])).astype(low)
     moved = spread_of(r, d, "head", lambda peer: r.head_parts.at[r.head], r.head_parts, r.heads_sems)
     moved.start()
+    keep_weights(chunks // 2, 3 * chunks // 4)
     normed_one, scale_one = norm_parts(r.lat_one[...])
-    put_parts(d, r.parts_early, 2 * column, tn(normed_one.astype(low), summed))
+    put_parts(d, r.parts_second, 0, tn(normed_one.astype(low), summed))
     moved.wait()
     grad_lat_one = norm_vjp(normed_one, scale_one, sum_slots(r.head_parts, d.head_count))
     r.grad_own[...] = grad_lat_one
@@ -698,36 +774,38 @@
     r.output_all[r.tok, :, column:] = pick_lanes((owned, d.packed - column), extra).astype(low)
     outputs = spread_of(r, d, "tok", lambda peer: r.output_all.at[r.tok], r.output_all, r.output_sems)
     outputs.start()
-    put_parts(d, r.parts_early, 4 * column, tn(narrow, mixed.astype(low)))
+    put_parts(d, r.parts_second, 2 * column, tn(narrow, mixed.astype(low)))
     r.query_sum[...] = jnp.zeros_like(r.query_sum)
+    keep_weights(3 * chunks // 4, chunks)
     outputs.wait()
-    early.start()
-    by_out.forward()
+    early.forward()
 
     def turn(b, carry):
         here = block_at(d, b)[1]
         turned = r.output_all[pl.ds(b * d.per, d.per)].reshape(d.block, d.packed).astype(wide).T
-        r.output_t[:, here] = turned[:column].astype(low)
-        for h in range(2 * heads):
-            at = column + 3 * h
-            r.rows[h : h + 1, here] = turned[at : at + 1] + turned[at + 1 : at + 2] + turned[at + 2 : at + 3]
+        def joined(k):
+            at = column + 3 * k
+            return turned[at : at + 1] + turned[at + 1 : at + 2] + turned[at + 2 : at + 3]
+
+        for h in range(heads):
+            inverse = jnp.exp2(joined(heads + h))
+            r.output_t[head_rows(h), here] = (turned[head_rows(h)] * inverse).astype(low)
+            r.rows[h : h + 1, here] = joined(h) * inverse
         return carry
 
     each_block(d, turn, 0)
 
-    def key_grads(count, key_of, value_of, key_t_of, images):
+    def key_grads(count, weights_of, value_of, key_t_of, images):
         def body(b, carry):
-            start, here = block_at(d, b)
-            row_image = latent_row_image(r.counts, start, d.block)
+            here = block_at(d, b)[1]
+            masks = masks_of(b, images)
             kept = []
             for h in range(heads):
                 hr = head_rows(h)
-                logs = r.rows[heads + h : heads + h + 1, here]
-                rows = [jnp.where(row_image == image, logs, MASKED) for image in images]
                 query, output = r.read_query_t[hr, here], r.output_t[hr, here]
-                weights = jnp.exp2(add_rows(nn(key_of(h), query) * (SCALE * LOG2E), rows))
-                grad_weights = nn(value_of(h), output)
-                grad_scores = (weights * (grad_weights - r.rows[h : h + 1, here])).astype(low)
+                weights = weights_of(h, here, masks)
+                grad_weights = nn(value_of(h), output) - r.rows[h : h + 1, here]
+                grad_scores = (weights.astype(wide) * grad_weights).astype(low)
                 r.query_sum[hr, here] += nn(key_t_of(h), grad_scores)
                 kept.append(
                     (carry[h][0] + nt(grad_scores, query), carry[h][1] + nt(weights.astype(low), output))
@@ -762,9 +840,12 @@
         )
 
     def compute(c):
+        def weights_of(h, here, masks):
+            return kept_weights(c, h) if keeps_weights(d) else plain_weights(r.read_key[c, h], h, here, masks)
+
         dk, dv = key_grads(
             4 * SUB,
-            lambda h: r.read_key[c, h],
+            weights_of,
             lambda h: r.read_value[c, h],
             lambda h: r.read_key_t[c, head_rows(h), :],
             token_images(r, d, c),
@@ -789,15 +870,19 @@
         def _():
             cross(c - 1)
 
+        @pl.when(c >= first_f)
+        def _():
+            cross_f(r, c).start()
+
         compute(c)
+        trickle(later, c)
         return carry
 
     lax.fori_loop(0, chunks // 2, step, 0)
-    early.forward()
     lax.fori_loop(chunks // 2, chunks, step, 0)
     own_dk, own_dv = key_grads(
         owned,
-        lambda h: r.own_key[h],
+        lambda h, here, masks: plain_weights(r.own_key[h], h, here, masks),
         lambda h: r.own_value[h],
         lambda h: r.own_key_t[head_rows(h), :],
         [image_of(r.counts, r.tok * d.groups_here + g) for g in range(d.groups_here)],
@@ -839,6 +924,7 @@
     r.lat_grad[...] = r.grad_own[mine, :] + norm_vjp(normed, scale, total)
     by_out.finish()
     early.finish()
+    later.finish()
 
     def wait_cross(c, carry):
         cross_copy(c).wait()
@@ -852,6 +938,10 @@
 
 FRONT, MIDDLE, BACK = 1, 2, 4
 OWN, CARRY, OUT = 0, 1, 2
+
+
+def keeps_weights(d):
+    return d.blocks == 1 and d.heads * d.block == 2 * d.width and d.chunks == 8 and d.quarter == 8 * SUB
 
 
 def buffers(d):
@@ -911,20 +1001,18 @@
         write_out=((d.column, d.width), low, middle, OWN),
         mlp_in=((d.width, d.hidden), low, middle, OWN),
         mlp_out=((d.hidden, d.width), low, middle, OWN),
-        cotangent=((4, d.quarter, d.width), low, middle, OWN),
+        store=((8, d.quarter, d.width), low, middle | back if keeps_weights(d) else middle, OWN),
         mixed_t=(by_chunk, low, middle, OWN),
         log_total=((d.chunks, 8, size), wide, middle, OWN),
         own_a=(half, wide, middle, OWN),
         send_a=(half, low, middle, OWN),
         got_a=((2, *half), low, middle, OWN),
-        half_a=(half, low, middle, OWN),
-        cross_a=((2, *half), low, middle, OWN),
+        half_a=((3, *half), low, middle, OWN),
+        cross_a=((d.chunks, *half), low, middle, OWN),
         own_d=(half, wide, middle, OWN),
         send_d=(half, low, middle, OWN),
         got_d=((2, *half), low, middle, OWN),
-        half_d=(half, low, middle, OWN),
-        cross_d=((2, *half), low, middle, OWN),
-        summed_d=((2, 2, *half), low, middle, OWN),
+        summed_d=((4, 2, *half), low, middle, OWN),
         own_f=(half, wide, middle | back, OWN),
         send_f=(half, low, middle | back, OWN),
         got_f=((2, *half), low, middle | back, OWN),
@@ -935,27 +1023,30 @@
         act_s=((size, d.hidden), low, middle, OWN),
         inner_s=((size, d.hidden), low, middle, OWN),
         wide_s=((2, *half), wide, middle | back, OWN),
-        latent_image=((d.latent_count, 128), jnp.int32, middle, OWN),
+        latent_image=((d.block, 128), jnp.int32, middle, OWN),
         grad_key=(by_head, wide, middle, OWN),
         grad_value=(by_head, wide, middle, OWN),
-        send_sems=((7, 2), None, middle, OWN),
-        recv_sems=((7, 2), None, middle, OWN),
+        send_sems=((7, d.chunks), None, middle, OWN),
+        recv_sems=((7, d.chunks), None, middle, OWN),
         load_sems=((4,), None, middle, OWN),
         f_cross=(quarters, low, back, OUT),
         x_half=(halves, low, back, OUT),
         x_cross=(quarters, low, back, OUT),
         in_two=(slots(d.hidden), low, back, OUT),
         out_two=(slots(d.hidden), low, back, OUT),
-        early_two=(slots(5 * d.column), low, back, OUT),
+        early_two=(slots(2 * d.column), low, back, OUT),
+        second_two=(slots(3 * d.column), low, back, OUT),
         late_two=(slots(2 * d.column), low, back, OUT),
         final_two=(slots(d.column), low, back, OUT),
         lat_grad=((d.owned // h, d.width), wide, back, OUT),
         in_one=(slots(d.hidden), low, back, OWN),
         out_one=(slots(d.hidden), low, back, OWN),
-        early_one=(slots(5 * d.column), low, back, OWN),
+        early_one=(slots(2 * d.column), low, back, OWN),
+        second_one=(slots(3 * d.column), low, back, OWN),
         late_one=(slots(2 * d.column), low, back, OWN),
         final_one=(slots(d.column), low, back, OWN),
-        parts_early=(parts(5 * d.column), low, back, OWN),
+        parts_early=(parts(2 * d.column), low, back, OWN),
+        parts_second=(parts(3 * d.column), low, back, OWN),
         parts_late=(parts(2 * d.column), low, back, OWN),
         parts_final=(parts(d.column), low, back, OWN),
         got_pairs=(pairs, low, back, OWN),
@@ -971,6 +1062,7 @@
         in_sems=(sum_sems, None, back, OWN),
         out_sems=(sum_sems, None, back, OWN),
         early_sems=(sum_sems, None, back, OWN),
+        second_sems=(sum_sems, None, back, OWN),
         late_sems=(sum_sems, None, back, OWN),
         final_sems=(sum_sems, None, back, OWN),
         pairs_sems=(tok_sems, None, back, OWN),
@@ -1023,7 +1115,7 @@
         out_specs=[pl.BlockSpec(memory_space=pltpu.VMEM) for x in wanted],
         scratch_shapes=[scratch(x) for x in inside],
         compiler_params=pltpu.CompilerParams(
-            collective_id=number, has_side_effects=True, vmem_limit_bytes=63 << 20
+            collective_id=number, has_side_effects=True, vmem_limit_bytes=127 << 19
         ),
         name="phases%d" % phases,
     )(*[array for array, memory in given.values()])
@@ -1031,7 +1123,7 @@
 
 
 def finish_kernel(
-    index, tokens, grad_one, f_own, f_cross, x_own, x_cross, in_two, out_two, early_two, early_all, late_two, final_two, lat,
+    index, tokens, grad_one, f_own, f_cross, x_own, x_cross, in_two, out_two, early_two, early_all, second_two, second_all, late_two, final_two, lat,
     layer_out, input_grad, latent_grad, g_rquery, g_rkey, g_rvalue, g_rout, g_wquery, g_wkey, g_wvalue, g_wout,
     g_in, g_out,
 ):
@@ -1059,16 +1151,15 @@
     late = total(late_two)
     g_rkey[...] = late[:, :column]
     g_rvalue[...] = late[:, column:]
-    early = total(early_two)
-    g_wquery[...] = early[:, :column]
-    g_wkey[...] = early[:, 2 * column : 3 * column]
-    g_wvalue[...] = early[:, 3 * column : 4 * column]
+    g_wquery[...] = total(early_two)[:, :column]
+    second = total(second_two)
+    g_wkey[...] = second[:, :column]
+    g_wvalue[...] = second[:, column : 2 * column]
 
     @pl.when(pl.program_id(0) == 0)
     def _():
-        early = total(early_all)
-        g_wout[...] = early[:, column : 2 * column].T
-        g_rout[...] = early[:, 4 * column :].T
+        g_wout[...] = total(early_all)[:, column:].T
+        g_rout[...] = total(second_all)[:, 2 * column :].T
 
 
 def finish(d, tokens, m):
@@ -1110,8 +1201,10 @@
                 cross,
                 slots(d.hidden),
                 slots(d.hidden),
-                slots(5 * column),
-                pl.BlockSpec((d.outer, d.share, 5 * column), lambda i, at: (0, 0, 0)),
+                slots(2 * column),
+                pl.BlockSpec((d.outer, d.share, 2 * column), lambda i, at: (0, 0, 0)),
+                slots(3 * column),
+                pl.BlockSpec((d.outer, d.share, 3 * column), lambda i, at: (0, 0, 0)),
                 slots(2 * column),
                 slots(column),
                 whole,
@@ -1130,7 +1223,7 @@
         name="finish",
     )(
         index, tokens, m.grad_one, m.f_half, m.f_cross, m.x_half, m.x_cross, m.in_two, m.out_two, m.early_two,
-        m.early_two, m.late_two, m.final_two, m.lat_grad,
+        m.early_two, m.second_two, m.second_two, m.late_two, m.final_two, m.lat_grad,
     )
 
 

time: 222 us -> 210 us (0.946)
  Pallas kernels: 221 us -> 209 us
    pallas_call x1, Pallas kernels: 214 us -> 202 us  [run(): pl.pallas_call(kernel, out_shape=[jax.ShapeDtypeStruct(*table[x][:2]) for...]
where the time goes in v5:
time: 210 us
  Pallas kernels  209 us (100%)
    pallas_call x1, Pallas kernels, run(): pl.pallas_call(kernel, out_shape=[jax.ShapeDtypeStruct(*table[x][:2]) for...  202 us
    pallas_call x1, Pallas kernels, finish(): pl.pallas_call(finish_kernel, out_shape=[jax.ShapeDtypeStruct((d.quarter,...  6.38 us

profile of v5, /device:TPU:0, one launch (start us, length us, event | category | flops | bytes accessed | tf_op | source)
XLA Modules:
  0.0 210.2 jit_solution(7633566271068909643)
XLA Ops:
  0.7 0.7 pad_add_fusion.index
  1.3 202.4 %phases7.1 = (f32[512,768]{1,0:T(8,128)}, bf16[8,2,64,768]{3,2,1,0:T(8,128)(2,1)}, bf16[8,64,768]{2,1,0:T(8,128)(2,1)}, bf16[8,2,64,768]{3,2,1,0:T(8,128)(2,1)},...) custom-call(s32[5]{0:T(128)} %refs_0_.1, ...), custom_call_target="tpu_custom_call" | custom-call | tf_op jit(solution)/shard_map/phases7/pallas_call | solution.py:1111
  203.7 6.4 %finish.1 = (bf16[512,768]{1,0:T(8,128)(2,1)}, f32[512,768]{1,0:T(8,128)}, f32[16,768]{1,0:T(8,128)}, f32[96,192]{1,0:T(8,128)}, f32[96,192]{1,0:T(8,128)}, /*in...) custom-call(s32[2]{0:T(128)} %pad_add_fusion.index, ...), custom_call_target="tpu_custom_call" | custom-call | tf_op jit(solution)/shard_map/finish/pallas_call | solution.py:1184

commit v6 on v5

--- a/solution.py
+++ b/solution.py
@@ -20,7 +20,7 @@
 GELU_A = 0.7978845608028654
 GELU_B = 0.044715
 LAG = 2
-DEPTH = 3
+WRITES = 3
 
 
 def nn(left, right):
@@ -69,7 +69,7 @@
 
 def chunk_rows(ref, c):
     part = pl.ds(pl.multiple_of(c * SUB, SUB), SUB)
-    return jnp.concatenate([ref[q, part, :] for q in (0, 2, 1, 3)], axis=0)
+    return jnp.concatenate([ref[q, part, :] for q in range(4)], axis=0)
 
 
 def greet_all(r, d):
@@ -206,15 +206,6 @@
     return value
 
 
-def chunk_bias(counts, tok, groups_here, c, quarter, row_image, rows):
-    kept = []
-    for q in (0, 2, 1, 3):
-        group = tok * groups_here + (q * quarter + c * SUB) // GROUP
-        image = image_of(counts, group)
-        kept.append([jnp.where(row_image == image, row, MASKED) for row in rows])
-    return kept
-
-
 def add_rows(values, rows):
     count = values.shape[0] // len(rows)
     return jnp.concatenate([values[k * count : (k + 1) * count] + row for k, row in enumerate(rows)], axis=0)
@@ -222,7 +213,7 @@
 
 def token_images(r, d, c):
     return [
-        image_of(r.counts, r.tok * d.groups_here + (q * d.quarter + c * SUB) // GROUP) for q in (0, 2, 1, 3)
+        image_of(r.counts, r.tok * d.groups_here + (q * d.quarter + c * SUB) // GROUP) for q in range(4)
     ]
 
 
@@ -256,17 +247,51 @@
     return lax.rem(r.head, 2), r.head // 2
 
 
-def loads(r):
-    pairs = (
-        (r.write_out_hbm, r.write_out),
-        (r.mlp_in_hbm, r.mlp_in),
-        (r.mlp_out_hbm, r.mlp_out),
-        (r.cotangent_hbm, r.store.at[0:4]),
+def load(r, k):
+    source = (r.write_out_hbm, r.mlp_in_hbm, r.mlp_out_hbm, r.cotangent_hbm)[k]
+    target = (r.write_out, r.mlp_in, r.mlp_out, r.store.at[0:4])[k]
+    return pltpu.make_async_copy(source, target, r.load_sems.at[k])
+
+
+def peer_of(r, across):
+    core, side = chunk_core_side(r)
+    return (r.tok, (1 - side) * 2 + core if across else side * 2 + 1 - core)
+
+
+def middle_copy(r, kind, chunk, source, target, across):
+    return pltpu.make_async_remote_copy(
+        src_ref=source,
+        dst_ref=target,
+        send_sem=r.send_sems.at[kind, chunk],
+        recv_sem=r.recv_sems.at[kind, chunk],
+        device_id=peer_of(r, across),
+        device_id_type=MESH,
     )
-    return [pltpu.make_async_copy(source, target, r.load_sems.at[k]) for k, (source, target) in enumerate(pairs)]
-
-
-def front_phase(r, d):
+
+
+def peer_weights(r):
+    return middle_copy(r, 10, 0, r.write_out, r.wo_peer, True)
+
+
+def peer_grads(r):
+    return middle_copy(r, 11, 0, r.wo_send, r.wo_got, True)
+
+
+def finish_write_out(r):
+    peer_grads(r).wait()
+    total = r.acc_write[0] + r.wo_got[...].astype(jnp.float32)
+    r.grad_write[...] = total.T.astype(jnp.bfloat16)
+
+
+def halve(r, wide, own, send):
+    core = chunk_core_side(r)[0]
+    r.wide_s[...] = wide.reshape(r.wide_s.shape)
+    for x in range(2):
+        own[x] = r.wide_s[x, core]
+        send[x] = r.wide_s[x, 1 - core].astype(jnp.bfloat16)
+
+
+def front_phase(r, d, merged):
     low = jnp.bfloat16
     heads, column, chunks, owned = d.heads, d.column, d.chunks, d.owned
     latents_wide = r.latents[...].astype(jnp.float32)
@@ -294,6 +319,9 @@
         return carry
 
     lax.fori_loop(0, chunks, project, 0)
+    if merged:
+        load(r, 0).wait()
+        peer_weights(r).start()
     r.sums[...] = jnp.zeros_like(r.sums)
     queries.wait()
 
@@ -401,50 +429,52 @@
     chunks, heads, width = d.chunks, d.heads, d.width
     core, side = chunk_core_side(r)
     other = 1 - core
-    core_peer = (r.tok, side * 2 + other)
-    side_peer = (r.tok, (1 - side) * 2 + core)
-    for load in loads(r):
-        load.wait()
-
-    def copy(kind, chunk, source, target, peer):
-        return pltpu.make_async_remote_copy(
-            src_ref=source,
-            dst_ref=target,
-            send_sem=r.send_sems.at[kind, chunk],
-            recv_sem=r.recv_sems.at[kind, chunk],
-            device_id=peer,
-            device_id_type=MESH,
-        )
+    for k in range(1 if merged else 0, 4):
+        load(r, k).wait()
+    if not merged:
+        peer_weights(r).start()
+    peer_weights(r).wait()
+
+    def copy(kind, chunk, source, target, across):
+        return middle_copy(r, kind, chunk, source, target, across)
+
+    def mixed_copy(c):
+        return copy(0, c, r.mixed_t.at[c, 1 - side], r.mixed_got.at[c], True)
 
     def core_a(c):
-        return copy(0, c, r.send_a, r.got_a.at[lax.rem(c, 2)], core_peer)
-
-    def cross_copy_a(c):
-        return copy(1, c, r.half_a.at[lax.rem(c, 3)], r.cross_a.at[c], side_peer)
+        return copy(1, c, r.send_a, r.got_a.at[lax.rem(c, 2)], False)
 
     def core_u(c):
-        return copy(2, c, r.update.at[c, core], r.update.at[c, core], core_peer)
+        return copy(2, c, r.update.at[c, side, core], r.update.at[c, side, core], False)
+
+    def cross_u(c):
+        return copy(3, c, r.update.at[c, side, core], r.update.at[c, side, core], True)
+
+    def core_v(c):
+        return copy(4, c, r.update.at[c, 1 - side, core], r.update.at[c, 1 - side, core], False)
 
     def core_d(c):
-        return copy(3, c, r.send_d, r.got_d.at[lax.rem(c, 2)], core_peer)
-
-    def half_d(c):
-        rows = pl.ds(pl.multiple_of(lax.rem(c, 4) * 2 * SUB, 2 * SUB), 2 * SUB)
-        return r.store.at[4 + c // 4, rows, :]
+        return copy(5, c, r.send_d, r.got_d.at[lax.rem(c, 2)], False)
+
+    def half_d(c, x, count):
+        at = pl.multiple_of(lax.rem(c, 4) * 2 * SUB + x * SUB, SUB)
+        return r.store.at[4 + c // 4, pl.ds(at, count), :]
 
     def cross_d(c):
-        rows = pl.ds(pl.multiple_of(lax.rem(c, 4) * 2 * SUB, 2 * SUB), 2 * SUB)
-        return r.store.at[6 + c // 4, rows, :]
+        return r.store.at[6, pl.ds(pl.multiple_of(c * SUB, SUB), SUB), :]
 
     def cross_copy_d(c):
-        return copy(4, c, half_d(c), cross_d(c), side_peer)
+        return copy(6, c, half_d(c, 1 - side, SUB), cross_d(c), True)
 
     def core_s(c):
-        half = r.summed_d.at[lax.rem(c, 4), core]
-        return copy(5, c, half, half, core_peer)
+        half = r.narrow_s.at[lax.rem(c, 4), core]
+        return copy(7, c, half, half, False)
 
     def core_f(c):
-        return copy(6, c, r.send_f, r.got_f.at[lax.rem(c, 2)], core_peer)
+        return copy(8, c, r.send_f, r.got_f.at[lax.rem(c, 2)], False)
+
+    def cross_o(c):
+        return copy(9, c, r.mixed_send.at[lax.rem(c, 4)], r.grad_mixed_t.at[c, side], True)
 
     def latent_images(start):
         row = lax.broadcasted_iota(jnp.int32, r.latent_image.shape, 0) + start
@@ -458,15 +488,9 @@
         image = jnp.concatenate([image, image], axis=1)
         lane = lax.broadcasted_iota(jnp.int32, (1, 4 * SUB), 1)
         part = lax.shift_right_logical(lane, 6)
-        part = 2 * lax.rem(part, 2) + part // 2
         row = part * d.quarter + c * SUB
         group = r.tok * d.groups_here + lax.shift_right_logical(row, 8)
         return jnp.where(image == image_of(r.counts, group), 0.0, MASKED)
-
-    def halve(wide, own, send):
-        r.wide_s[...] = wide.reshape(r.wide_s.shape)
-        own[...] = r.wide_s[core]
-        send[...] = r.wide_s[other].astype(jnp.bfloat16)
 
     r.acc_in[...] = jnp.zeros_like(r.acc_in)
     r.acc_out[...] = jnp.zeros_like(r.acc_out)
@@ -494,23 +518,29 @@
         totals = each_block(d, body, (zero,) * heads)
         mixed = jnp.concatenate([part / total for total, part in totals], axis=0)
         mixed = mixed.astype(jnp.bfloat16)
-        r.mixed_t[c] = mixed
+        r.mixed_t[c, 0] = mixed[:, : 2 * SUB]
+        r.mixed_t[c, 1] = mixed[:, 2 * SUB :]
+        mixed_copy(c).start()
         for h in range(heads):
             r.log_total[c, h : h + 1] = -jnp.log2(totals[h][0])
-        halve(tn(mixed, r.write_out[...]), r.own_a, r.send_a)
+
+    def part_update(c):
+        mixed_copy(c).wait()
+        part = tn(r.mixed_t[c, side], r.write_out[...]) + tn(r.mixed_got[c], r.wo_peer[...])
+        r.part_s[...] = part.reshape(r.part_s.shape)
+        r.send_a[...] = r.part_s[other].astype(jnp.bfloat16)
         core_a(c).start()
 
-    def finish_update(c):
-        cross_copy_a(c).wait()
-        mine = r.half_a[lax.rem(c, 3)].astype(jnp.float32) + r.cross_a[c].astype(jnp.float32)
-        r.update[c, core] = mine.astype(jnp.bfloat16)
+    def own_update(c):
+        core_a(c).wait()
+        total = r.part_s[core] + r.got_a[lax.rem(c, 2)].astype(jnp.float32)
+        r.update[c, side, core] = total.astype(jnp.bfloat16)
+        cross_u(c).start()
         core_u(c).start()
 
-    def cross_update(c):
-        core_a(c).wait()
-        half = r.own_a[...] + r.got_a[lax.rem(c, 2)].astype(jnp.float32)
-        r.half_a[lax.rem(c, 3)] = half.astype(jnp.bfloat16)
-        cross_copy_a(c).start()
+    def pass_update(c):
+        cross_u(c).wait()
+        core_v(c).start()
 
     def one_rows(c):
         moved = r.update[c].reshape(4 * SUB, width).astype(jnp.float32)
@@ -518,6 +548,7 @@
 
     def feed_forward(c):
         core_u(c).wait()
+        core_v(c).wait()
         normed = norm_parts(one_rows(c))[0].astype(jnp.bfloat16)
         r.normed_s[...] = normed
         inner = nn(normed, r.mlp_in[...])
@@ -529,30 +560,44 @@
         slope = half + 0.5 * GELU_A * inner * (1.0 - tanh * tanh) * (1.0 + 3.0 * GELU_B * square)
         grad_inner = (nt(chunk_rows(r.store, c), r.mlp_out[...]) * slope).astype(jnp.bfloat16)
         r.inner_s[...] = grad_inner
-        halve(nt(grad_inner, r.mlp_in[...]), r.own_d, r.send_d)
+        halve(r, nt(grad_inner, r.mlp_in[...]), r.own_d, r.send_d)
         core_d(c).start()
-        halve(nn(active, r.mlp_out[...]), r.own_f, r.send_f)
+        halve(r, nn(active, r.mlp_out[...]), r.own_f, r.send_f)
         core_f(c).start()
 
     def finish_grad(c):
         cross_copy_d(c).wait()
-        mine = half_d(c)[...].astype(jnp.float32) + cross_d(c)[...].astype(jnp.float32)
-        r.summed_d[lax.rem(c, 4), core] = mine.astype(jnp.bfloat16)
+        grad = half_d(c, side, SUB)[...].astype(jnp.float32) + cross_d(c)[...].astype(jnp.float32)
+        part = pl.ds(pl.multiple_of(c * SUB, SUB), SUB)
+        rows = r.tokens[r.head, part, :].astype(jnp.float32) + r.update[c, side, core].astype(jnp.float32)
+        normed, scale = norm_parts(rows)
+        wide = r.store[r.head, part, :].astype(jnp.float32) + norm_vjp(normed, scale, grad)
+        r.grad_one[part, :] = wide
+        r.narrow_s[lax.rem(c, 4), core] = wide.astype(jnp.bfloat16)
         core_s(c).start()
+
+    def send_mixed_grad(c):
+        core_s(c).wait()
+        narrow = r.narrow_s[lax.rem(c, 4)].reshape(2 * SUB, width)
+        r.mixed_send[lax.rem(c, 4)] = nt(r.wo_peer[...], narrow).astype(jnp.bfloat16)
+        cross_o(c).start()
+        r.grad_mixed_t[c, side] = nt(r.write_out[...], narrow).astype(jnp.bfloat16)
+        r.acc_write[0] += nn(r.mixed_t[c, side], narrow)
+        r.acc_write[1] += nn(r.mixed_got[c], narrow)
 
     def cross_grad(c):
         slot = lax.rem(c, 2)
         core_d(c).wait()
-        half_d(c)[...] = (r.own_d[...] + r.got_d[slot].astype(jnp.float32)).astype(jnp.bfloat16)
+        total = (r.own_d[...] + r.got_d[slot].astype(jnp.float32)).astype(jnp.bfloat16)
+        half_d(c, 0, 2 * SUB)[...] = total.reshape(2 * SUB, width)
 
     def keep_forward(c):
         slot = lax.rem(c, 2)
         core_f(c).wait()
-        total = (r.own_f[...] + r.got_f[slot].astype(jnp.float32)).reshape(2, SUB, width)
+        total = r.own_f[...] + r.got_f[slot].astype(jnp.float32)
         r.f_half[c] = total.astype(jnp.bfloat16)
         part = pl.ds(pl.multiple_of(c * SUB, SUB), SUB)
-        rows = pl.ds(pl.multiple_of(side * SUB, SUB), SUB)
-        mine = jnp.where(side == 0, total[0], total[1]) + r.update[c, core, rows, :].astype(jnp.float32)
+        mine = jnp.where(side == 0, total[0], total[1]) + r.update[c, side, core].astype(jnp.float32)
         r.f_half[c, side] = (mine + r.tokens[r.head, part, :].astype(jnp.float32)).astype(jnp.bfloat16)
 
     def weight_grads(c):
@@ -560,18 +605,9 @@
         r.acc_out[...] += tn(chunk_rows(r.store, c), r.act_s[...])
 
     def write_backward(c):
-        core_s(c).wait()
-        normed, scale = norm_parts(one_rows(c))
-        grad = r.summed_d[lax.rem(c, 4)].reshape(4 * SUB, width).astype(jnp.float32)
-        wide = chunk_rows(r.store, c).astype(jnp.float32) + norm_vjp(normed, scale, grad)
-        r.wide_s[...] = wide.reshape(r.wide_s.shape)
-        part = pl.ds(pl.multiple_of(c * SUB, SUB), SUB)
-        mine = pl.ds(pl.multiple_of(side * SUB, SUB), SUB)
-        r.grad_one[part, :] = r.wide_s[core, mine, :]
-        narrow = wide.astype(jnp.bfloat16)
-        mixed = r.mixed_t[c]
-        r.acc_write[...] += nn(mixed, narrow)
-        grad_mixed = nt(r.write_out[...], narrow).astype(jnp.bfloat16)
+        cross_o(c).wait()
+        mixed = jnp.concatenate([r.mixed_t[c, 0], r.mixed_t[c, 1]], axis=1)
+        grad_mixed = jnp.concatenate([r.grad_mixed_t[c, 0], r.grad_mixed_t[c, 1]], axis=1)
         query = r.query_t[c]
         product = grad_mixed.astype(jnp.float32) * mixed.astype(jnp.float32)
 
@@ -595,37 +631,46 @@
         grads = each_block(d, body, (zero,) * heads)
         r.grad_query_t[c] = (jnp.concatenate(grads, axis=0) * SCALE).astype(jnp.bfloat16)
 
+    def between(first, i, last):
+        return pl.when(jnp.logical_and(i >= first, i < last))
+
     def step(i, carry):
-        @pl.when(jnp.logical_and(i >= DEPTH, i < chunks + DEPTH))
+        @between(3, i, chunks + 3)
         def _():
-            finish_update(i - DEPTH)
-
-        @pl.when(i < chunks)
+            pass_update(i - 3)
+
+        def write(c, carry):
+            write_forward(c)
+            return carry
+
+        lax.fori_loop(jnp.minimum(WRITES * i, chunks), jnp.minimum(WRITES * (i + 1), chunks), write, 0)
+
+        @between(1, i, chunks + 1)
         def _():
-            write_forward(i)
-
-        @pl.when(i > DEPTH)
+            part_update(i - 1)
+
+        @pl.when(i >= 4)
         def _():
-            weight_grads(i - DEPTH - 1)
-            keep_forward(i - DEPTH - 1)
-            cross_grad(i - DEPTH - 1)
-
-        @pl.when(i < chunks)
+            weight_grads(i - 4)
+            keep_forward(i - 4)
+            cross_grad(i - 4)
+
+        @between(1, i, chunks + 1)
         def _():
-            cross_update(i)
-
-        @pl.when(i >= chunks)
+            own_update(i - 1)
+
+        @pl.when(i > chunks)
         def _():
-            cross_copy_d(i - chunks).start()
-
-        @pl.when(jnp.logical_and(i >= DEPTH, i < chunks + DEPTH))
+            cross_copy_d(i - chunks - 1).start()
+
+        @between(3, i, chunks + 3)
         def _():
-            feed_forward(i - DEPTH)
+            feed_forward(i - 3)
 
         return carry
 
-    ahead = DEPTH + 1
-    lax.fori_loop(0, chunks + ahead, step, 0)
+    ahead = 3
+    lax.fori_loop(0, chunks + 4, step, 0)
     put_parts(d, r.parts_in, 0, r.acc_in)
     put_parts(d, r.parts_out, 0, r.acc_out)
     by_in, by_out = mlp_scatters(r) if merged else (None, None)
@@ -643,13 +688,19 @@
             trickle(by_in, c)
             trickle(by_out, c - d.outer)
 
-        @pl.when(c >= 1)
+        @between(1, c, chunks + 1)
         def _():
-            write_backward(c - 1)
+            send_mixed_grad(c - 1)
+
+        @pl.when(c >= 3)
+        def _():
+            write_backward(c - 3)
 
         return carry
 
-    lax.fori_loop(0, chunks + 1, back_step, 0)
+    lax.fori_loop(0, chunks + 3, back_step, 0)
+    r.wo_send[...] = r.acc_write[1].astype(jnp.bfloat16)
+    peer_grads(r).start()
     def pack(b, carry):
         here = block_at(d, b)[1]
         there = pl.ds(b * d.per, d.per)
@@ -660,7 +711,8 @@
         return carry
 
     each_block(d, pack, 0)
-    r.grad_write[...] = r.acc_write[...].T.astype(jnp.bfloat16)
+    if not merged:
+        finish_write_out(r)
 
 
 def trickle(scatter, k):
@@ -740,8 +792,10 @@
 
     lax.fori_loop(0, chunks, query_weights, 0)
     put_parts(d, r.parts_early, 0, r.acc_in[:, :column])
+    keep_weights(0, chunks // 2)
+    if merged:
+        finish_write_out(r)
     put_parts(d, r.parts_early, column, r.grad_write)
-    keep_weights(0, chunks // 2)
     pairs.wait()
     early.start()
     if not merged:
@@ -851,9 +905,7 @@
             token_images(r, d, c),
         )
         moved = nn(dk, r.rkey[...]) + nn(dv, r.rvalue[...]) + tn(r.grad_query_t[c], r.wquery[...])
-        r.wide_s[...] = moved.reshape(r.wide_s.shape)
-        r.own_f[...] = r.wide_s[core]
-        r.send_f[...] = r.wide_s[other].astype(low)
+        halve(r, moved, r.own_f, r.send_f)
         core_copy(c).start()
         normed = r.update[c].reshape(4 * SUB, width)
         r.acc_out[:, at_key] += tn(normed, dk)
@@ -862,7 +914,7 @@
     def cross(c):
         core_copy(c).wait()
         total = r.own_f[...] + r.got_f[lax.rem(c, 2)].astype(wide)
-        r.x_half[c] = total.astype(low).reshape(2, SUB, width)
+        r.x_half[c] = total.astype(low)
         cross_copy(c).start()
 
     def step(c, carry):
@@ -875,9 +927,14 @@
             cross_f(r, c).start()
 
         compute(c)
-        trickle(later, c)
+        if few:
+            trickle(later, c)
         return carry
 
+    few = d.outer + LAG <= chunks
+    if not few:
+        later.start()
+        later.forward()
     lax.fori_loop(0, chunks // 2, step, 0)
     lax.fori_loop(chunks // 2, chunks, step, 0)
     own_dk, own_dv = key_grads(
@@ -946,7 +1003,7 @@
 
 def buffers(d):
     low, wide = jnp.bfloat16, jnp.float32
-    size, half = 4 * SUB, (2 * SUB, d.width)
+    size, half = 4 * SUB, (2, SUB, d.width)
     n, h = d.tok_count, d.head_count
     front, middle, back = FRONT, MIDDLE, BACK
     every = front | middle | back
@@ -980,7 +1037,7 @@
         read_query_t=(by_column, low, front | back, CARRY),
         lat_one=((d.owned, d.width), wide, front | back, CARRY),
         mixed=((d.owned, d.packed), wide, front | back, CARRY),
-        update=((d.chunks, 2, *half), low, every, OWN),
+        update=((d.chunks, 2, 2, SUB, d.width), low, every, OWN),
         query_all=(queries, low, front, OWN),
         sums=((d.packed, d.latent_count), wide, front, OWN),
         sums_send=(wide_rows, low, front, OWN),
@@ -1002,23 +1059,27 @@
         mlp_in=((d.width, d.hidden), low, middle, OWN),
         mlp_out=((d.hidden, d.width), low, middle, OWN),
         store=((8, d.quarter, d.width), low, middle | back if keeps_weights(d) else middle, OWN),
-        mixed_t=(by_chunk, low, middle, OWN),
+        mixed_t=((d.chunks, 2, d.column, 2 * SUB), low, middle, OWN),
         log_total=((d.chunks, 8, size), wide, middle, OWN),
-        own_a=(half, wide, middle, OWN),
-        send_a=(half, low, middle, OWN),
-        got_a=((2, *half), low, middle, OWN),
-        half_a=((3, *half), low, middle, OWN),
-        cross_a=((d.chunks, *half), low, middle, OWN),
+        send_a=((SUB, d.width), low, middle, OWN),
+        got_a=(half, low, middle, OWN),
+        part_s=(half, wide, middle, OWN),
+        mixed_got=((d.chunks, d.column, 2 * SUB), low, middle, OWN),
+        grad_mixed_t=((d.chunks, 2, d.column, 2 * SUB), low, middle, OWN),
+        mixed_send=((4, d.column, 2 * SUB), low, middle, OWN),
+        narrow_s=((4, *half), low, middle, OWN),
+        wo_peer=((d.column, d.width), low, middle, OWN),
+        wo_send=((d.column, d.width), low, middle, OWN),
+        wo_got=((d.column, d.width), low, middle, OWN),
         own_d=(half, wide, middle, OWN),
         send_d=(half, low, middle, OWN),
         got_d=((2, *half), low, middle, OWN),
-        summed_d=((4, 2, *half), low, middle, OWN),
         own_f=(half, wide, middle | back, OWN),
         send_f=(half, low, middle | back, OWN),
         got_f=((2, *half), low, middle | back, OWN),
         acc_in=((d.width, d.hidden), wide, middle | back, OWN),
         acc_out=((d.width, d.hidden), wide, middle | back, OWN),
-        acc_write=((d.column, d.width), wide, middle, OWN),
+        acc_write=((2, d.column, d.width), wide, middle, OWN),
         normed_s=((size, d.width), low, middle, OWN),
         act_s=((size, d.hidden), low, middle, OWN),
         inner_s=((size, d.hidden), low, middle, OWN),
@@ -1026,8 +1087,8 @@
         latent_image=((d.block, 128), jnp.int32, middle, OWN),
         grad_key=(by_head, wide, middle, OWN),
         grad_value=(by_head, wide, middle, OWN),
-        send_sems=((7, d.chunks), None, middle, OWN),
-        recv_sems=((7, d.chunks), None, middle, OWN),
+        send_sems=((12, d.chunks), None, middle, OWN),
+        recv_sems=((12, d.chunks), None, middle, OWN),
         load_sems=((4,), None, middle, OWN),
         f_cross=(quarters, low, back, OUT),
         x_half=(halves, low, back, OUT),
@@ -1093,12 +1154,12 @@
         r = SimpleNamespace(**dict(zip(names, refs, strict=True)))
         r.tok, r.head = lax.axis_index("tok"), lax.axis_index("head")
         if phases & MIDDLE:
-            for load in loads(r):
-                load.start()
+            for k in range(4):
+                load(r, k).start()
         if not phases & FRONT:
             greet_all(r, d)
         if phases & FRONT:
-            front_phase(r, d)
+            front_phase(r, d, merged)
         if phases & MIDDLE:
             middle_phase(r, d, merged)
         if phases & BACK:

time: 210 us -> 207 us (0.986)
  Pallas kernels: 209 us -> 206 us
    pallas_call x1, Pallas kernels: 202 us -> 199 us  [run(): pl.pallas_call(kernel, out_shape=[jax.ShapeDtypeStruct(*table[x][:2]) for...]
where the time goes in v6:
time: 207 us
  Pallas kernels  206 us (100%)
    pallas_call x1, Pallas kernels, run(): pl.pallas_call(kernel, out_shape=[jax.ShapeDtypeStruct(*table[x][:2]) for...  199 us
    pallas_call x1, Pallas kernels, finish(): pl.pallas_call(finish_kernel, out_shape=[jax.ShapeDtypeStruct((d.quarter,...  6.38 us

profile of v6, /device:TPU:0, one launch (start us, length us, event | category | flops | bytes accessed | tf_op | source)
XLA Modules:
  0.0 207.1 jit_solution(13816287078647204046)
XLA Ops:
  0.7 0.7 pad_add_fusion.index
  1.3 199.2 %phases7.1 = (f32[512,768]{1,0:T(8,128)}, bf16[8,2,64,768]{3,2,1,0:T(8,128)(2,1)}, bf16[8,64,768]{2,1,0:T(8,128)(2,1)}, bf16[8,2,64,768]{3,2,1,0:T(8,128)(2,1)},...) custom-call(s32[5]{0:T(128)} %refs_0_.1, ...), custom_call_target="tpu_custom_call" | custom-call | tf_op jit(solution)/shard_map/phases7/pallas_call | solution.py:1172
  200.5 6.4 %finish.1 = (bf16[512,768]{1,0:T(8,128)(2,1)}, f32[512,768]{1,0:T(8,128)}, f32[16,768]{1,0:T(8,128)}, f32[96,192]{1,0:T(8,128)}, f32[96,192]{1,0:T(8,128)}, /*in...) custom-call(s32[2]{0:T(128)} %pad_add_fusion.index, ...), custom_call_target="tpu_custom_call" | custom-call | tf_op jit(solution)/shard_map/finish/pallas_call | solution.py:1245

commit v7 on v6

--- a/solution.py
+++ b/solution.py
@@ -300,6 +300,8 @@
     greet_all(r, d)
     queries = spread_of(r, d, "tok", lambda peer: r.query_all.at[r.tok], r.query_all, r.query_sems)
     queries.start()
+    for copy in r.pending:
+        copy.wait()
     keys = nt(normed_lat, r.rkey[...]).astype(low)
     values = nt(normed_lat, r.rvalue[...]).astype(low)
     keep_heads(r.own_key, keys, heads)
@@ -1149,9 +1151,20 @@
         (wanted if keep == OUT or (keep == CARRY and uses & later) else inside).append(x)
     names = [*given, *wanted, *inside]
     merged = phases == FRONT | MIDDLE | BACK
+    first = ("counts", "latents", "rquery")
+    loaded = [x for x, (array, memory) in given.items() if merged and memory == pltpu.VMEM and x not in first]
+    given = {x: (array, pl.ANY if x in loaded else memory) for x, (array, memory) in given.items()}
 
     def kernel(*refs):
-        r = SimpleNamespace(**dict(zip(names, refs, strict=True)))
+        found = dict(zip(names, refs[: len(names)], strict=True))
+        targets = refs[len(names) :]
+        pending = [
+            pltpu.make_async_copy(found[x], targets[k], targets[-1].at[k]) for k, x in enumerate(loaded)
+        ]
+        found |= dict(zip(loaded, targets))
+        r = SimpleNamespace(**found, pending=pending)
+        for copy in pending:
+            copy.start()
         r.tok, r.head = lax.axis_index("tok"), lax.axis_index("head")
         if phases & MIDDLE:
             for k in range(4):
@@ -1174,7 +1187,9 @@
         out_shape=[jax.ShapeDtypeStruct(*table[x][:2]) for x in wanted],
         in_specs=[pl.BlockSpec(memory_space=memory) for array, memory in given.values()],
         out_specs=[pl.BlockSpec(memory_space=pltpu.VMEM) for x in wanted],
-        scratch_shapes=[scratch(x) for x in inside],
+        scratch_shapes=[scratch(x) for x in inside]
+        + [pltpu.VMEM(given[x][0].shape, given[x][0].dtype) for x in loaded]
+        + [pltpu.SemaphoreType.DMA((len(loaded),))] * min(1, len(loaded)),
         compiler_params=pltpu.CompilerParams(
             collective_id=number, has_side_effects=True, vmem_limit_bytes=127 << 19
         ),

time: 207 us -> 206 us (level)
  no operation moved by 1% of the time
where the time goes in v7:
time: 206 us
  Pallas kernels  204 us (99%)
    pallas_call x1, Pallas kernels, run(): pl.pallas_call(kernel, out_shape=[jax.ShapeDtypeStruct(*table[x][:2]) for...  198 us
    pallas_call x1, Pallas kernels, finish(): pl.pallas_call(finish_kernel, out_shape=[jax.ShapeDtypeStruct((d.quarter,...  6.38 us

profile of v7, /device:TPU:0, one launch (start us, length us, event | category | flops | bytes accessed | tf_op | source)
XLA Modules:
  0.0 205.7 jit_solution(4652856742485326330)
XLA Ops:
  0.7 0.7 pad_add_fusion.index
  1.3 197.9 %phases7.1 = (f32[512,768]{1,0:T(8,128)}, bf16[8,2,64,768]{3,2,1,0:T(8,128)(2,1)}, bf16[8,64,768]{2,1,0:T(8,128)(2,1)}, bf16[8,2,64,768]{3,2,1,0:T(8,128)(2,1)},...) custom-call(s32[5]{0:T(128)} %refs_0_.1, ...), custom_call_target="tpu_custom_call" | custom-call | tf_op jit(solution)/shard_map/phases7/pallas_call | solution.py:1185
  199.2 6.4 %finish.1 = (bf16[512,768]{1,0:T(8,128)(2,1)}, f32[512,768]{1,0:T(8,128)}, f32[16,768]{1,0:T(8,128)}, f32[96,192]{1,0:T(8,128)}, f32[96,192]{1,0:T(8,128)}, /*in...) custom-call(s32[2]{0:T(128)} %pad_add_fusion.index, ...), custom_call_target="tpu_custom_call" | custom-call | tf_op jit(solution)/shard_map/finish/pallas_call | solution.py:1260
